TPU v7x, 256 devices: a whole 4x4x8 slice. The times are simulated.
256 devices in a mesh: img: 64 (over y, x_lo, z), ori: 4 (over x_hi, core).
Axes of the slice: x: 4 (x_hi: 2, x_lo: 2; x = x_hi * 2 + x_lo), y: 4, z: 8, core: 2. Of those that a mesh axis runs over, the one named last changes fastest.
Arguments:
- images: bfloat16 [65536, 4096], P('img'), may hold values from -34 to 34
- img_scale: float32 [65536], P('img'), may hold values from 0.5 to 2
- references: bfloat16 [2048, 4096], P('ori', 'img'), may hold values from -4 to 4
- pattern: int32 [65536, 8], P('img', 'ori'), may hold values from 0 to 1, as said below
- tile_owner: int32 [4, 16384, 1], P('ori', 'img'), may hold values from 0 to 63; in each aligned block of 256 rows (0 to 255, 256 to 511, ..., all dimensions but the last counted through in order) at most 12 rows name the same one
- tile_brick: int32 [4, 16384], P('ori', 'img'), may hold values from 0 to 15
- tile_block: int32 [4, 16384], P('ori', 'img'), may hold values from 0 to 7
- distance_weights: bfloat16 [8, 128, 512], replicated, may hold values from -0.0625 to 0.0625
Outputs:
- bricks: float32 [1024, 512], P(('img', 'ori'))
- log_evidence: float32 [65536], P('img')
Inputs may be any that keep to these rules, and one draw needn't show every extreme that they name: `pattern`: each image has at least one orientation group set. `tile_owner`: among the 256 tiles of each aligned block, at most 12 name the same owner, and some block reaches 12.
All inputs are finite; a program needn't handle non-finite values.
Results may differ from a plain program's by a relative error of at most 0.002.
Values may be sent and summed in bfloat16 or wider, within the bound.
No kernel may reach another device: no remote copies, remote signals or barrier semaphores. Data moves between devices by JAX's collectives and lax.ppermute only.
A program may use at most 128 MiB of HBM per device.

v0:
```python
import math

import jax
import jax.numpy as jnp
from jax import lax
from jax.sharding import PartitionSpec as P

BRICK_DEV = 16


def collected_together(shard, axis):
    leaves = jax.tree.leaves(shard)
    turns = sorted(range(len(leaves)), key=lambda k: -leaves[k].size)
    width = (1, *leaves[turns[0]].shape)[-1]
    lines = [
        jnp.pad(leaves[k].reshape(-1), (0, -leaves[k].size % width)).reshape(-1, width)
        for k in turns
    ]
    both, at, found = (lax.all_gather(jnp.concatenate(lines), axis), 0, {})
    for k, line in zip(turns, lines):
        share = both[:, at : at + len(line)].reshape(len(both), -1)
        found[k] = share[:, : leaves[k].size].reshape(-1, *leaves[k].shape)
        at += len(line)
    numbers = iter(range(len(leaves)))
    return jax.tree.map(lambda _: found[next(numbers)], shard)


def combined_all(part, axis, combine):
    gathered = collected_together(part, axis)

    def take(source):
        return jax.tree.map(lambda a: lax.dynamic_index_in_dim(a, source, 0, False), gathered)

    return lax.fori_loop(
        1, lax.axis_size(axis), lambda source, state: combine(state, take(source)), take(0)
    )


def split_up(shard, dim, length):
    before, after = (shard.shape[:dim], shard.shape[dim + 1 :])
    return jnp.moveaxis(shard.reshape(*before, length, -1, *after), dim, 0)


def sent_and_summed(shard, axis, dim):
    length = lax.axis_size(axis)
    parts = lax.all_to_all(split_up(shard, dim, length), axis, 0, 0, tiled=True)
    return jnp.sum(parts, axis=0)


def combine_pairs(first_pair, second_pair):
    peak = jnp.maximum(first_pair[0], second_pair[0])
    mass = first_pair[1] * jnp.exp(first_pair[0] - peak) + second_pair[1] * jnp.exp(
        second_pair[0] - peak
    )
    return (peak, mass)


def select_rows(codes, values, count):
    cell_ids = jnp.arange(count, dtype=jnp.int32)
    selector = (codes[None, :] == cell_ids[:, None]).astype(jnp.float32)
    return jnp.dot(
        selector, values, preferred_element_type=jnp.float32, precision=lax.Precision.HIGHEST
    )


def body(
    images, img_scale, references, pattern, tile_owner, tile_brick, tile_block, distance_weights
):
    image_rows, width = images.shape
    ref_local = references.shape[0]
    group_size = ref_local // pattern.shape[1]
    positions, tile_width, voxels = distance_weights.shape
    inv_root = 1.0 / math.sqrt(width)
    weight_table = distance_weights.astype(jnp.float32)
    raw_scores = lax.dot_general(
        images,
        lax.all_gather(references, "img", axis=1, tiled=True),
        (((1,), (1,)), ((), ())),
        preferred_element_type=jnp.float32,
    )
    scores = raw_scores * img_scale[:, None] * inv_root
    active = jnp.repeat(pattern > 0, group_size, axis=1)
    masked = jnp.where(active, scores, -1e30)
    local_peak = jnp.max(masked, axis=1)
    local_expo = jnp.where(active, jnp.exp(masked - local_peak[:, None]), 0.0)
    local_mass = jnp.sum(local_expo, axis=1)
    peak, mass = combined_all((local_peak, local_mass), "ori", combine_pairs)
    weights = local_expo * (jnp.exp(local_peak - peak) / mass)[:, None]
    log_evidence = peak + jnp.log(mass)
    scaled = (weights * img_scale[:, None]).astype(jnp.bfloat16)
    partial_value = lax.dot_general(
        scaled, images, (((0,), (0,)), ((), ())), preferred_element_type=jnp.float32
    )
    owners = tile_owner.reshape(-1)
    local_code = tile_brick.reshape(-1) * positions + tile_block.reshape(-1)
    cells = BRICK_DEV * positions
    class_sums = lax.psum_scatter(partial_value, "img", scatter_dimension=0, tiled=True)
    tiles = class_sums.reshape(-1, tile_width)
    peers = lax.axis_size("img")
    tile_count = tiles.shape[0]
    capacity = max(2, 3 * tile_count // peers)
    dest_hot = (owners[:, None] == jnp.arange(peers, dtype=jnp.int32)[None, :]).astype(jnp.int32)
    rank_within = jnp.sum((jnp.cumsum(dest_hot, axis=0) - dest_hot) * dest_hot, axis=1)
    slot_index = owners * capacity + rank_within
    send_tiles = jnp.zeros((peers * capacity, tile_width), jnp.float32).at[slot_index].set(tiles)
    send_codes = jnp.full((peers * capacity,), -1, jnp.int32).at[slot_index].set(local_code)
    got_tiles, got_codes = (
        lax.all_to_all(
            send_tiles.reshape(peers, capacity, tile_width),
            "img",
            split_axis=0,
            concat_axis=0,
            tiled=True,
        ),
        lax.all_to_all(
            send_codes.reshape(peers, capacity), "img", split_axis=0, concat_axis=0, tiled=True
        ),
    )
    collected = select_rows(
        got_codes.reshape(peers * capacity), got_tiles.reshape(peers * capacity, tile_width), cells
    )
    brick_terms = jnp.einsum(
        "bpt,ptv->bv",
        collected.reshape(BRICK_DEV, positions, tile_width),
        weight_table,
        precision=lax.Precision.HIGHEST,
    )
    bricks = sent_and_summed(brick_terms, "ori", 0)
    return (bricks, log_evidence)


def solution(mesh):
    placed = (
        P("img", None),
        P("img"),
        P("ori", "img"),
        P("img", "ori"),
        P("ori", "img", None),
        P("ori", "img"),
        P("ori", "img"),
        P(),
    )
    return jax.shard_map(
        body,
        mesh=mesh,
        in_specs=placed,
        out_specs=(P(("img", "ori"), None), P("img")),
        check_vma=False,
    )
```

profile of v0, /device:TPU:2, one launch (start us, length us, event | category | flops | bytes accessed | tf_op | source)
XLA Modules:
  0.0 714.3 jit_solution(12287116248976301158)
XLA Ops:
  7.2 0.0 copy-start
  7.2 0.0 all-gather.4.cloned.1.call-start
  7.2 0.7 all-gather.4.cloned.1.call-update
  7.9 0.0 reduce-scatter.2.cloned.1.call-start
  8.0 0.7 broadcast_compare_fusion
  8.7 0.0 copy-start.1
  8.7 296.6 %all-gather.4.cloned.1.call-done = bf16[512,4096]{0,1:T(8,128)(2,1)} async-done(((bf16[512,64]{0,1:T(8,128)(2,1)}), bf16[512,4096]{0,1:T(8,128)(2,1)}) %all-gather.4.cloned.1.call-update) | async-done | bytes 4194320 | tf_op jit(solution)/shard_map/all_gather | solution.py:77
  305.3 8.3 %fusion = (f32[1024]{0:T(1024)S(1)}, f32[1024,512]{0,1:T(8,128)S(1)}) fusion(f32[1024]{0:T(1024)} %param.11, pred[1024,2]{0,1:T(4,128)(4,1)S(1)} %broadcast_compare_fusion, bf16[1024,4096]{1,0:T(8,128)(2,1)} %param.10, bf16[512,4096]{0,1:T(8,128)(2,1)} %all-gather.4.cloned.1.call-done), kind=kOutput, calls=%fused_computation.8 | convolution fusion | flops 4297063424 | bytes 14690304 | tf_op jit(solution)/shard_map/dot_general | solution.py:75
  313.6 0.0 copy-done.1
  313.6 0.6 fusion.1
  314.2 6.7 all-gather.1
  320.9 0.2 while.17
  321.1 0.6 log_add_fusion
  321.7 0.7 multiply_convert_fusion
  322.4 10.1 %fusion.16 = f32[512,4096]{1,0:T(8,128)} fusion(bf16[1024,512]{0,1:T(8,128)(2,1)S(1)} %multiply_convert_fusion, bf16[1024,4096]{1,0:T(8,128)(2,1)} %param.10), kind=kOutput, calls=%fused_computation.40 | convolution fusion | flops 4294967296 | bytes 17825792 | tf_op jit(solution)/shard_map/dot_general | solution.py:91
  332.5 0.0 copy-start.2
  332.5 0.0 copy-start.3
  332.5 0.0 copy-start.4
  332.5 0.0 reduce-scatter.2.cloned.1.call-update
  332.5 0.6 copy-done.2
  333.2 0.6 reduce-window.6
  333.8 0.2 slice_reduce_fusion
  334.0 0.1 fusion.10
  334.2 0.0 copy-done.3
  334.2 0.0 copy-done.4
  334.2 1.4 scatter_custom_fusion
  335.6 0.7 all_to_all.12
  336.3 19.1 %all-to-all-start = ((s32[64,1,12]{2,1,0:T(1,128)}), s32[64,1,12]{2,1,0:T(1,128)S(1)}, u32[]{:S(2)}, u32[]{:S(2)}) async-start(s32[64,1,12]{2,1,0:T(1,128)} %bitcast.9), calls=%async_computation | async-start | bytes 65536 | tf_op jit(solution)/shard_map/all_to_all | solution.py:115
  355.4 303.9 %reduce-scatter.2.cloned.1.call-done = f32[8,4096]{1,0:T(8,128)} async-done(((f32[512,4096]{1,0:T(8,128)}), f32[8,4096]{1,0:T(8,128)}) %reduce-scatter.2.cloned.1.call-update) | async-done | bytes 131088 | tf_op jit(solution)/shard_map/reduce_scatter | solution.py:97
  659.3 0.9 reshape.136
  660.2 1.2 scatter_custom_fusion.1
  661.5 0.8 reshape.121
  662.3 0.0 all-to-all-done
  662.3 21.5 %all-to-all-start.1 = ((f32[64,12,128]{2,1,0:T(8,128)}), f32[64,12,128]{2,1,0:T(8,128)S(1)}, u32[]{:S(2)}, u32[]{:S(2)}) async-start(f32[64,12,128]{2,1,0:T(8,128)} %reshape.121), calls=%async_computation.2 | async-start | bytes 1048576 | tf_op jit(solution)/shard_map/all_to_all | solution.py:108
  683.8 0.5 broadcast.78
  684.4 0.7 reduce.5
  685.1 0.1 eq.59
  685.2 11.7 %all-to-all-done.1 = f32[64,12,128]{2,1,0:T(8,128)S(1)} async-done(((f32[64,12,128]{2,1,0:T(8,128)}), f32[64,12,128]{2,1,0:T(8,128)S(1)}, u32[]{:S(2)}, u32[]{:S(2)}) %all-to-all-start.1) | async-done | bytes 393248 | tf_op jit(solution)/shard_map/all_to_all | solution.py:108
  697.0 0.4 fusion.2
  697.3 0.0 copy-done
  697.3 0.5 convolution_bitcast_fusion
  697.9 8.9 %all_to_all.19 = f32[4,4,512]{2,1,0:T(4,128)S(1)} all-to-all(f32[4,4,512]{2,1,0:T(4,128)S(1)} %reshape.123), channel_id=1, replica_groups=mesh['img'=64,'ori'=4] {'ori'}, dimensions={0} | all-to-all | bytes 65536 | tf_op jit(solution)/shard_map/all_to_all | solution.py:46
  706.8 0.6 reduce_sum.32
  (18 shorter events, 0.3 us)
Async XLA Ops:
  7.2 690.2 %copy-start = (bf16[8,128,512]{2,1,0:T(8,128)(2,1)S(1)}, bf16[8,128,512]{2,1,0:T(8,128)(2,1)}, u32[]{:S(2)}) copy-start(bf16[8,128,512]{2,1,0:T(8,128)(2,1)} %param.17) | copy-start | bytes 3145732
  7.2 298.1 %all-gather.4.cloned.1.call-start = ((), (), s32[]{:S(2)}) async-start(), calls=%async_computation.4 | async-start | bytes 4259840 | tf_op jit(solution)/shard_map/all_gather | solution.py:77
  7.9 651.4 %reduce-scatter.2.cloned.1.call-start = ((), (), s32[]{:S(2)}) async-start(), calls=%async_computation.5 | async-start | bytes 8519680 | tf_op jit(solution)/shard_map/reduce_scatter | solution.py:97
  8.7 304.9 %copy-start.1 = (f32[1024]{0:T(1024)S(1)}, f32[1024]{0:T(1024)}, u32[]{:S(2)}) copy-start(f32[1024]{0:T(1024)} %param.11) | copy-start | bytes 12292
  332.5 0.7 copy-start.2
  332.5 1.7 copy-start.3
  332.5 1.7 copy-start.4
  336.3 326.0 %all-to-all-start = ((s32[64,1,12]{2,1,0:T(1,128)}), s32[64,1,12]{2,1,0:T(1,128)S(1)}, u32[]{:S(2)}, u32[]{:S(2)}) async-start(s32[64,1,12]{2,1,0:T(1,128)} %bitcast.9), calls=%async_computation | async-start | bytes 65536 | tf_op jit(solution)/shard_map/all_to_all | solution.py:115
  662.3 34.6 %all-to-all-start.1 = ((f32[64,12,128]{2,1,0:T(8,128)}), f32[64,12,128]{2,1,0:T(8,128)S(1)}, u32[]{:S(2)}, u32[]{:S(2)}) async-start(f32[64,12,128]{2,1,0:T(8,128)} %reshape.121), calls=%async_computation.2 | async-start | bytes 1048576 | tf_op jit(solution)/shard_map/all_to_all | solution.py:108
Sparse Core Ops, SparseCore 0:
  9.8 295.4 all-gather.3
  332.6 326.5 reduce-scatter.1
where the time goes:
time: 717 us; the launch traced here: 714 us
  waiting for transfers between devices  613 us (85%)
  starting transfers between devices  40.7 us (6%)
  matrix products  19.3 us (3%)
  blocking collectives  15.6 us (2%)
  between operations  14.2 us (2%)
    reduce_scatter x1, waiting for transfers between devices, body(): lax.psum_scatter(partial_value, 'img', scatter_dimension=0, tiled=True)  304 us
    all_gather x1, waiting for transfers between devices, body(): lax.all_gather(references, 'img', axis=1, tiled=True)  297 us
    all_to_all x1, starting transfers between devices, body(): lax.all_to_all(send_tiles.reshape(peers, capacity, tile_width), 'img', sp...  21.5 us
    all_to_all x1, starting transfers between devices, body(): lax.all_to_all(send_codes.reshape(peers, capacity), 'img', split_axis=0,...  19.1 us
  transfers between devices with their start and end apart: 4, of which 3 were waited for; matrix products, arithmetic and copies ran while one was open for 1% of the time, Pallas kernels for 0%

commit v1 on v0

v1 whole, which is shorter than its diff:
```python
import functools
import math

import jax
import jax.numpy as jnp
from jax import lax
from jax.experimental import pallas as pl
from jax.experimental.pallas import tpu as pltpu
from jax.sharding import Mesh
from jax.sharding import PartitionSpec as P

BF16, F32, I32 = jnp.bfloat16, jnp.float32, jnp.int32
AXES = {"y": 4, "xl": 2, "z": 8, "xh": 2, "core": 2}
IMG, ORI = ("y", "xl", "z"), ("xh", "core")
REFS, VALUES, IMAGES = 512, 4096, 1024
SHARE = 64
CELLS = 8192
LANES = 128
VMEM = 58 * 2**20


def moved(x, axes, target):
    sizes = [AXES[a] for a in axes]
    pairs = []
    for i in range(math.prod(sizes)):
        at, k = [], i
        for n in reversed(sizes):
            at.insert(0, k % n)
            k //= n
        to = 0
        for n, c in zip(sizes, target(*at)):
            to = to * n + c % n
        pairs.append((i, to))
    return lax.ppermute(x, axes, pairs)


def along_x(x, step):
    def target(xl, xh):
        at = (xh * 2 + xl + step) % 4
        return at % 2, at // 2

    return moved(x, ("xl", "xh"), target)


def spread(x, axes):
    n = math.prod(AXES[a] for a in axes)
    return lax.all_to_all(jnp.broadcast_to(x[None], (n, *x.shape)), axes, 0, 0)


def gathered_references(references, cut):
    share = references.T
    near = spread(share[:cut], ("y", "xl"))
    ended_z = lax.all_gather(near, "z", axis=0)
    own = spread(share[cut:], ("z",))
    other = moved(own, ("xl",), lambda xl: (xl + 1,))
    pair = jnp.stack([own, other])
    ended_y = [pair] + [moved(pair, ("y",), lambda y: (y + d,)) for d in (1, 2, 3)]
    return [ended_z, *ended_y]


def eye():
    return lax.broadcasted_iota(I32, (LANES, LANES), 0) == lax.broadcasted_iota(
        I32, (LANES, LANES), 1
    )


def scores_kernel(
    cut, me, images, scale, pattern, by_z, y0, y1, y2, y3, expo, peaks, masses, refs, sems
):
    step = pl.program_id(0)
    rows = images.shape[0]

    @pl.when(step == 0)
    def _():
        copies = [(by_z.at[z], refs.at[:, z, pl.ds(0, cut)]) for z in range(8)]
        for d, part in enumerate((y0, y1, y2, y3)):
            y = (me[0] + 4 - d) % 4
            for r in range(2):
                xl = (me[1] + r) % 2
                copies.append((part.at[r], refs.at[y * 2 + xl, :, pl.ds(cut, SHARE - cut)]))
        copies = [pltpu.make_async_copy(a, b, sems.at[i]) for i, (a, b) in enumerate(copies)]
        for c in copies:
            c.start()
        for c in copies:
            c.wait()

    total = jnp.zeros((rows, REFS), F32)
    wide = 8 * SHARE
    for q in range(8):
        total += jnp.dot(
            images[:, q * wide : (q + 1) * wide],
            refs[q].reshape(wide, REFS),
            preferred_element_type=F32,
        )
    scores = total * scale[...] * (1.0 / math.sqrt(VALUES))
    group = lax.broadcasted_iota(I32, (rows, REFS), 1) // (REFS // 2)
    flags = pattern[...]
    active = jnp.where(group == 0, flags[:, 0:1], flags[:, 1:2]) > 0
    masked = jnp.where(active, scores, -1e30)
    peak = jnp.max(masked, axis=1, keepdims=True)
    value = jnp.where(active, jnp.exp(masked - peak), 0.0)
    mass = jnp.sum(value, axis=1, keepdims=True)
    expo[...] = value
    for j in range(rows // LANES):
        part = slice(j * LANES, (j + 1) * LANES)
        row = pl.ds(step * (rows // LANES) + j, 1)
        peaks[row, :] = jnp.sum(jnp.where(eye(), peak[part], 0.0), axis=0, keepdims=True)
        masses[row, :] = jnp.sum(jnp.where(eye(), mass[part], 0.0), axis=0, keepdims=True)


def scores_of(me, images, scale, pattern, parts, cut, rows=256):
    here = pl.BlockSpec((8, LANES), lambda i: (0, 0))
    return pl.pallas_call(
        functools.partial(scores_kernel, cut),
        grid=(IMAGES // rows,),
        in_specs=[
            pl.BlockSpec(memory_space=pltpu.SMEM),
            pl.BlockSpec((rows, VALUES), lambda i: (i, 0)),
            pl.BlockSpec((rows, 1), lambda i: (i, 0)),
            pl.BlockSpec((rows, 2), lambda i: (i, 0)),
        ]
        + [pl.BlockSpec(memory_space=pl.ANY)] * len(parts),
        out_specs=[pl.BlockSpec((rows, REFS), lambda i: (i, 0)), here, here],
        out_shape=[
            jax.ShapeDtypeStruct((IMAGES, REFS), F32),
            jax.ShapeDtypeStruct((8, LANES), F32),
            jax.ShapeDtypeStruct((8, LANES), F32),
        ],
        scratch_shapes=[
            pltpu.VMEM((8, 8, SHARE, REFS), BF16),
            pltpu.SemaphoreType.DMA((16,)),
        ],
        compiler_params=pltpu.CompilerParams(vmem_limit_bytes=VMEM),
        name="scores",
    )(me, images, scale, pattern, *parts)


UNROLL = 32


def bricks_kernel(cells, factor, expo, images, weights, out, scaled, tiles, c0, c1, c2, c3):
    step = pl.program_id(0)
    sums = (c0, c1, c2, c3)

    @pl.when(step == 0)
    def _():
        for j in range(IMAGES // LANES):
            part = slice(j * LANES, (j + 1) * LANES)
            column = jnp.sum(
                jnp.where(eye(), factor[j : j + 1, :], 0.0), axis=1, keepdims=True
            )
            scaled[:, part] = (expo[part, :] * column).T.astype(BF16)

        def clear(i, _):
            for c in sums:
                c[pl.ds(i * 256, 256), :] = jnp.zeros((256, LANES), F32)
            return 0

        lax.fori_loop(0, CELLS // 256, clear, 0)

    block = jnp.dot(scaled[...], images[...], preferred_element_type=F32)
    tiles[0:REFS, :] = block[:, 0:LANES]
    tiles[REFS:, :] = block[:, LANES:]

    def add(i, _):
        for u in range(UNROLL):
            row = i * UNROLL + u
            cell = pl.ds(cells[step * (2 * REFS) + row], 1)
            c = sums[u % 4]
            c[cell, :] = c[cell, :] + tiles[pl.ds(row, 1), :]
        return 0

    lax.fori_loop(0, 2 * REFS // UNROLL, add, 0)

    @pl.when(step == pl.num_programs(0) - 1)
    def _():
        for r in range(0, 1024, 256):
            total = jnp.zeros((256, weights.shape[2]), F32)
            for p in range(8):
                part = pl.ds(p * 1024 + r, 256)
                cell = (c0[part, :] + c1[part, :]) + (c2[part, :] + c3[part, :])
                high = cell.astype(BF16)
                low = (cell - high.astype(F32)).astype(BF16)
                w = weights[p]
                total += jnp.dot(
                    jnp.concatenate([high, low], axis=1),
                    jnp.concatenate([w, w], axis=0),
                    preferred_element_type=F32,
                )
            out[r : r + 256, :] = total


def bricks_of(cells, factor, expo, images, weights):
    positions, width, voxels = weights.shape
    wide = 2 * LANES
    return pl.pallas_call(
        bricks_kernel,
        grid=(VALUES // wide,),
        in_specs=[
            pl.BlockSpec(memory_space=pltpu.SMEM),
            pl.BlockSpec((8, LANES), lambda i: (0, 0)),
            pl.BlockSpec((IMAGES, REFS), lambda i: (0, 0)),
            pl.BlockSpec((IMAGES, wide), lambda i: (0, i)),
            pl.BlockSpec((positions, width, voxels), lambda i: (0, 0, 0)),
        ],
        out_specs=pl.BlockSpec((CELLS // positions, voxels), lambda i: (0, 0)),
        out_shape=jax.ShapeDtypeStruct((CELLS // positions, voxels), F32),
        scratch_shapes=[
            pltpu.VMEM((REFS, IMAGES), BF16),
            pltpu.VMEM((2 * REFS, LANES), F32),
        ]
        + [pltpu.VMEM((CELLS, LANES), F32)] * 4,
        compiler_params=pltpu.CompilerParams(vmem_limit_bytes=VMEM),
        name="bricks",
    )(cells, factor, expo, images, weights)


def merged(pairs):
    peak = functools.reduce(jnp.maximum, [p for p, _ in pairs])
    return peak, sum(m * jnp.exp(p - peak) for p, m in pairs)


def brick_share(terms, me_free=None):
    voxels = terms.shape[1]
    x = terms.reshape(2, -1, voxels)
    x = x[0] + moved(x[1], ("core",), lambda c: (c + 1,))
    x = x.reshape(4, -1, voxels)
    got = [moved(x[d].astype(BF16), ("y",), lambda y: (y + d,)) for d in (1, 2, 3)]
    x = x[0] + sum(g.astype(F32) for g in got)
    x = x.reshape(4, -1, voxels)
    got = [along_x(x[d], d) for d in (1, 2, 3)]
    x = x[0] + sum(got)
    x = x.reshape(8, -1, voxels)
    for half in (4, 2, 1):
        x = x[:half] + moved(x[half:], ("z",), lambda z: (z ^ half,))
    return x[0]


def body(images, img_scale, references, pattern, tile_owner, tile_brick, tile_block, weights):
    cut = 32
    at = {a: lax.axis_index(a) for a in AXES}
    parts = gathered_references(references, cut)

    code = tile_owner.reshape(-1) * 16 + tile_brick.reshape(-1)
    code = code * 8 + tile_block.reshape(-1)
    code = lax.all_gather(code, IMG, axis=0, tiled=True).reshape(REFS, -1).T.reshape(-1)
    block, row = code % 8, code // 8 % 4
    core, xh = code // 32 % 2, code // 64 % 2
    z, xl, y = code // 128 % 8, code // 1024 % 2, code // 2048
    away = jnp.bitwise_xor(core, at["core"]) * 4 + (y - at["y"]) % 4
    away = away * 4 + (xh * 2 + xl - at["xh"] * 2 - at["xl"]) % 4
    away = away * 8 + jnp.bitwise_xor(z, at["z"])
    cells = block * (CELLS // 8) + away * 4 + row

    me = jnp.stack([at["y"], at["xl"]]).astype(I32)
    expo, peak, mass = scores_of(me, images, img_scale[:, None], pattern, parts, cut)
    mine = jnp.concatenate([peak, mass])
    others = [
        moved(mine, ORI, lambda h, c: (h + dh, c + dc)) for dh, dc in ((0, 1), (1, 0), (1, 1))
    ]
    all_peak, all_mass = merged([(s[:8], s[8:]) for s in (mine, *others)])
    factor = jnp.exp(peak - all_peak) / all_mass * img_scale.reshape(8, LANES)
    terms = bricks_of(cells, factor, expo, images, weights)
    log_evidence = (all_peak + jnp.log(all_mass)).reshape(-1)
    return brick_share(terms), log_evidence


def solution(mesh):
    cut_mesh = Mesh(mesh.devices.reshape(*AXES.values()), tuple(AXES))
    placed = (
        P(IMG, None),
        P(IMG),
        P(ORI, IMG),
        P(IMG, ORI),
        P(ORI, IMG, None),
        P(ORI, IMG),
        P(ORI, IMG),
        P(),
    )
    return jax.shard_map(
        body,
        mesh=cut_mesh,
        in_specs=placed,
        out_specs=(P(IMG + ORI, None), P(IMG)),
        check_vma=False,
    )
```

time: 717 us -> 310 us (0.43)
  waiting for transfers between devices: 613 us -> 33.9 us
  blocking collectives: 15.6 us -> 167 us
  Pallas kernels: 0 us -> 49.5 us
  matrix products: 19.3 us -> 0 us
  starting transfers between devices: 40.7 us -> 31.4 us
    reduce_scatter x1 -> x0, waiting for transfers between devices: 304 us -> none  [body(): lax.psum_scatter(partial_value, 'img', scatter_dimension=0, tiled=True)]
    all_gather x1, waiting for transfers between devices: 297 us -> 0.02 us  [gathered_references(): ended_z = lax.all_gather(near, 'z', axis=0)]
    all_gather x1, blocking collectives: 6.7 us -> 137 us  [body(): lax.all_gather(code, IMG, axis=0, tiled=True).reshape(REFS, -1)]
    pallas_call x0 -> x2, Pallas kernels: none -> 49.5 us  [the longest x1 38.4 us: bricks_of(): pl.pallas_call(bricks_kernel, grid=(VALUES // wide,), in_specs=[pl.BlockS...]
    all_to_all x2 -> x0, starting transfers between devices: 40.6 us -> none  [the longest x1 21.5 us: body(): lax.all_to_all(send_tiles.reshape(peers, capacity, tile_width), 'img', sp...]
    ppermute x0 -> x17, waiting for transfers between devices: none -> 33.8 us  [moved(): return lax.ppermute(x, axes, pairs)]
    ppermute x0 -> x17, starting transfers between devices: none -> 31.3 us  [moved(): return lax.ppermute(x, axes, pairs)]
    all_to_all x1 -> x2, blocking collectives: 8.94 us -> 30.6 us  [spread(): return lax.all_to_all(jnp.broadcast_to(x[None], (n, *x.shape)), axes, 0, 0)]
  transfers between devices with their start and end apart: 4 -> 18, of which waited for: 3 -> 12; matrix products, arithmetic and copies ran while one was open for 1% -> 2% of each run, Pallas kernels for 0% -> 0%
where the time goes in v1:
time: 310 us
  blocking collectives  167 us (54%)
  Pallas kernels  49.5 us (16%)
  waiting for transfers between devices  33.9 us (11%)
  starting transfers between devices  31.4 us (10%)
  between operations  14.3 us (5%)
  local copies, waits for them, and re-layouts  7.84 us (3%)
  other arithmetic  5.38 us (2%)
    all_gather x1, blocking collectives, body(): lax.all_gather(code, IMG, axis=0, tiled=True).reshape(REFS, -1)  137 us
    pallas_call x1, Pallas kernels, bricks_of(): pl.pallas_call(bricks_kernel, grid=(VALUES // wide,), in_specs=[pl.BlockS...  38.4 us
    ppermute x17, waiting for transfers between devices, moved(): return lax.ppermute(x, axes, pairs)  33.8 us
    ppermute x17, starting transfers between devices, moved(): return lax.ppermute(x, axes, pairs)  31.3 us
    all_to_all x2, blocking collectives, spread(): return lax.all_to_all(jnp.broadcast_to(x[None], (n, *x.shape)), axes, 0, 0)  30.6 us
    pallas_call x1, Pallas kernels, scores_of(): pl.pallas_call(functools.partial(scores_kernel, cut), grid=(IMAGES // row...  11.1 us
  transfers between devices with their start and end apart: 18, of which 12 were waited for; matrix products, arithmetic and copies ran while one was open for 2% of the time, Pallas kernels for 0%

profile of v1, /device:TPU:2, one launch (start us, length us, event | category | flops | bytes accessed | tf_op | source)
XLA Modules:
  0.0 309.5 jit_solution(6049859887773807149)
XLA Ops:
  7.3 0.8 fusion.44
  8.1 11.9 %all_to_all.10 = bf16[8,32,512]{2,1,0:T(8,128)(2,1)} all-to-all(bf16[8,32,512]{2,1,0:T(8,128)(2,1)S(1)} %broadcast_in_dim.7), channel_id=1, replica_groups=mesh['y'=4,'xl'=2,'z'=8,'xh'=2,'core'=2] {'y','xl'}, dimensions={0} | all-to-all | bytes 524288 | tf_op jit(solution)/shard_map/all_to_all | solution.py:47
  20.1 18.7 %all_to_all.11 = bf16[8,32,512]{2,1,0:T(8,128)(2,1)S(1)} all-to-all(bf16[8,32,512]{2,1,0:T(8,128)(2,1)S(1)} %broadcast_in_dim.8), channel_id=1, replica_groups=mesh['y'=4,'xl'=2,'z'=8,'xh'=2,'core'=2] {'z'}, dimensions={0} | all-to-all | bytes 524288 | tf_op jit(solution)/shard_map/all_to_all | solution.py:47
  38.7 1.5 collective-permute-start
  40.2 1.7 copy.15.scale
  42.0 1.1 copy.16.pattern
  43.0 2.1 collective-permute-done
  45.2 1.2 collective-permute-start.1
  46.3 1.7 collective-permute-start.2
  48.1 1.0 collective-permute-start.3
  49.1 136.7 %all-gather.1 = s32[64,1,256]{2,1,0:T(1,128)S(1)} all-gather(s32[1,1,256]{2,1,0:T(1,128)S(1)} %bitcast.28), channel_id=1, replica_groups=mesh['y'=4,'xl'=2,'z'=8,'xh'=2,'core'=2] {'y','xl','z'}, dimensions={0}, use_global_device_ids=true | all-gather | bytes 66560 | tf_op jit(solution)/shard_map/all_gather | solution.py:246
  185.8 0.2 reduce
  186.0 0.1 reshape.55
  186.1 0.1 copy.14
  186.2 0.6 pad_add_fusion.me
  186.9 0.7 copy-done.2
  187.7 0.2 copy-done.3
  187.9 0.1 copy-done.4
  188.0 11.1 %scores.1 = (f32[1024,512]{1,0:T(8,128)}, f32[8,128]{1,0:T(8,128)}, f32[8,128]{1,0:T(8,128)}) custom-call(s32[2]{0:T(128)} %pad_add_fusion.me, bf16[1024,4096]{1,0:T(8,128)(2,1)} %images.3, f32[1024,1]{1,0:T(8,128)} %copy.15.scale, s32[1024,2]{1,0:T(8,128)} %copy.16.pattern, bf16[8,8,32,512]{3,2,1,0:T(8,128)(2,1)} %bitcast.20, ...), custom_call_target="tpu_custom_call" | custom-call | tf_op jit(solution)/shard_map/scores/pallas_call | solution.py:113
  199.1 0.7 constant_dynamic-update-slice_fusion.1
  199.8 0.7 constant_dynamic-update-slice_fusion
  200.4 1.7 collective-permute-start.5
  202.2 1.6 collective-permute-start.6
  203.8 1.0 fusion.2.cells
  204.8 0.8 collective-permute-done.5
  205.6 1.1 collective-permute-done.6
  206.7 1.3 add_bitcast_fusion
  208.1 1.3 bitcast_multiply_fusion.factor
  209.3 38.4 %bricks.1 = f32[1024,512]{1,0:T(8,128)} custom-call(s32[16384]{0:T(1024)} %fusion.2.cells, f32[8,128]{1,0:T(8,128)} %bitcast_multiply_fusion.factor, f32[1024,512]{1,0:T(8,128)} %get-tuple-element.7.expo, bf16[1024,4096]{1,0:T(8,128)(2,1)} %images.3, bf16[8,128,512]{2,1,0:T(8,128)(2,1)} %weights.1), custom_call_target="tpu_custom_call" | custom-call | tf_op jit(solution)/shard_map/bricks/pallas_call | solution.py:196
  247.8 1.4 slice.126
  249.2 0.3 collective-permute-start.7
  249.5 2.4 collective-permute-done.7
  252.0 0.3 fusion.40
  252.3 1.4 collective-permute-start.10
  253.7 0.8 collective-permute-start.8
  254.6 0.7 collective-permute-start.9
  255.3 2.9 collective-permute-done.10
  258.2 5.0 %collective-permute-done.8 = bf16[128,512]{1,0:T(8,128)(2,1)S(1)} collective-permute-done((bf16[128,512]{1,0:T(8,128)(2,1)S(1)}, bf16[128,512]{1,0:T(8,128)(2,1)S(1)}, u32[]{:S(2)}, u32[]{:S(2)}) %collective-permute-start.8) | collective-permute-done | bytes 131104 | tf_op jit(solution)/shard_map/ppermute | solution.py:34
  263.2 15.2 %collective-permute-start.11 = (f32[32,512]{1,0:T(8,128)S(1)}, f32[32,512]{1,0:T(8,128)S(1)}, u32[]{:S(2)}, u32[]{:S(2)}) collective-permute-start(f32[32,512]{1,0:T(8,128)S(1)} %get-tuple-element.18), channel_id=1, source_target_pairs={{0,32},{2,34},{32,2},{34,0},{1,33},{3,35},{33,3},{35,1},{4,36},{6,... | collective-permute-start | bytes 196616 | tf_op jit(solution)/shard_map/ppermute | solution.py:34
  278.4 2.9 collective-permute-start.12
  281.3 0.6 collective-permute-done.11
  282.0 2.2 collective-permute-done.12
  284.2 1.4 collective-permute-done.13
  285.8 7.8 %collective-permute-done.14 = f32[4,4,512]{2,1,0:T(4,128)S(1)} collective-permute-done((f32[4,4,512]{2,1,0:T(4,128)S(1)}, f32[4,4,512]{2,1,0:T(4,128)S(1)}, u32[]{:S(2)}, u32[]{:S(2)}) %collective-permute-start.14) | collective-permute-done | bytes 32800 | tf_op jit(solution)/shard_map/ppermute | solution.py:34
  293.7 4.6 %collective-permute-done.15 = f32[2,4,512]{2,1,0:T(4,128)S(1)} collective-permute-done((f32[2,4,512]{2,1,0:T(4,128)S(1)}, f32[2,4,512]{2,1,0:T(4,128)S(1)}, u32[]{:S(2)}, u32[]{:S(2)}) %collective-permute-start.15) | collective-permute-done | bytes 16416 | tf_op jit(solution)/shard_map/ppermute | solution.py:34
  298.3 0.9 collective-permute-start.16
  299.2 2.9 collective-permute-done.16
  302.1 0.6 fusion.35
  (46 shorter events, 0.6 us)
Async XLA Ops:
  7.2 34.8 %copy-start.6 = (s32[1024,2]{0,1:T(2,128)S(1)}, s32[1024,2]{0,1:T(2,128)}, u32[]{:S(2)}) copy-start(s32[1024,2]{0,1:T(2,128)} %param.11) | copy-start | bytes 24580
  7.2 41.9 %copy-start.7 = (s32[1,256,1]{1,2,0:T(1,128)S(1)}, s32[1,256,1]{1,2,0:T(1,128)}, u32[]{:S(2)}) copy-start(s32[1,256,1]{1,2,0:T(1,128)} %param.12) | copy-start | bytes 3076
  7.2 41.9 %copy-start.9 = (s32[1,256]{1,0:T(1,128)S(1)}, s32[1,256]{1,0:T(1,128)}, u32[]{:S(2)}) copy-start(s32[1,256]{1,0:T(1,128)} %param.13) | copy-start | bytes 3076
  7.2 41.9 %copy-start.8 = (s32[1,256]{1,0:T(1,128)S(1)}, s32[1,256]{1,0:T(1,128)}, u32[]{:S(2)}) copy-start(s32[1,256]{1,0:T(1,128)} %param.14) | copy-start | bytes 3076
  7.2 179.7 %all-gather.4.cloned.1.call-start = ((), (), s32[]{:S(2)}) async-start(), calls=%async_computation.2 | async-start | bytes 2359296 | tf_op jit(solution)/shard_map/all_gather | solution.py:53
  38.7 6.4 %collective-permute-start = (bf16[8,32,512]{2,1,0:T(8,128)(2,1)S(1)}, bf16[8,32,512]{2,1,0:T(8,128)(2,1)S(1)}, u32[]{:S(2)}, u32[]{:S(2)}) collective-permute-start(bf16[8,32,512]{2,1,0:T(8,128)(2,1)S(1)} %all_to_all.11), channel_id=1, source_target_pairs={{0,32},{32,0},{1,33},{33,1},{2,34},{34,2},{3,35},{35,3},{4,36},{36... | collective-permute-start | bytes 786440 | tf_op jit(solution)/shard_map/ppermute | solution.py:34
  45.1 141.8 %copy-start.1 = (bf16[2,8,32,512]{3,2,1,0:T(8,128)(2,1)}, bf16[2,8,32,512]{3,2,1,0:T(8,128)(2,1)S(1)}, u32[]{:S(2)}) copy-start(bf16[2,8,32,512]{3,2,1,0:T(8,128)(2,1)S(1)} %pad_maximum_fusion.y0) | copy-start | bytes 1572868
  45.2 141.7 %collective-permute-start.1 = (bf16[2,8,32,512]{3,2,1,0:T(8,128)(2,1)S(1)}, bf16[2,8,32,512]{3,2,1,0:T(8,128)(2,1)S(1)}, u32[]{:S(2)}, u32[]{:S(2)}) collective-permute-start(bf16[2,8,32,512]{3,2,1,0:T(8,128)(2,1)S(1)} %pad_maximum_fusion.y0), channel_id=1, source_target_pairs={{0,64},{64,128},{128,192},{192,0},{1,65},{65,129},{129,193},{193,1... | collective-permute-start | bytes 1572872 | tf_op jit(solution)/shard_map/ppermute | solution.py:34
  46.3 140.5 %collective-permute-start.2 = (bf16[2,8,32,512]{3,2,1,0:T(8,128)(2,1)S(1)}, bf16[2,8,32,512]{3,2,1,0:T(8,128)(2,1)S(1)}, u32[]{:S(2)}, u32[]{:S(2)}) collective-permute-start(bf16[2,8,32,512]{3,2,1,0:T(8,128)(2,1)S(1)} %pad_maximum_fusion.y0), channel_id=1, source_target_pairs={{0,128},{64,192},{128,0},{192,64},{1,129},{65,193},{129,1},{193,65... | collective-permute-start | bytes 1572872 | tf_op jit(solution)/shard_map/ppermute | solution.py:34
  48.1 138.8 %collective-permute-start.3 = (bf16[2,8,32,512]{3,2,1,0:T(8,128)(2,1)S(1)}, bf16[2,8,32,512]{3,2,1,0:T(8,128)(2,1)S(1)}, u32[]{:S(2)}, u32[]{:S(2)}) collective-permute-start(bf16[2,8,32,512]{3,2,1,0:T(8,128)(2,1)S(1)} %pad_maximum_fusion.y0), channel_id=1, source_target_pairs={{0,192},{64,0},{128,64},{192,128},{1,193},{65,1},{129,65},{193,129... | collective-permute-start | bytes 1572872 | tf_op jit(solution)/shard_map/ppermute | solution.py:34
  186.9 0.8 copy-start.2
  186.9 1.0 copy-start.3
  186.9 1.1 copy-start.4
  188.0 20.1 %copy-start.5 = (f32[1024]{0:T(1024)S(1)}, f32[1024]{0:T(1024)}, u32[]{:S(2)}) copy-start(f32[1024]{0:T(1024)} %param.9) | copy-start | bytes 12292
  200.4 4.4 %collective-permute-start.4 = (f32[16,128]{1,0:T(8,128)S(1)}, f32[16,128]{1,0:T(8,128)S(1)}, u32[]{:S(2)}, u32[]{:S(2)}) collective-permute-start(f32[16,128]{1,0:T(8,128)S(1)} %constant_dynamic-update-slice_fusion), channel_id=1, source_target_pairs={{0,1},{1,0},{2,3},{3,2},{4,5},{5,4},{6,7},{7,6},{8,9},{9,8},{10,11... | collective-permute-start | bytes 24584 | tf_op jit(solution)/shard_map/ppermute | solution.py:34
  200.4 5.2 %collective-permute-start.5 = (f32[16,128]{1,0:T(8,128)S(1)}, f32[16,128]{1,0:T(8,128)S(1)}, u32[]{:S(2)}, u32[]{:S(2)}) collective-permute-start(f32[16,128]{1,0:T(8,128)S(1)} %constant_dynamic-update-slice_fusion), channel_id=1, source_target_pairs={{0,2},{1,3},{2,0},{3,1},{4,6},{5,7},{6,4},{7,5},{8,10},{9,11},{10,... | collective-permute-start | bytes 24584 | tf_op jit(solution)/shard_map/ppermute | solution.py:34
  202.2 4.6 %collective-permute-start.6 = (f32[16,128]{1,0:T(8,128)S(1)}, f32[16,128]{1,0:T(8,128)S(1)}, u32[]{:S(2)}, u32[]{:S(2)}) collective-permute-start(f32[16,128]{1,0:T(8,128)S(1)} %constant_dynamic-update-slice_fusion), channel_id=1, source_target_pairs={{0,3},{1,2},{2,1},{3,0},{4,7},{5,6},{6,5},{7,4},{8,11},{9,10},{10,... | collective-permute-start | bytes 24584 | tf_op jit(solution)/shard_map/ppermute | solution.py:34
  247.8 4.2 %copy-start = (f32[1024,512]{1,0:T(8,128)S(1)}, f32[1024,512]{1,0:T(8,128)}, u32[]{:S(2)}) copy-start(f32[1024,512]{1,0:T(8,128)} %bricks.1) | copy-start | bytes 6291460
  249.2 2.7 collective-permute-start.7
  252.3 5.9 %collective-permute-start.10 = (bf16[128,512]{1,0:T(8,128)(2,1)S(1)}, bf16[128,512]{1,0:T(8,128)(2,1)S(1)}, u32[]{:S(2)}, u32[]{:S(2)}) collective-permute-start(bf16[128,512]{1,0:T(8,128)(2,1)S(1)} %get-tuple-element.14), channel_id=1, source_target_pairs={{0,192},{64,0},{128,64},{192,128},{1,193},{65,1},{129,65},{193,129... | collective-permute-start | bytes 393224 | tf_op jit(solution)/shard_map/ppermute | solution.py:34
  253.7 9.4 %collective-permute-start.8 = (bf16[128,512]{1,0:T(8,128)(2,1)S(1)}, bf16[128,512]{1,0:T(8,128)(2,1)S(1)}, u32[]{:S(2)}, u32[]{:S(2)}) collective-permute-start(bf16[128,512]{1,0:T(8,128)(2,1)S(1)} %get-tuple-element.13), channel_id=1, source_target_pairs={{0,64},{64,128},{128,192},{192,0},{1,65},{65,129},{129,193},{193,1... | collective-permute-start | bytes 393224 | tf_op jit(solution)/shard_map/ppermute | solution.py:34
  254.6 8.6 %collective-permute-start.9 = (bf16[128,512]{1,0:T(8,128)(2,1)S(1)}, bf16[128,512]{1,0:T(8,128)(2,1)S(1)}, u32[]{:S(2)}, u32[]{:S(2)}) collective-permute-start(bf16[128,512]{1,0:T(8,128)(2,1)S(1)} %get-tuple-element.15), channel_id=1, source_target_pairs={{0,128},{64,192},{128,0},{192,64},{1,129},{65,193},{129,1},{193,65... | collective-permute-start | bytes 393224 | tf_op jit(solution)/shard_map/ppermute | solution.py:34
  263.2 18.8 %collective-permute-start.11 = (f32[32,512]{1,0:T(8,128)S(1)}, f32[32,512]{1,0:T(8,128)S(1)}, u32[]{:S(2)}, u32[]{:S(2)}) collective-permute-start(f32[32,512]{1,0:T(8,128)S(1)} %get-tuple-element.18), channel_id=1, source_target_pairs={{0,32},{2,34},{32,2},{34,0},{1,33},{3,35},{33,3},{35,1},{4,36},{6,... | collective-permute-start | bytes 196616 | tf_op jit(solution)/shard_map/ppermute | solution.py:34
  278.4 5.8 %collective-permute-start.12 = (f32[32,512]{1,0:T(8,128)S(1)}, f32[32,512]{1,0:T(8,128)S(1)}, u32[]{:S(2)}, u32[]{:S(2)}) collective-permute-start(f32[32,512]{1,0:T(8,128)S(1)} %get-tuple-element.16), channel_id=1, source_target_pairs={{0,2},{2,0},{32,34},{34,32},{1,3},{3,1},{33,35},{35,33},{4,6},{6,4... | collective-permute-start | bytes 196616 | tf_op jit(solution)/shard_map/ppermute | solution.py:34
  281.3 4.3 %collective-permute-start.13 = (f32[32,512]{1,0:T(8,128)S(1)}, f32[32,512]{1,0:T(8,128)S(1)}, u32[]{:S(2)}, u32[]{:S(2)}) collective-permute-start(f32[32,512]{1,0:T(8,128)S(1)} %get-tuple-element.17), channel_id=1, source_target_pairs={{0,34},{2,32},{32,0},{34,2},{1,35},{3,33},{33,1},{35,3},{4,38},{6,... | collective-permute-start | bytes 196616 | tf_op jit(solution)/shard_map/ppermute | solution.py:34
  285.7 7.9 %collective-permute-start.14 = (f32[4,4,512]{2,1,0:T(4,128)S(1)}, f32[4,4,512]{2,1,0:T(4,128)S(1)}, u32[]{:S(2)}, u32[]{:S(2)}) collective-permute-start(f32[4,4,512]{2,1,0:T(4,128)S(1)} %slice.112), channel_id=1, source_target_pairs={{0,16},{4,20},{8,24},{12,28},{16,0},{20,4},{24,8},{28,12},{1,17},{... | collective-permute-start | bytes 98312 | tf_op jit(solution)/shard_map/ppermute | solution.py:34
  293.6 4.7 %collective-permute-start.15 = (f32[2,4,512]{2,1,0:T(4,128)S(1)}, f32[2,4,512]{2,1,0:T(4,128)S(1)}, u32[]{:S(2)}, u32[]{:S(2)}) collective-permute-start(f32[2,4,512]{2,1,0:T(4,128)S(1)} %slice.138), channel_id=1, source_target_pairs={{0,8},{4,12},{8,0},{12,4},{16,24},{20,28},{24,16},{28,20},{1,9},{5... | collective-permute-start | bytes 49160 | tf_op jit(solution)/shard_map/ppermute | solution.py:34
  298.3 3.7 %collective-permute-start.16 = (f32[1,4,512]{2,1,0:T(4,128)S(1)}, f32[1,4,512]{2,1,0:T(4,128)S(1)}, u32[]{:S(2)}, u32[]{:S(2)}) collective-permute-start(f32[1,4,512]{2,1,0:T(4,128)S(1)} %slice.140), channel_id=1, source_target_pairs={{0,4},{4,0},{8,12},{12,8},{16,20},{20,16},{24,28},{28,24},{1,5},{5... | collective-permute-start | bytes 24584 | tf_op jit(solution)/shard_map/ppermute | solution.py:34
Sparse Core Ops, SparseCore 0:
  20.2 43.3 all-gather.3

commit v2 on v1

--- a/solution.py
+++ b/solution.py
@@ -47,9 +47,10 @@
     return lax.all_to_all(jnp.broadcast_to(x[None], (n, *x.shape)), axes, 0, 0)
 
 
-def gathered_references(references, cut):
+def gathered_references(references, codes, cut):
     share = references.T
-    near = spread(share[:cut], ("y", "xl"))
+    more = jnp.pad(codes.astype(BF16)[None], ((0, 7), (0, 0)))
+    near = spread(jnp.concatenate([share[:cut], more]), ("y", "xl"))
     ended_z = lax.all_gather(near, "z", axis=0)
     own = spread(share[cut:], ("z",))
     other = moved(own, ("xl",), lambda xl: (xl + 1,))
@@ -65,14 +66,14 @@
 
 
 def scores_kernel(
-    cut, me, images, scale, pattern, by_z, y0, y1, y2, y3, expo, peaks, masses, refs, sems
+    cut, me, images, scale, pattern, by_z, y0, y1, y2, y3, expo, stats, refs, sems
 ):
     step = pl.program_id(0)
     rows = images.shape[0]
 
     @pl.when(step == 0)
     def _():
-        copies = [(by_z.at[z], refs.at[:, z, pl.ds(0, cut)]) for z in range(8)]
+        copies = [(by_z.at[z, :, pl.ds(0, cut)], refs.at[:, z, pl.ds(0, cut)]) for z in range(8)]
         for d, part in enumerate((y0, y1, y2, y3)):
             y = (me[0] + 4 - d) % 4
             for r in range(2):
@@ -103,13 +104,14 @@
     expo[...] = value
     for j in range(rows // LANES):
         part = slice(j * LANES, (j + 1) * LANES)
-        row = pl.ds(step * (rows // LANES) + j, 1)
-        peaks[row, :] = jnp.sum(jnp.where(eye(), peak[part], 0.0), axis=0, keepdims=True)
-        masses[row, :] = jnp.sum(jnp.where(eye(), mass[part], 0.0), axis=0, keepdims=True)
+        at = step * (rows // LANES) + j
+        for k, column in enumerate((peak, mass)):
+            stats[pl.ds(k * 8 + at, 1), :] = jnp.sum(
+                jnp.where(eye(), column[part], 0.0), axis=0, keepdims=True
+            )
 
 
 def scores_of(me, images, scale, pattern, parts, cut, rows=256):
-    here = pl.BlockSpec((8, LANES), lambda i: (0, 0))
     return pl.pallas_call(
         functools.partial(scores_kernel, cut),
         grid=(IMAGES // rows,),
@@ -120,11 +122,13 @@
             pl.BlockSpec((rows, 2), lambda i: (i, 0)),
         ]
         + [pl.BlockSpec(memory_space=pl.ANY)] * len(parts),
-        out_specs=[pl.BlockSpec((rows, REFS), lambda i: (i, 0)), here, here],
+        out_specs=[
+            pl.BlockSpec((rows, REFS), lambda i: (i, 0)),
+            pl.BlockSpec((16, LANES), lambda i: (0, 0)),
+        ],
         out_shape=[
             jax.ShapeDtypeStruct((IMAGES, REFS), F32),
-            jax.ShapeDtypeStruct((8, LANES), F32),
-            jax.ShapeDtypeStruct((8, LANES), F32),
+            jax.ShapeDtypeStruct((16, LANES), F32),
         ],
         scratch_shapes=[
             pltpu.VMEM((8, 8, SHARE, REFS), BF16),
@@ -138,12 +142,20 @@
 UNROLL = 32
 
 
-def bricks_kernel(cells, factor, expo, images, weights, out, scaled, tiles, c0, c1, c2, c3):
+def bricks_kernel(
+    cells, scale, s0, s1, s2, s3, expo, images, weights,
+    keep, send, evidence, scaled, tiles, c0, c1, c2, c3,
+):
     step = pl.program_id(0)
     sums = (c0, c1, c2, c3)
 
     @pl.when(step == 0)
     def _():
+        pairs = [(s[0:8, :], s[8:16, :]) for s in (s0, s1, s2, s3)]
+        peak = functools.reduce(jnp.maximum, [p for p, _ in pairs])
+        mass = sum(m * jnp.exp(p - peak) for p, m in pairs)
+        evidence[...] = peak + jnp.log(mass)
+        factor = jnp.exp(pairs[0][0] - peak) / mass * scale[...]
         for j in range(IMAGES // LANES):
             part = slice(j * LANES, (j + 1) * LANES)
             column = jnp.sum(
@@ -187,24 +199,33 @@
                     jnp.concatenate([w, w], axis=0),
                     preferred_element_type=F32,
                 )
-            out[r : r + 256, :] = total
-
-
-def bricks_of(cells, factor, expo, images, weights):
+            if r < 512:
+                keep[r : r + 256, :] = total
+            else:
+                send[r - 512 : r - 256, :] = total
+
+
+def bricks_of(cells, scale, stats, expo, images, weights):
     positions, width, voxels = weights.shape
     wide = 2 * LANES
+    half = pl.BlockSpec((512, voxels), lambda i: (0, 0))
     return pl.pallas_call(
         bricks_kernel,
         grid=(VALUES // wide,),
         in_specs=[
             pl.BlockSpec(memory_space=pltpu.SMEM),
             pl.BlockSpec((8, LANES), lambda i: (0, 0)),
+            *[pl.BlockSpec((16, LANES), lambda i: (0, 0))] * 4,
             pl.BlockSpec((IMAGES, REFS), lambda i: (0, 0)),
             pl.BlockSpec((IMAGES, wide), lambda i: (0, i)),
             pl.BlockSpec((positions, width, voxels), lambda i: (0, 0, 0)),
         ],
-        out_specs=pl.BlockSpec((CELLS // positions, voxels), lambda i: (0, 0)),
-        out_shape=jax.ShapeDtypeStruct((CELLS // positions, voxels), F32),
+        out_specs=[half, half, pl.BlockSpec((8, LANES), lambda i: (0, 0))],
+        out_shape=[
+            jax.ShapeDtypeStruct((512, voxels), F32),
+            jax.ShapeDtypeStruct((512, voxels), F32),
+            jax.ShapeDtypeStruct((8, LANES), F32),
+        ],
         scratch_shapes=[
             pltpu.VMEM((REFS, IMAGES), BF16),
             pltpu.VMEM((2 * REFS, LANES), F32),
@@ -212,18 +233,12 @@
         + [pltpu.VMEM((CELLS, LANES), F32)] * 4,
         compiler_params=pltpu.CompilerParams(vmem_limit_bytes=VMEM),
         name="bricks",
-    )(cells, factor, expo, images, weights)
-
-
-def merged(pairs):
-    peak = functools.reduce(jnp.maximum, [p for p, _ in pairs])
-    return peak, sum(m * jnp.exp(p - peak) for p, m in pairs)
-
-
-def brick_share(terms, me_free=None):
-    voxels = terms.shape[1]
-    x = terms.reshape(2, -1, voxels)
-    x = x[0] + moved(x[1], ("core",), lambda c: (c + 1,))
+    )(cells, scale, *stats, expo, images, weights)
+
+
+def brick_share(keep, send):
+    voxels = keep.shape[1]
+    x = keep + moved(send, ("core",), lambda c: (c + 1,))
     x = x.reshape(4, -1, voxels)
     got = [moved(x[d].astype(BF16), ("y",), lambda y: (y + d,)) for d in (1, 2, 3)]
     x = x[0] + sum(g.astype(F32) for g in got)
@@ -239,11 +254,13 @@
 def body(images, img_scale, references, pattern, tile_owner, tile_brick, tile_block, weights):
     cut = 32
     at = {a: lax.axis_index(a) for a in AXES}
-    parts = gathered_references(references, cut)
-
-    code = tile_owner.reshape(-1) * 16 + tile_brick.reshape(-1)
-    code = code * 8 + tile_block.reshape(-1)
-    code = lax.all_gather(code, IMG, axis=0, tiled=True).reshape(REFS, -1).T.reshape(-1)
+    owned = tile_owner.reshape(-1)
+    codes = jnp.concatenate([owned, (tile_brick * 8 + tile_block).reshape(-1)])
+    parts = gathered_references(references, codes, cut)
+
+    code = parts[0][:, :, cut].astype(I32)
+    code = code[..., : owned.size] * 128 + code[..., owned.size :]
+    code = code.swapaxes(0, 1).reshape(REFS, -1).T.reshape(-1)
     block, row = code % 8, code // 8 % 4
     core, xh = code // 32 % 2, code // 64 % 2
     z, xl, y = code // 128 % 8, code // 1024 % 2, code // 2048
@@ -253,16 +270,13 @@
     cells = block * (CELLS // 8) + away * 4 + row
 
     me = jnp.stack([at["y"], at["xl"]]).astype(I32)
-    expo, peak, mass = scores_of(me, images, img_scale[:, None], pattern, parts, cut)
-    mine = jnp.concatenate([peak, mass])
+    expo, stats = scores_of(me, images, img_scale[:, None], pattern, parts, cut)
     others = [
-        moved(mine, ORI, lambda h, c: (h + dh, c + dc)) for dh, dc in ((0, 1), (1, 0), (1, 1))
+        moved(stats, ORI, lambda h, c: (h + dh, c + dc)) for dh, dc in ((0, 1), (1, 0), (1, 1))
     ]
-    all_peak, all_mass = merged([(s[:8], s[8:]) for s in (mine, *others)])
-    factor = jnp.exp(peak - all_peak) / all_mass * img_scale.reshape(8, LANES)
-    terms = bricks_of(cells, factor, expo, images, weights)
-    log_evidence = (all_peak + jnp.log(all_mass)).reshape(-1)
-    return brick_share(terms), log_evidence
+    scale = img_scale.reshape(8, LANES)
+    keep, send, evidence = bricks_of(cells, scale, (stats, *others), expo, images, weights)
+    return brick_share(keep, send), evidence.reshape(-1)
 
 
 def solution(mesh):

time: 310 us -> 179 us (0.58)
  blocking collectives: 167 us -> 31.5 us
  waiting for transfers between devices: 33.9 us -> 52.4 us
  starting transfers between devices: 31.4 us -> 19.1 us
  local copies, waits for them, and re-layouts: 7.84 us -> 4.67 us
    all_gather x1 -> x0, blocking collectives: 137 us -> none  [body(): lax.all_gather(code, IMG, axis=0, tiled=True).reshape(REFS, -1)]
    ppermute x17, waiting for transfers between devices: 33.8 us -> 52.4 us  [moved(): return lax.ppermute(x, axes, pairs)]
    ppermute x17, starting transfers between devices: 31.3 us -> 19.1 us  [moved(): return lax.ppermute(x, axes, pairs)]
  transfers between devices with their start and end apart: 18 -> 18, of which waited for: 12 -> 13; matrix products, arithmetic and copies ran while one was open for 2% -> 3% of each run, Pallas kernels for 0% -> 0%
where the time goes in v2:
time: 179 us; the launch traced here: 178 us
  waiting for transfers between devices  52.4 us (29%)
  Pallas kernels  49.8 us (28%)
  blocking collectives  31.5 us (18%)
  starting transfers between devices  19.1 us (11%)
  between operations  14.2 us (8%)
  other arithmetic  6.45 us (4%)
  local copies, waits for them, and re-layouts  4.67 us (3%)
    ppermute x17, waiting for transfers between devices, moved(): return lax.ppermute(x, axes, pairs)  52.4 us
    pallas_call x1, Pallas kernels, bricks_of(): pl.pallas_call(bricks_kernel, grid=(VALUES // wide,), in_specs=[pl.BlockS...  38.7 us
    all_to_all x2, blocking collectives, spread(): return lax.all_to_all(jnp.broadcast_to(x[None], (n, *x.shape)), axes, 0, 0)  31.5 us
    ppermute x17, starting transfers between devices, moved(): return lax.ppermute(x, axes, pairs)  19.1 us
    pallas_call x1, Pallas kernels, scores_of(): pl.pallas_call(functools.partial(scores_kernel, cut), grid=(IMAGES // row...  11.1 us
  transfers between devices with their start and end apart: 18, of which 13 were waited for; matrix products, arithmetic and copies ran while one was open for 3% of the time, Pallas kernels for 0%

profile of v2, /device:TPU:2, one launch (start us, length us, event | category | flops | bytes accessed | tf_op | source)
XLA Modules:
  0.0 178.2 jit_solution(17247272719583552819)
XLA Ops:
  7.2 0.8 fusion.44
  8.0 0.7 convert_bitcast_fusion
  8.7 0.7 add_convert_fusion
  9.5 12.6 %all_to_all.10 = bf16[8,40,512]{2,1,0:T(8,128)(2,1)} all-to-all(bf16[8,40,512]{2,1,0:T(8,128)(2,1)S(1)} %broadcast_in_dim.6), channel_id=1, replica_groups=mesh['y'=4,'xl'=2,'z'=8,'xh'=2,'core'=2] {'y','xl'}, dimensions={0} | all-to-all | bytes 655360 | tf_op jit(solution)/shard_map/all_to_all | solution.py:47
  22.1 18.8 %all_to_all.11 = bf16[8,32,512]{2,1,0:T(8,128)(2,1)S(1)} all-to-all(bf16[8,32,512]{2,1,0:T(8,128)(2,1)S(1)} %broadcast_in_dim.8), channel_id=1, replica_groups=mesh['y'=4,'xl'=2,'z'=8,'xh'=2,'core'=2] {'z'}, dimensions={0} | all-to-all | bytes 524288 | tf_op jit(solution)/shard_map/all_to_all | solution.py:47
  41.0 1.3 collective-permute-start
  42.3 5.1 %collective-permute-done = bf16[8,32,512]{2,1,0:T(8,128)(2,1)S(1)} collective-permute-done((bf16[8,32,512]{2,1,0:T(8,128)(2,1)S(1)}, bf16[8,32,512]{2,1,0:T(8,128)(2,1)S(1)}, u32[]{:S(2)}, u32[]{:S(2)}) %collective-permute-start) | collective-permute-done | bytes 262176 | tf_op jit(solution)/shard_map/ppermute | solution.py:34
  47.4 0.7 collective-permute-start.1
  48.1 2.2 %collective-permute-start.2 = (bf16[2,8,32,512]{3,2,1,0:T(8,128)(2,1)S(1)}, bf16[2,8,32,512]{3,2,1,0:T(8,128)(2,1)S(1)}, u32[]{:S(2)}, u32[]{:S(2)}) collective-permute-start(bf16[2,8,32,512]{3,2,1,0:T(8,128)(2,1)S(1)} %pad_maximum_fusion.y0), channel_id=1, source_target_pairs={{0,128},{64,192},{128,0},{192,64},{1,129},{65,193},{129,1},{193,65... | collective-permute-start | bytes 1572872 | tf_op jit(solution)/shard_map/ppermute | solution.py:34
  50.3 1.1 collective-permute-start.3
  51.4 1.0 copy.17.scale
  52.4 1.0 copy.18.pattern
  53.4 0.7 pad_add_fusion.me
  54.1 16.0 %collective-permute-done.1.y1 = bf16[2,8,32,512]{3,2,1,0:T(8,128)(2,1)S(1)} collective-permute-done((bf16[2,8,32,512]{3,2,1,0:T(8,128)(2,1)S(1)}, bf16[2,8,32,512]{3,2,1,0:T(8,128)(2,1)S(1)}, u32[]{:S(2)}, u32[]{:S(2)}) %collective-permute-start.1) | collective-permute-done | bytes 524320 | tf_op jit(solution)/shard_map/ppermute | solution.py:34
  70.1 0.6 collective-permute-done.3.y3
  70.7 0.2 copy-done.1
  70.9 0.1 copy-done.2
  71.0 0.5 copy-done.3
  71.6 11.1 %scores.1 = (f32[1024,512]{1,0:T(8,128)}, f32[16,128]{1,0:T(8,128)}) custom-call(s32[2]{0:T(128)} %pad_add_fusion.me, bf16[1024,4096]{1,0:T(8,128)(2,1)} %images.3, f32[1024,1]{1,0:T(8,128)} %copy.17.scale, s32[1024,2]{1,0:T(8,128)} %copy.18.pattern, bf16[8,8,40,512]{3,2,1,0:T(8,128)(2,1)} %bitcast.21, bf16[2,8,32,512]{3,2,1,0:T(8,128)(2,1)} %copy-done, ...), custom_call_target="tpu_custom_call" | custom-call | tf_op jit(solution)/shard_map/scores/pallas_call | solution.py:115
  82.6 0.1 collective-permute-start.4
  82.7 2.2 %collective-permute-start.5 = (f32[16,128]{1,0:T(8,128)}, f32[16,128]{1,0:T(8,128)S(1)}, u32[]{:S(2)}, u32[]{:S(2)}) collective-permute-start(f32[16,128]{1,0:T(8,128)} %get-tuple-element.7.s0), channel_id=1, source_target_pairs={{0,2},{1,3},{2,0},{3,1},{4,6},{5,7},{6,4},{7,5},{8,10},{9,11},{10,... | collective-permute-start | bytes 24584 | tf_op jit(solution)/shard_map/ppermute | solution.py:34
  85.0 1.2 collective-permute-start.6
  86.1 1.1 slice_convert_fusion
  87.3 0.1 reshape.72
  87.4 0.1 copy.16
  87.6 1.0 fusion.2.cells
  88.6 1.1 collective-permute-done.6.s3
  89.8 0.6 copy-done.8
  90.3 38.7 %bricks.1 = (f32[512,512]{1,0:T(8,128)}, f32[512,512]{1,0:T(8,128)}, f32[8,128]{1,0:T(8,128)}) custom-call(s32[16384]{0:T(1024)} %fusion.2.cells, f32[8,128]{1,0:T(8,128)} %bitcast.30, f32[16,128]{1,0:T(8,128)} %get-tuple-element.7.s0, f32[16,128]{1,0:T(8,128)} %copy-done.6, f32[16,128]{1,0:T(8,128)} %copy-done.7, f32[16,128]{1,0:T(8,128)} %copy-done.8, ...), custom_call_target="tpu_custom_call" | custom-call | tf_op jit(solution)/shard_map/bricks/pallas_call | solution.py:212
  129.1 0.1 collective-permute-start.7
  129.2 2.7 %collective-permute-done.7 = f32[512,512]{1,0:T(8,128)S(1)} collective-permute-done((f32[512,512]{1,0:T(8,128)}, f32[512,512]{1,0:T(8,128)S(1)}, u32[]{:S(2)}, u32[]{:S(2)}) %collective-permute-start.7) | collective-permute-done | bytes 1048608 | tf_op jit(solution)/shard_map/ppermute | solution.py:34
  131.9 1.5 fusion.40
  133.5 2.6 %collective-permute-start.10 = (bf16[128,512]{1,0:T(8,128)(2,1)S(1)}, bf16[128,512]{1,0:T(8,128)(2,1)S(1)}, u32[]{:S(2)}, u32[]{:S(2)}) collective-permute-start(bf16[128,512]{1,0:T(8,128)(2,1)S(1)} %get-tuple-element.15), channel_id=1, source_target_pairs={{0,192},{64,0},{128,64},{192,128},{1,193},{65,1},{129,65},{193,129... | collective-permute-start | bytes 393224 | tf_op jit(solution)/shard_map/ppermute | solution.py:34
  136.0 1.7 collective-permute-start.9
  137.8 1.3 collective-permute-done.10
  139.1 6.2 %collective-permute-done.8 = bf16[128,512]{1,0:T(8,128)(2,1)S(1)} collective-permute-done((bf16[128,512]{1,0:T(8,128)(2,1)S(1)}, bf16[128,512]{1,0:T(8,128)(2,1)S(1)}, u32[]{:S(2)}, u32[]{:S(2)}) %collective-permute-start.8) | collective-permute-done | bytes 131104 | tf_op jit(solution)/shard_map/ppermute | solution.py:34
  145.4 1.3 collective-permute-start.11
  146.7 2.9 %collective-permute-start.12 = (f32[32,512]{1,0:T(8,128)S(1)}, f32[32,512]{1,0:T(8,128)S(1)}, u32[]{:S(2)}, u32[]{:S(2)}) collective-permute-start(f32[32,512]{1,0:T(8,128)S(1)} %get-tuple-element.17), channel_id=1, source_target_pairs={{0,2},{2,0},{32,34},{34,32},{1,3},{3,1},{33,35},{35,33},{4,6},{6,4... | collective-permute-start | bytes 196616 | tf_op jit(solution)/shard_map/ppermute | solution.py:34
  149.7 0.7 collective-permute-done.11
  150.4 2.1 %collective-permute-done.12 = f32[32,512]{1,0:T(8,128)S(1)} collective-permute-done((f32[32,512]{1,0:T(8,128)S(1)}, f32[32,512]{1,0:T(8,128)S(1)}, u32[]{:S(2)}, u32[]{:S(2)}) %collective-permute-start.12) | collective-permute-done | bytes 65568 | tf_op jit(solution)/shard_map/ppermute | solution.py:34
  152.5 1.4 collective-permute-done.13
  154.0 1.1 collective-permute-start.14
  155.1 7.1 %collective-permute-done.14 = f32[4,4,512]{2,1,0:T(4,128)S(1)} collective-permute-done((f32[4,4,512]{2,1,0:T(4,128)S(1)}, f32[4,4,512]{2,1,0:T(4,128)S(1)}, u32[]{:S(2)}, u32[]{:S(2)}) %collective-permute-start.14) | collective-permute-done | bytes 32800 | tf_op jit(solution)/shard_map/ppermute | solution.py:34
  162.2 0.1 collective-permute-start.15
  162.3 4.7 %collective-permute-done.15 = f32[2,4,512]{2,1,0:T(4,128)S(1)} collective-permute-done((f32[2,4,512]{2,1,0:T(4,128)S(1)}, f32[2,4,512]{2,1,0:T(4,128)S(1)}, u32[]{:S(2)}, u32[]{:S(2)}) %collective-permute-start.15) | collective-permute-done | bytes 16416 | tf_op jit(solution)/shard_map/ppermute | solution.py:34
  167.0 0.5 collective-permute-start.16
  167.5 3.3 %collective-permute-done.16 = f32[1,4,512]{2,1,0:T(4,128)S(1)} collective-permute-done((f32[1,4,512]{2,1,0:T(4,128)S(1)}, f32[1,4,512]{2,1,0:T(4,128)S(1)}, u32[]{:S(2)}, u32[]{:S(2)}) %collective-permute-start.16) | collective-permute-done | bytes 8224 | tf_op jit(solution)/shard_map/ppermute | solution.py:34
  170.7 0.6 fusion.39
  (43 shorter events, 0.5 us)
Async XLA Ops:
  7.2 44.2 %copy-start.4 = (f32[1024]{0:T(1024)S(1)}, f32[1024]{0:T(1024)}, u32[]{:S(2)}) copy-start(f32[1024]{0:T(1024)} %param.9) | copy-start | bytes 12292
  7.2 45.2 %copy-start.5 = (s32[1024,2]{0,1:T(2,128)S(1)}, s32[1024,2]{0,1:T(2,128)}, u32[]{:S(2)}) copy-start(s32[1024,2]{0,1:T(2,128)} %param.11) | copy-start | bytes 24580
  7.2 63.5 %all-gather.3.cloned.1.call-start = ((), (), s32[]{:S(2)}) async-start(), calls=%async_computation.2 | async-start | bytes 2949120 | tf_op jit(solution)/shard_map/all_gather | solution.py:54
  41.0 6.4 %collective-permute-start = (bf16[8,32,512]{2,1,0:T(8,128)(2,1)S(1)}, bf16[8,32,512]{2,1,0:T(8,128)(2,1)S(1)}, u32[]{:S(2)}, u32[]{:S(2)}) collective-permute-start(bf16[8,32,512]{2,1,0:T(8,128)(2,1)S(1)} %all_to_all.11), channel_id=1, source_target_pairs={{0,32},{32,0},{1,33},{33,1},{2,34},{34,2},{3,35},{35,3},{4,36},{36... | collective-permute-start | bytes 786440 | tf_op jit(solution)/shard_map/ppermute | solution.py:34
  47.4 23.3 %copy-start = (bf16[2,8,32,512]{3,2,1,0:T(8,128)(2,1)}, bf16[2,8,32,512]{3,2,1,0:T(8,128)(2,1)S(1)}, u32[]{:S(2)}) copy-start(bf16[2,8,32,512]{3,2,1,0:T(8,128)(2,1)S(1)} %pad_maximum_fusion.y0) | copy-start | bytes 1572868
  47.4 22.7 %collective-permute-start.1 = (bf16[2,8,32,512]{3,2,1,0:T(8,128)(2,1)S(1)}, bf16[2,8,32,512]{3,2,1,0:T(8,128)(2,1)S(1)}, u32[]{:S(2)}, u32[]{:S(2)}) collective-permute-start(bf16[2,8,32,512]{3,2,1,0:T(8,128)(2,1)S(1)} %pad_maximum_fusion.y0), channel_id=1, source_target_pairs={{0,64},{64,128},{128,192},{192,0},{1,65},{65,129},{129,193},{193,1... | collective-permute-start | bytes 1572872 | tf_op jit(solution)/shard_map/ppermute | solution.py:34
  48.1 22.0 %collective-permute-start.2 = (bf16[2,8,32,512]{3,2,1,0:T(8,128)(2,1)S(1)}, bf16[2,8,32,512]{3,2,1,0:T(8,128)(2,1)S(1)}, u32[]{:S(2)}, u32[]{:S(2)}) collective-permute-start(bf16[2,8,32,512]{3,2,1,0:T(8,128)(2,1)S(1)} %pad_maximum_fusion.y0), channel_id=1, source_target_pairs={{0,128},{64,192},{128,0},{192,64},{1,129},{65,193},{129,1},{193,65... | collective-permute-start | bytes 1572872 | tf_op jit(solution)/shard_map/ppermute | solution.py:34
  50.3 20.4 %collective-permute-start.3 = (bf16[2,8,32,512]{3,2,1,0:T(8,128)(2,1)S(1)}, bf16[2,8,32,512]{3,2,1,0:T(8,128)(2,1)S(1)}, u32[]{:S(2)}, u32[]{:S(2)}) collective-permute-start(bf16[2,8,32,512]{3,2,1,0:T(8,128)(2,1)S(1)} %pad_maximum_fusion.y0), channel_id=1, source_target_pairs={{0,192},{64,0},{128,64},{192,128},{1,193},{65,1},{129,65},{193,129... | collective-permute-start | bytes 1572872 | tf_op jit(solution)/shard_map/ppermute | solution.py:34
  70.1 0.8 copy-start.1
  70.1 1.0 copy-start.2
  70.7 0.8 copy-start.3
  82.6 6.0 %collective-permute-start.4 = (f32[16,128]{1,0:T(8,128)}, f32[16,128]{1,0:T(8,128)S(1)}, u32[]{:S(2)}, u32[]{:S(2)}) collective-permute-start(f32[16,128]{1,0:T(8,128)} %get-tuple-element.7.s0), channel_id=1, source_target_pairs={{0,1},{1,0},{2,3},{3,2},{4,5},{5,4},{6,7},{7,6},{8,9},{9,8},{10,11... | collective-permute-start | bytes 24584 | tf_op jit(solution)/shard_map/ppermute | solution.py:34
  82.7 5.9 %collective-permute-start.5 = (f32[16,128]{1,0:T(8,128)}, f32[16,128]{1,0:T(8,128)S(1)}, u32[]{:S(2)}, u32[]{:S(2)}) collective-permute-start(f32[16,128]{1,0:T(8,128)} %get-tuple-element.7.s0), channel_id=1, source_target_pairs={{0,2},{1,3},{2,0},{3,1},{4,6},{5,7},{6,4},{7,5},{8,10},{9,11},{10,... | collective-permute-start | bytes 24584 | tf_op jit(solution)/shard_map/ppermute | solution.py:34
  85.0 4.8 %collective-permute-start.6 = (f32[16,128]{1,0:T(8,128)}, f32[16,128]{1,0:T(8,128)S(1)}, u32[]{:S(2)}, u32[]{:S(2)}) collective-permute-start(f32[16,128]{1,0:T(8,128)} %get-tuple-element.7.s0), channel_id=1, source_target_pairs={{0,3},{1,2},{2,1},{3,0},{4,7},{5,6},{6,5},{7,4},{8,11},{9,10},{10,... | collective-permute-start | bytes 24584 | tf_op jit(solution)/shard_map/ppermute | solution.py:34
  88.6 1.2 copy-start.6
  88.6 1.1 copy-start.7
  89.7 0.6 copy-start.8
  129.1 2.9 %collective-permute-start.7 = (f32[512,512]{1,0:T(8,128)}, f32[512,512]{1,0:T(8,128)S(1)}, u32[]{:S(2)}, u32[]{:S(2)}) collective-permute-start(f32[512,512]{1,0:T(8,128)} %get-tuple-element.10), channel_id=1, source_target_pairs={{0,1},{1,0},{2,3},{3,2},{4,5},{5,4},{6,7},{7,6},{8,9},{9,8},{10,11... | collective-permute-start | bytes 3145736 | tf_op jit(solution)/shard_map/ppermute | solution.py:34
  133.5 5.7 %collective-permute-start.10 = (bf16[128,512]{1,0:T(8,128)(2,1)S(1)}, bf16[128,512]{1,0:T(8,128)(2,1)S(1)}, u32[]{:S(2)}, u32[]{:S(2)}) collective-permute-start(bf16[128,512]{1,0:T(8,128)(2,1)S(1)} %get-tuple-element.15), channel_id=1, source_target_pairs={{0,192},{64,0},{128,64},{192,128},{1,193},{65,1},{129,65},{193,129... | collective-permute-start | bytes 393224 | tf_op jit(solution)/shard_map/ppermute | solution.py:34
  136.0 9.3 %collective-permute-start.8 = (bf16[128,512]{1,0:T(8,128)(2,1)S(1)}, bf16[128,512]{1,0:T(8,128)(2,1)S(1)}, u32[]{:S(2)}, u32[]{:S(2)}) collective-permute-start(bf16[128,512]{1,0:T(8,128)(2,1)S(1)} %get-tuple-element.14), channel_id=1, source_target_pairs={{0,64},{64,128},{128,192},{192,0},{1,65},{65,129},{129,193},{193,1... | collective-permute-start | bytes 393224 | tf_op jit(solution)/shard_map/ppermute | solution.py:34
  136.0 9.3 %collective-permute-start.9 = (bf16[128,512]{1,0:T(8,128)(2,1)S(1)}, bf16[128,512]{1,0:T(8,128)(2,1)S(1)}, u32[]{:S(2)}, u32[]{:S(2)}) collective-permute-start(bf16[128,512]{1,0:T(8,128)(2,1)S(1)} %get-tuple-element.16), channel_id=1, source_target_pairs={{0,128},{64,192},{128,0},{192,64},{1,129},{65,193},{129,1},{193,65... | collective-permute-start | bytes 393224 | tf_op jit(solution)/shard_map/ppermute | solution.py:34
  145.4 5.0 %collective-permute-start.11 = (f32[32,512]{1,0:T(8,128)S(1)}, f32[32,512]{1,0:T(8,128)S(1)}, u32[]{:S(2)}, u32[]{:S(2)}) collective-permute-start(f32[32,512]{1,0:T(8,128)S(1)} %get-tuple-element.19), channel_id=1, source_target_pairs={{0,32},{2,34},{32,2},{34,0},{1,33},{3,35},{33,3},{35,1},{4,36},{6,... | collective-permute-start | bytes 196616 | tf_op jit(solution)/shard_map/ppermute | solution.py:34
  146.7 5.8 %collective-permute-start.12 = (f32[32,512]{1,0:T(8,128)S(1)}, f32[32,512]{1,0:T(8,128)S(1)}, u32[]{:S(2)}, u32[]{:S(2)}) collective-permute-start(f32[32,512]{1,0:T(8,128)S(1)} %get-tuple-element.17), channel_id=1, source_target_pairs={{0,2},{2,0},{32,34},{34,32},{1,3},{3,1},{33,35},{35,33},{4,6},{6,4... | collective-permute-start | bytes 196616 | tf_op jit(solution)/shard_map/ppermute | solution.py:34
  149.7 4.3 %collective-permute-start.13 = (f32[32,512]{1,0:T(8,128)S(1)}, f32[32,512]{1,0:T(8,128)S(1)}, u32[]{:S(2)}, u32[]{:S(2)}) collective-permute-start(f32[32,512]{1,0:T(8,128)S(1)} %get-tuple-element.18), channel_id=1, source_target_pairs={{0,34},{2,32},{32,0},{34,2},{1,35},{3,33},{33,1},{35,3},{4,38},{6,... | collective-permute-start | bytes 196616 | tf_op jit(solution)/shard_map/ppermute | solution.py:34
  154.0 8.2 %collective-permute-start.14 = (f32[4,4,512]{2,1,0:T(4,128)S(1)}, f32[4,4,512]{2,1,0:T(4,128)S(1)}, u32[]{:S(2)}, u32[]{:S(2)}) collective-permute-start(f32[4,4,512]{2,1,0:T(4,128)S(1)} %slice.90), channel_id=1, source_target_pairs={{0,16},{4,20},{8,24},{12,28},{16,0},{20,4},{24,8},{28,12},{1,17},{... | collective-permute-start | bytes 98312 | tf_op jit(solution)/shard_map/ppermute | solution.py:34
  162.2 4.8 %collective-permute-start.15 = (f32[2,4,512]{2,1,0:T(4,128)S(1)}, f32[2,4,512]{2,1,0:T(4,128)S(1)}, u32[]{:S(2)}, u32[]{:S(2)}) collective-permute-start(f32[2,4,512]{2,1,0:T(4,128)S(1)} %slice.111), channel_id=1, source_target_pairs={{0,8},{4,12},{8,0},{12,4},{16,24},{20,28},{24,16},{28,20},{1,9},{5... | collective-permute-start | bytes 49160 | tf_op jit(solution)/shard_map/ppermute | solution.py:34
  167.0 3.7 %collective-permute-start.16 = (f32[1,4,512]{2,1,0:T(4,128)S(1)}, f32[1,4,512]{2,1,0:T(4,128)S(1)}, u32[]{:S(2)}, u32[]{:S(2)}) collective-permute-start(f32[1,4,512]{2,1,0:T(4,128)S(1)} %slice.113), channel_id=1, source_target_pairs={{0,4},{4,0},{8,12},{12,8},{16,20},{20,16},{24,28},{28,24},{1,5},{5... | collective-permute-start | bytes 24584 | tf_op jit(solution)/shard_map/ppermute | solution.py:34
Sparse Core Ops, SparseCore 0:
  22.2 44.1 all-gather.2

commit v3 on v2

--- a/solution.py
+++ b/solution.py
@@ -34,14 +34,6 @@
     return lax.ppermute(x, axes, pairs)
 
 
-def along_x(x, step):
-    def target(xl, xh):
-        at = (xh * 2 + xl + step) % 4
-        return at % 2, at // 2
-
-    return moved(x, ("xl", "xh"), target)
-
-
 def spread(x, axes):
     n = math.prod(AXES[a] for a in axes)
     return lax.all_to_all(jnp.broadcast_to(x[None], (n, *x.shape)), axes, 0, 0)
@@ -54,8 +46,10 @@
     ended_z = lax.all_gather(near, "z", axis=0)
     own = spread(share[cut:], ("z",))
     other = moved(own, ("xl",), lambda xl: (xl + 1,))
-    pair = jnp.stack([own, other])
-    ended_y = [pair] + [moved(pair, ("y",), lambda y: (y + d,)) for d in (1, 2, 3)]
+    ended_y = []
+    for part in (own, other):
+        ended_y.append(part)
+        ended_y += [moved(part, ("y",), lambda y: (y + d,)) for d in (1, 2, 3)]
     return [ended_z, *ended_y]
 
 
@@ -66,7 +60,7 @@
 
 
 def scores_kernel(
-    cut, me, images, scale, pattern, by_z, y0, y1, y2, y3, expo, stats, refs, sems
+    cut, me, images, scale, pattern, by_z, a0, a1, a2, a3, b0, b1, b2, b3, expo, stats, refs, sems
 ):
     step = pl.program_id(0)
     rows = images.shape[0]
@@ -74,11 +68,9 @@
     @pl.when(step == 0)
     def _():
         copies = [(by_z.at[z, :, pl.ds(0, cut)], refs.at[:, z, pl.ds(0, cut)]) for z in range(8)]
-        for d, part in enumerate((y0, y1, y2, y3)):
-            y = (me[0] + 4 - d) % 4
-            for r in range(2):
-                xl = (me[1] + r) % 2
-                copies.append((part.at[r], refs.at[y * 2 + xl, :, pl.ds(cut, SHARE - cut)]))
+        for i, part in enumerate((a0, a1, a2, a3, b0, b1, b2, b3)):
+            y, xl = (me[0] + 4 - i % 4) % 4, (me[1] + i // 4) % 2
+            copies.append((part, refs.at[y * 2 + xl, :, pl.ds(cut, SHARE - cut)]))
         copies = [pltpu.make_async_copy(a, b, sems.at[i]) for i, (a, b) in enumerate(copies)]
         for c in copies:
             c.start()
@@ -101,7 +93,7 @@
     peak = jnp.max(masked, axis=1, keepdims=True)
     value = jnp.where(active, jnp.exp(masked - peak), 0.0)
     mass = jnp.sum(value, axis=1, keepdims=True)
-    expo[...] = value
+    expo[...] = value.T
     for j in range(rows // LANES):
         part = slice(j * LANES, (j + 1) * LANES)
         at = step * (rows // LANES) + j
@@ -123,11 +115,11 @@
         ]
         + [pl.BlockSpec(memory_space=pl.ANY)] * len(parts),
         out_specs=[
-            pl.BlockSpec((rows, REFS), lambda i: (i, 0)),
+            pl.BlockSpec((REFS, rows), lambda i: (0, i)),
             pl.BlockSpec((16, LANES), lambda i: (0, 0)),
         ],
         out_shape=[
-            jax.ShapeDtypeStruct((IMAGES, REFS), F32),
+            jax.ShapeDtypeStruct((REFS, IMAGES), F32),
             jax.ShapeDtypeStruct((16, LANES), F32),
         ],
         scratch_shapes=[
@@ -139,15 +131,16 @@
     )(me, images, scale, pattern, *parts)
 
 
-UNROLL = 32
+UNROLL = 64
+SUMS = 8
+WIDE = 1024
 
 
 def bricks_kernel(
     cells, scale, s0, s1, s2, s3, expo, images, weights,
-    keep, send, evidence, scaled, tiles, c0, c1, c2, c3,
+    keep, send, evidence, scaled, tiles, *sums,
 ):
     step = pl.program_id(0)
-    sums = (c0, c1, c2, c3)
 
     @pl.when(step == 0)
     def _():
@@ -158,10 +151,7 @@
         factor = jnp.exp(pairs[0][0] - peak) / mass * scale[...]
         for j in range(IMAGES // LANES):
             part = slice(j * LANES, (j + 1) * LANES)
-            column = jnp.sum(
-                jnp.where(eye(), factor[j : j + 1, :], 0.0), axis=1, keepdims=True
-            )
-            scaled[:, part] = (expo[part, :] * column).T.astype(BF16)
+            scaled[:, part] = (expo[:, part] * factor[j : j + 1, :]).astype(BF16)
 
         def clear(i, _):
             for c in sums:
@@ -170,19 +160,23 @@
 
         lax.fori_loop(0, CELLS // 256, clear, 0)
 
-    block = jnp.dot(scaled[...], images[...], preferred_element_type=F32)
-    tiles[0:REFS, :] = block[:, 0:LANES]
-    tiles[REFS:, :] = block[:, LANES:]
+    for n in range(0, WIDE, 256):
+        block = jnp.dot(scaled[...], images[:, n : n + 256], preferred_element_type=F32)
+        for k in range(2):
+            at = (n // LANES + k) * REFS
+            tiles[at : at + REFS, :] = block[:, k * LANES : (k + 1) * LANES]
+
+    count = tiles.shape[0]
 
     def add(i, _):
         for u in range(UNROLL):
             row = i * UNROLL + u
-            cell = pl.ds(cells[step * (2 * REFS) + row], 1)
-            c = sums[u % 4]
+            cell = pl.ds(cells[step * count + row], 1)
+            c = sums[u % SUMS]
             c[cell, :] = c[cell, :] + tiles[pl.ds(row, 1), :]
         return 0
 
-    lax.fori_loop(0, 2 * REFS // UNROLL, add, 0)
+    lax.fori_loop(0, count // UNROLL, add, 0)
 
     @pl.when(step == pl.num_programs(0) - 1)
     def _():
@@ -190,7 +184,7 @@
             total = jnp.zeros((256, weights.shape[2]), F32)
             for p in range(8):
                 part = pl.ds(p * 1024 + r, 256)
-                cell = (c0[part, :] + c1[part, :]) + (c2[part, :] + c3[part, :])
+                cell = functools.reduce(jnp.add, [c[part, :] for c in sums])
                 high = cell.astype(BF16)
                 low = (cell - high.astype(F32)).astype(BF16)
                 w = weights[p]
@@ -207,17 +201,16 @@
 
 def bricks_of(cells, scale, stats, expo, images, weights):
     positions, width, voxels = weights.shape
-    wide = 2 * LANES
     half = pl.BlockSpec((512, voxels), lambda i: (0, 0))
     return pl.pallas_call(
         bricks_kernel,
-        grid=(VALUES // wide,),
+        grid=(VALUES // WIDE,),
         in_specs=[
             pl.BlockSpec(memory_space=pltpu.SMEM),
             pl.BlockSpec((8, LANES), lambda i: (0, 0)),
             *[pl.BlockSpec((16, LANES), lambda i: (0, 0))] * 4,
-            pl.BlockSpec((IMAGES, REFS), lambda i: (0, 0)),
-            pl.BlockSpec((IMAGES, wide), lambda i: (0, i)),
+            pl.BlockSpec((REFS, IMAGES), lambda i: (0, 0)),
+            pl.BlockSpec((IMAGES, WIDE), lambda i: (0, i)),
             pl.BlockSpec((positions, width, voxels), lambda i: (0, 0, 0)),
         ],
         out_specs=[half, half, pl.BlockSpec((8, LANES), lambda i: (0, 0))],
@@ -228,9 +221,9 @@
         ],
         scratch_shapes=[
             pltpu.VMEM((REFS, IMAGES), BF16),
-            pltpu.VMEM((2 * REFS, LANES), F32),
+            pltpu.VMEM((WIDE // LANES * REFS, LANES), F32),
         ]
-        + [pltpu.VMEM((CELLS, LANES), F32)] * 4,
+        + [pltpu.VMEM((CELLS, LANES), F32)] * SUMS,
         compiler_params=pltpu.CompilerParams(vmem_limit_bytes=VMEM),
         name="bricks",
     )(cells, scale, *stats, expo, images, weights)
@@ -239,16 +232,12 @@
 def brick_share(keep, send):
     voxels = keep.shape[1]
     x = keep + moved(send, ("core",), lambda c: (c + 1,))
+    x = x.reshape(16, -1, voxels).astype(BF16)
+    x = jnp.sum(lax.all_to_all(x, ("y", "xl", "xh"), 0, 0).astype(F32), axis=0)
+    x = x.reshape(2, -1, voxels)
+    x = x[0] + moved(x[1], ("z",), lambda z: (z ^ 4,))
     x = x.reshape(4, -1, voxels)
-    got = [moved(x[d].astype(BF16), ("y",), lambda y: (y + d,)) for d in (1, 2, 3)]
-    x = x[0] + sum(g.astype(F32) for g in got)
-    x = x.reshape(4, -1, voxels)
-    got = [along_x(x[d], d) for d in (1, 2, 3)]
-    x = x[0] + sum(got)
-    x = x.reshape(8, -1, voxels)
-    for half in (4, 2, 1):
-        x = x[:half] + moved(x[half:], ("z",), lambda z: (z ^ half,))
-    return x[0]
+    return x[0] + sum([moved(x[k], ("z",), lambda z: (z ^ k,)) for k in (1, 2, 3)])
 
 
 def body(images, img_scale, references, pattern, tile_owner, tile_brick, tile_block, weights):
@@ -264,8 +253,7 @@
     block, row = code % 8, code // 8 % 4
     core, xh = code // 32 % 2, code // 64 % 2
     z, xl, y = code // 128 % 8, code // 1024 % 2, code // 2048
-    away = jnp.bitwise_xor(core, at["core"]) * 4 + (y - at["y"]) % 4
-    away = away * 4 + (xh * 2 + xl - at["xh"] * 2 - at["xl"]) % 4
+    away = ((jnp.bitwise_xor(core, at["core"]) * 4 + y) * 2 + xl) * 2 + xh
     away = away * 8 + jnp.bitwise_xor(z, at["z"])
     cells = block * (CELLS // 8) + away * 4 + row
 

time: 179 us -> 163 us (0.911)
  waiting for transfers between devices: 52.4 us -> 27 us
  blocking collectives: 31.5 us -> 46.9 us
  Pallas kernels: 49.8 us -> 44.4 us
    ppermute x17 -> x15, waiting for transfers between devices: 52.4 us -> 26.7 us  [moved(): return lax.ppermute(x, axes, pairs)]
    all_to_all x0 -> x1, blocking collectives: none -> 15.4 us  [brick_share(): x = jnp.sum(lax.all_to_all(x, ('y', 'xl', 'xh'), 0, 0).astype(F32), axis=0)]
    pallas_call x1, Pallas kernels: 38.7 us -> 32.6 us  [bricks_of(): pl.pallas_call(bricks_kernel, grid=(VALUES // WIDE,), in_specs=[pl.BlockS...]
    ppermute x17 -> x15, starting transfers between devices: 19.1 us -> 19 us  [moved(): return lax.ppermute(x, axes, pairs)]
  transfers between devices with their start and end apart: 18 -> 16, of which waited for: 13 -> 10; matrix products, arithmetic and copies ran while one was open for 3% -> 4% of each run, Pallas kernels for 0% -> 0%
where the time goes in v3:
time: 163 us
  blocking collectives  46.9 us (29%)
  Pallas kernels  44.4 us (27%)
  waiting for transfers between devices  27 us (17%)
  starting transfers between devices  19.1 us (12%)
  between operations  14.2 us (9%)
  other arithmetic  6.12 us (4%)
  local copies, waits for them, and re-layouts  4.92 us (3%)
    pallas_call x1, Pallas kernels, bricks_of(): pl.pallas_call(bricks_kernel, grid=(VALUES // WIDE,), in_specs=[pl.BlockS...  32.6 us
    all_to_all x2, blocking collectives, spread(): return lax.all_to_all(jnp.broadcast_to(x[None], (n, *x.shape)), axes, 0, 0)  31.5 us
    ppermute x15, waiting for transfers between devices, moved(): return lax.ppermute(x, axes, pairs)  26.7 us
    ppermute x15, starting transfers between devices, moved(): return lax.ppermute(x, axes, pairs)  19 us
    all_to_all x1, blocking collectives, brick_share(): x = jnp.sum(lax.all_to_all(x, ('y', 'xl', 'xh'), 0, 0).astype(F32), axis=0)  15.4 us
    pallas_call x1, Pallas kernels, scores_of(): pl.pallas_call(functools.partial(scores_kernel, cut), grid=(IMAGES // row...  11.8 us
  transfers between devices with their start and end apart: 16, of which 10 were waited for; matrix products, arithmetic and copies ran while one was open for 4% of the time, Pallas kernels for 0%

profile of v3, /device:TPU:2, one launch (start us, length us, event | category | flops | bytes accessed | tf_op | source)
XLA Modules:
  0.0 162.6 jit_solution(8442272293886175180)
XLA Ops:
  7.2 0.0 all-gather.3.cloned.1.call-start
  7.2 0.8 fusion.36
  8.0 0.7 convert_bitcast_fusion
  8.7 0.7 add_convert_fusion.1
  9.4 12.6 %all_to_all.15 = bf16[8,40,512]{2,1,0:T(8,128)(2,1)} all-to-all(bf16[8,40,512]{2,1,0:T(8,128)(2,1)S(1)} %broadcast_in_dim.6), channel_id=1, replica_groups=mesh['y'=4,'xl'=2,'z'=8,'xh'=2,'core'=2] {'y','xl'}, dimensions={0} | all-to-all | bytes 655360 | tf_op jit(solution)/shard_map/all_to_all | solution.py:39
  22.1 0.0 all-gather.3.cloned.1.call-update
  22.1 18.8 %all_to_all.16.a0 = bf16[8,32,512]{2,1,0:T(8,128)(2,1)S(1)} all-to-all(bf16[8,32,512]{2,1,0:T(8,128)(2,1)S(1)} %broadcast_in_dim.8), channel_id=1, replica_groups=mesh['y'=4,'xl'=2,'z'=8,'xh'=2,'core'=2] {'z'}, dimensions={0} | all-to-all | bytes 524288 | tf_op jit(solution)/shard_map/all_to_all | solution.py:39
  41.0 1.3 collective-permute-start.3
  42.3 0.5 collective-permute-start
  42.8 2.0 %collective-permute-start.1 = (bf16[8,32,512]{2,1,0:T(8,128)(2,1)S(1)}, bf16[8,32,512]{2,1,0:T(8,128)(2,1)S(1)}, u32[]{:S(2)}, u32[]{:S(2)}) collective-permute-start(bf16[8,32,512]{2,1,0:T(8,128)(2,1)S(1)} %all_to_all.16.a0), channel_id=1, source_target_pairs={{0,128},{64,192},{128,0},{192,64},{1,129},{65,193},{129,1},{193,65... | collective-permute-start | bytes 786440 | tf_op jit(solution)/shard_map/ppermute | solution.py:34
  44.8 1.4 collective-permute-start.2
  46.2 1.2 collective-permute-done.3.b0
  47.3 0.6 collective-permute-start.4
  47.9 2.2 %collective-permute-start.5 = (bf16[8,32,512]{2,1,0:T(8,128)(2,1)S(1)}, bf16[8,32,512]{2,1,0:T(8,128)(2,1)S(1)}, u32[]{:S(2)}, u32[]{:S(2)}) collective-permute-start(bf16[8,32,512]{2,1,0:T(8,128)(2,1)S(1)} %collective-permute-done.3.b0), channel_id=1, source_target_pairs={{0,128},{64,192},{128,0},{192,64},{1,129},{65,193},{129,1},{193,65... | collective-permute-start | bytes 786440 | tf_op jit(solution)/shard_map/ppermute | solution.py:34
  50.1 8.2 %collective-permute-done.a1 = bf16[8,32,512]{2,1,0:T(8,128)(2,1)S(1)} collective-permute-done((bf16[8,32,512]{2,1,0:T(8,128)(2,1)S(1)}, bf16[8,32,512]{2,1,0:T(8,128)(2,1)S(1)}, u32[]{:S(2)}, u32[]{:S(2)}) %collective-permute-start) | collective-permute-done | bytes 262176 | tf_op jit(solution)/shard_map/ppermute | solution.py:34
  58.4 0.0 collective-permute-start.6
  58.4 1.7 %copy.17.scale = f32[1024,1]{1,0:T(8,128)} copy(f32[1024,1]{0,1:T(1,128)} %bitcast.26) | data formatting | bytes 8192 | tf_op jit(solution)/shard_map/broadcast_in_dim | solution.py:261
  60.1 1.0 copy.18.pattern
  61.2 0.6 pad_add_fusion.me
  61.7 0.0 collective-permute-done.1.a2
  61.7 3.7 %collective-permute-done.4.b1 = bf16[8,32,512]{2,1,0:T(8,128)(2,1)S(1)} collective-permute-done((bf16[8,32,512]{2,1,0:T(8,128)(2,1)S(1)}, bf16[8,32,512]{2,1,0:T(8,128)(2,1)S(1)}, u32[]{:S(2)}, u32[]{:S(2)}) %collective-permute-start.4) | collective-permute-done | bytes 262176 | tf_op jit(solution)/shard_map/ppermute | solution.py:34
  65.4 0.7 collective-permute-done.6.b3
  66.1 0.3 all-gather.3.cloned.1.call-done
  66.5 0.4 copy-done.7
  66.8 11.8 %scores.1 = (f32[512,1024]{1,0:T(8,128)}, f32[16,128]{1,0:T(8,128)}) custom-call(s32[2]{0:T(128)} %pad_add_fusion.me, bf16[1024,4096]{1,0:T(8,128)(2,1)} %images.3, f32[1024,1]{1,0:T(8,128)} %copy.17.scale, s32[1024,2]{1,0:T(8,128)} %copy.18.pattern, bf16[8,8,40,512]{3,2,1,0:T(8,128)(2,1)} %bitcast.18, bf16[8,32,512]{2,1,0:T(8,128)(2,1)} %copy-done, ...), custom_call_target="tpu_custom_call" | custom-call | tf_op jit(solution)/shard_map/scores/pallas_call | solution.py:107
  78.7 0.1 collective-permute-start.7
  78.8 2.2 %collective-permute-start.8 = (f32[16,128]{1,0:T(8,128)}, f32[16,128]{1,0:T(8,128)S(1)}, u32[]{:S(2)}, u32[]{:S(2)}) collective-permute-start(f32[16,128]{1,0:T(8,128)} %get-tuple-element.7.s0), channel_id=1, source_target_pairs={{0,2},{1,3},{2,0},{3,1},{4,6},{5,7},{6,4},{7,5},{8,10},{9,11},{10,... | collective-permute-start | bytes 24584 | tf_op jit(solution)/shard_map/ppermute | solution.py:34
  81.0 1.2 collective-permute-start.9
  82.1 1.1 slice_convert_fusion
  83.3 0.1 reshape.67
  83.5 0.1 copy.16
  83.6 0.9 fusion.2.cells
  84.6 1.2 collective-permute-done.9.s3
  85.8 0.6 copy-done.11
  86.4 32.6 %bricks.1 = (f32[512,512]{1,0:T(8,128)}, f32[512,512]{1,0:T(8,128)}, f32[8,128]{1,0:T(8,128)}) custom-call(s32[16384]{0:T(1024)} %fusion.2.cells, f32[8,128]{1,0:T(8,128)} %bitcast.27, f32[16,128]{1,0:T(8,128)} %get-tuple-element.7.s0, f32[16,128]{1,0:T(8,128)} %copy-done.9, f32[16,128]{1,0:T(8,128)} %copy-done.10, f32[16,128]{1,0:T(8,128)} %copy-done.11, ...), custom_call_target="tpu_custom_call" | custom-call | tf_op jit(solution)/shard_map/bricks/pallas_call | solution.py:205
  119.0 0.1 collective-permute-start.10
  119.1 2.7 %collective-permute-done.10 = f32[512,512]{1,0:T(8,128)S(1)} collective-permute-done((f32[512,512]{1,0:T(8,128)}, f32[512,512]{1,0:T(8,128)S(1)}, u32[]{:S(2)}, u32[]{:S(2)}) %collective-permute-start.10) | collective-permute-done | bytes 1048608 | tf_op jit(solution)/shard_map/ppermute | solution.py:34
  121.8 1.4 add_convert_fusion
  123.2 15.4 %all_to_all.17 = bf16[16,32,512]{2,1,0:T(8,128)(2,1)S(1)} all-to-all(bf16[16,32,512]{2,1,0:T(8,128)(2,1)S(1)} %bitcast.20), channel_id=1, replica_groups=mesh['y'=4,'xl'=2,'z'=8,'xh'=2,'core'=2] {'y','xl','xh'}, dimensions={0} | all-to-all | bytes 1048576 | tf_op jit(solution)/shard_map/all_to_all | solution.py:236
  138.6 0.1 convert_reduce_fusion
  138.7 3.0 %collective-permute-start.11 = (f32[16,512]{1,0:T(8,128)S(1)}, f32[16,512]{1,0:T(8,128)S(1)}, u32[]{:S(2)}, u32[]{:S(2)}) collective-permute-start(f32[16,512]{1,0:T(8,128)S(1)} %slice.56), channel_id=1, source_target_pairs={{0,16},{4,20},{8,24},{12,28},{16,0},{20,4},{24,8},{28,12},{1,17},{... | collective-permute-start | bytes 98312 | tf_op jit(solution)/shard_map/ppermute | solution.py:34
  141.7 5.0 %collective-permute-done.11 = f32[16,512]{1,0:T(8,128)S(1)} collective-permute-done((f32[16,512]{1,0:T(8,128)S(1)}, f32[16,512]{1,0:T(8,128)S(1)}, u32[]{:S(2)}, u32[]{:S(2)}) %collective-permute-start.11) | collective-permute-done | bytes 32800 | tf_op jit(solution)/shard_map/ppermute | solution.py:34
  146.7 1.1 collective-permute-start.12
  147.8 1.8 %collective-permute-start.13 = (f32[4,512]{1,0:T(4,128)S(1)}, f32[4,512]{1,0:T(4,128)S(1)}, u32[]{:S(2)}, u32[]{:S(2)}) collective-permute-start(f32[4,512]{1,0:T(4,128)S(1)} %get-tuple-element.14), channel_id=1, source_target_pairs={{0,8},{4,12},{8,0},{12,4},{16,24},{20,28},{24,16},{28,20},{1,9},{5... | collective-permute-start | bytes 24584 | tf_op jit(solution)/shard_map/ppermute | solution.py:34
  149.7 1.5 collective-permute-start.14
  151.2 1.2 collective-permute-done.13
  152.4 2.7 %collective-permute-done.14 = f32[4,512]{1,0:T(4,128)S(1)} collective-permute-done((f32[4,512]{1,0:T(4,128)S(1)}, f32[4,512]{1,0:T(4,128)S(1)}, u32[]{:S(2)}, u32[]{:S(2)}) %collective-permute-start.14) | collective-permute-done | bytes 8224 | tf_op jit(solution)/shard_map/ppermute | solution.py:34
  155.1 0.6 slice_add_fusion.2
  (38 shorter events, 0.2 us)
Async XLA Ops:
  7.2 53.0 %copy-start.8 = (s32[1024,2]{0,1:T(2,128)S(1)}, s32[1024,2]{0,1:T(2,128)}, u32[]{:S(2)}) copy-start(s32[1024,2]{0,1:T(2,128)} %param.11) | copy-start | bytes 24580
  7.2 59.2 %all-gather.3.cloned.1.call-start = ((), (), s32[]{:S(2)}) async-start(), calls=%async_computation.3 | async-start | bytes 2949120 | tf_op jit(solution)/shard_map/all_gather | solution.py:46
  41.0 25.4 %copy-start = (bf16[8,32,512]{2,1,0:T(8,128)(2,1)}, bf16[8,32,512]{2,1,0:T(8,128)(2,1)S(1)}, u32[]{:S(2)}) copy-start(bf16[8,32,512]{2,1,0:T(8,128)(2,1)S(1)} %all_to_all.16.a0) | copy-start | bytes 786436
  41.0 6.4 %collective-permute-start.3 = (bf16[8,32,512]{2,1,0:T(8,128)(2,1)S(1)}, bf16[8,32,512]{2,1,0:T(8,128)(2,1)S(1)}, u32[]{:S(2)}, u32[]{:S(2)}) collective-permute-start(bf16[8,32,512]{2,1,0:T(8,128)(2,1)S(1)} %all_to_all.16.a0), channel_id=1, source_target_pairs={{0,32},{32,0},{1,33},{33,1},{2,34},{34,2},{3,35},{35,3},{4,36},{36... | collective-permute-start | bytes 786440 | tf_op jit(solution)/shard_map/ppermute | solution.py:34
  42.3 16.1 %collective-permute-start = (bf16[8,32,512]{2,1,0:T(8,128)(2,1)S(1)}, bf16[8,32,512]{2,1,0:T(8,128)(2,1)S(1)}, u32[]{:S(2)}, u32[]{:S(2)}) collective-permute-start(bf16[8,32,512]{2,1,0:T(8,128)(2,1)S(1)} %all_to_all.16.a0), channel_id=1, source_target_pairs={{0,64},{64,128},{128,192},{192,0},{1,65},{65,129},{129,193},{193,1... | collective-permute-start | bytes 786440 | tf_op jit(solution)/shard_map/ppermute | solution.py:34
  42.8 18.9 %collective-permute-start.1 = (bf16[8,32,512]{2,1,0:T(8,128)(2,1)S(1)}, bf16[8,32,512]{2,1,0:T(8,128)(2,1)S(1)}, u32[]{:S(2)}, u32[]{:S(2)}) collective-permute-start(bf16[8,32,512]{2,1,0:T(8,128)(2,1)S(1)} %all_to_all.16.a0), channel_id=1, source_target_pairs={{0,128},{64,192},{128,0},{192,64},{1,129},{65,193},{129,1},{193,65... | collective-permute-start | bytes 786440 | tf_op jit(solution)/shard_map/ppermute | solution.py:34
  44.8 16.9 %collective-permute-start.2 = (bf16[8,32,512]{2,1,0:T(8,128)(2,1)S(1)}, bf16[8,32,512]{2,1,0:T(8,128)(2,1)S(1)}, u32[]{:S(2)}, u32[]{:S(2)}) collective-permute-start(bf16[8,32,512]{2,1,0:T(8,128)(2,1)S(1)} %all_to_all.16.a0), channel_id=1, source_target_pairs={{0,192},{64,0},{128,64},{192,128},{1,193},{65,1},{129,65},{193,129... | collective-permute-start | bytes 786440 | tf_op jit(solution)/shard_map/ppermute | solution.py:34
  47.3 19.1 %copy-start.1 = (bf16[8,32,512]{2,1,0:T(8,128)(2,1)}, bf16[8,32,512]{2,1,0:T(8,128)(2,1)S(1)}, u32[]{:S(2)}) copy-start(bf16[8,32,512]{2,1,0:T(8,128)(2,1)S(1)} %collective-permute-done.3.b0) | copy-start | bytes 786436
  47.3 18.1 %collective-permute-start.4 = (bf16[8,32,512]{2,1,0:T(8,128)(2,1)S(1)}, bf16[8,32,512]{2,1,0:T(8,128)(2,1)S(1)}, u32[]{:S(2)}, u32[]{:S(2)}) collective-permute-start(bf16[8,32,512]{2,1,0:T(8,128)(2,1)S(1)} %collective-permute-done.3.b0), channel_id=1, source_target_pairs={{0,64},{64,128},{128,192},{192,0},{1,65},{65,129},{129,193},{193,1... | collective-permute-start | bytes 786440 | tf_op jit(solution)/shard_map/ppermute | solution.py:34
  47.9 17.5 %collective-permute-start.5 = (bf16[8,32,512]{2,1,0:T(8,128)(2,1)S(1)}, bf16[8,32,512]{2,1,0:T(8,128)(2,1)S(1)}, u32[]{:S(2)}, u32[]{:S(2)}) collective-permute-start(bf16[8,32,512]{2,1,0:T(8,128)(2,1)S(1)} %collective-permute-done.3.b0), channel_id=1, source_target_pairs={{0,128},{64,192},{128,0},{192,64},{1,129},{65,193},{129,1},{193,65... | collective-permute-start | bytes 786440 | tf_op jit(solution)/shard_map/ppermute | solution.py:34
  58.4 8.0 %copy-start.2 = (bf16[8,32,512]{2,1,0:T(8,128)(2,1)}, bf16[8,32,512]{2,1,0:T(8,128)(2,1)S(1)}, u32[]{:S(2)}) copy-start(bf16[8,32,512]{2,1,0:T(8,128)(2,1)S(1)} %collective-permute-done.a1) | copy-start | bytes 786436
  58.4 7.7 %collective-permute-start.6 = (bf16[8,32,512]{2,1,0:T(8,128)(2,1)S(1)}, bf16[8,32,512]{2,1,0:T(8,128)(2,1)S(1)}, u32[]{:S(2)}, u32[]{:S(2)}) collective-permute-start(bf16[8,32,512]{2,1,0:T(8,128)(2,1)S(1)} %collective-permute-done.3.b0), channel_id=1, source_target_pairs={{0,192},{64,0},{128,64},{192,128},{1,193},{65,1},{129,65},{193,129... | collective-permute-start | bytes 786440 | tf_op jit(solution)/shard_map/ppermute | solution.py:34
  61.7 4.7 %copy-start.3 = (bf16[8,32,512]{2,1,0:T(8,128)(2,1)}, bf16[8,32,512]{2,1,0:T(8,128)(2,1)S(1)}, u32[]{:S(2)}) copy-start(bf16[8,32,512]{2,1,0:T(8,128)(2,1)S(1)} %collective-permute-done.1.a2) | copy-start | bytes 786436
  61.7 4.7 %copy-start.4 = (bf16[8,32,512]{2,1,0:T(8,128)(2,1)}, bf16[8,32,512]{2,1,0:T(8,128)(2,1)S(1)}, u32[]{:S(2)}) copy-start(bf16[8,32,512]{2,1,0:T(8,128)(2,1)S(1)} %collective-permute-done.2.a3) | copy-start | bytes 786436
  65.4 1.0 copy-start.5
  65.4 1.0 copy-start.6
  66.1 0.7 copy-start.7
  78.7 5.9 %collective-permute-start.7 = (f32[16,128]{1,0:T(8,128)}, f32[16,128]{1,0:T(8,128)S(1)}, u32[]{:S(2)}, u32[]{:S(2)}) collective-permute-start(f32[16,128]{1,0:T(8,128)} %get-tuple-element.7.s0), channel_id=1, source_target_pairs={{0,1},{1,0},{2,3},{3,2},{4,5},{5,4},{6,7},{7,6},{8,9},{9,8},{10,11... | collective-permute-start | bytes 24584 | tf_op jit(solution)/shard_map/ppermute | solution.py:34
  78.8 5.8 %collective-permute-start.8 = (f32[16,128]{1,0:T(8,128)}, f32[16,128]{1,0:T(8,128)S(1)}, u32[]{:S(2)}, u32[]{:S(2)}) collective-permute-start(f32[16,128]{1,0:T(8,128)} %get-tuple-element.7.s0), channel_id=1, source_target_pairs={{0,2},{1,3},{2,0},{3,1},{4,6},{5,7},{6,4},{7,5},{8,10},{9,11},{10,... | collective-permute-start | bytes 24584 | tf_op jit(solution)/shard_map/ppermute | solution.py:34
  81.0 4.8 %collective-permute-start.9 = (f32[16,128]{1,0:T(8,128)}, f32[16,128]{1,0:T(8,128)S(1)}, u32[]{:S(2)}, u32[]{:S(2)}) collective-permute-start(f32[16,128]{1,0:T(8,128)} %get-tuple-element.7.s0), channel_id=1, source_target_pairs={{0,3},{1,2},{2,1},{3,0},{4,7},{5,6},{6,5},{7,4},{8,11},{9,10},{10,... | collective-permute-start | bytes 24584 | tf_op jit(solution)/shard_map/ppermute | solution.py:34
  84.6 1.2 copy-start.9
  84.6 1.2 copy-start.10
  85.8 0.6 copy-start.11
  119.0 2.9 %collective-permute-start.10 = (f32[512,512]{1,0:T(8,128)}, f32[512,512]{1,0:T(8,128)S(1)}, u32[]{:S(2)}, u32[]{:S(2)}) collective-permute-start(f32[512,512]{1,0:T(8,128)} %get-tuple-element.10), channel_id=1, source_target_pairs={{0,1},{1,0},{2,3},{3,2},{4,5},{5,4},{6,7},{7,6},{8,9},{9,8},{10,11... | collective-permute-start | bytes 3145736 | tf_op jit(solution)/shard_map/ppermute | solution.py:34
  138.7 8.0 %collective-permute-start.11 = (f32[16,512]{1,0:T(8,128)S(1)}, f32[16,512]{1,0:T(8,128)S(1)}, u32[]{:S(2)}, u32[]{:S(2)}) collective-permute-start(f32[16,512]{1,0:T(8,128)S(1)} %slice.56), channel_id=1, source_target_pairs={{0,16},{4,20},{8,24},{12,28},{16,0},{20,4},{24,8},{28,12},{1,17},{... | collective-permute-start | bytes 98312 | tf_op jit(solution)/shard_map/ppermute | solution.py:34
  146.7 4.5 %collective-permute-start.12 = (f32[4,512]{1,0:T(4,128)S(1)}, f32[4,512]{1,0:T(4,128)S(1)}, u32[]{:S(2)}, u32[]{:S(2)}) collective-permute-start(f32[4,512]{1,0:T(4,128)S(1)} %get-tuple-element.16), channel_id=1, source_target_pairs={{0,4},{4,0},{8,12},{12,8},{16,20},{20,16},{24,28},{28,24},{1,5},{5... | collective-permute-start | bytes 24584 | tf_op jit(solution)/shard_map/ppermute | solution.py:34
  147.8 4.5 %collective-permute-start.13 = (f32[4,512]{1,0:T(4,128)S(1)}, f32[4,512]{1,0:T(4,128)S(1)}, u32[]{:S(2)}, u32[]{:S(2)}) collective-permute-start(f32[4,512]{1,0:T(4,128)S(1)} %get-tuple-element.14), channel_id=1, source_target_pairs={{0,8},{4,12},{8,0},{12,4},{16,24},{20,28},{24,16},{28,20},{1,9},{5... | collective-permute-start | bytes 24584 | tf_op jit(solution)/shard_map/ppermute | solution.py:34
  149.7 5.4 %collective-permute-start.14 = (f32[4,512]{1,0:T(4,128)S(1)}, f32[4,512]{1,0:T(4,128)S(1)}, u32[]{:S(2)}, u32[]{:S(2)}) collective-permute-start(f32[4,512]{1,0:T(4,128)S(1)} %get-tuple-element.15), channel_id=1, source_target_pairs={{0,12},{4,8},{8,4},{12,0},{16,28},{20,24},{24,20},{28,16},{1,13},{... | collective-permute-start | bytes 24584 | tf_op jit(solution)/shard_map/ppermute | solution.py:34
Sparse Core Ops, SparseCore 0:
  22.2 44.1 all-gather.2

commit v4 on v3

--- a/solution.py
+++ b/solution.py
@@ -13,6 +13,7 @@
 AXES = {"y": 4, "xl": 2, "z": 8, "xh": 2, "core": 2}
 IMG, ORI = ("y", "xl", "z"), ("xh", "core")
 REFS, VALUES, IMAGES = 512, 4096, 1024
+GROUP = REFS // 2
 SHARE = 64
 CELLS = 8192
 LANES = 128
@@ -39,18 +40,19 @@
     return lax.all_to_all(jnp.broadcast_to(x[None], (n, *x.shape)), axes, 0, 0)
 
 
-def gathered_references(references, codes, cut):
+def gathered_references(references, codes):
     share = references.T
-    more = jnp.pad(codes.astype(BF16)[None], ((0, 7), (0, 0)))
-    near = spread(jnp.concatenate([share[:cut], more]), ("y", "xl"))
-    ended_z = lax.all_gather(near, "z", axis=0)
-    own = spread(share[cut:], ("z",))
+    near = spread(share[:, :GROUP], ("y", "xl"))
+    first = lax.all_gather(near, "z", axis=0)
+    more = jnp.pad(codes.astype(BF16).reshape(2, GROUP), ((0, 6), (0, 0)))
+    own = spread(jnp.concatenate([share[:, GROUP:], more]), ("z",))
+    codes = spread(own[:, SHARE : SHARE + 2].reshape(8, -1), ("y", "xl"))
+    own = own[:, :SHARE]
     other = moved(own, ("xl",), lambda xl: (xl + 1,))
-    ended_y = []
-    for part in (own, other):
-        ended_y.append(part)
-        ended_y += [moved(part, ("y",), lambda y: (y + d,)) for d in (1, 2, 3)]
-    return [ended_z, *ended_y]
+    near = [own] + [moved(own, ("y",), lambda y: (y + d,)) for d in (1, 2, 3)]
+    far = [other] + [moved(other, ("y",), lambda y: (y + d,)) for d in (1, 3)]
+    far.insert(2, moved(near[2], ("xl",), lambda xl: (xl + 1,)))
+    return [first], near + far, codes.astype(I32)
 
 
 def eye():
@@ -59,36 +61,33 @@
     )
 
 
-def scores_kernel(
-    cut, me, images, scale, pattern, by_z, a0, a1, a2, a3, b0, b1, b2, b3, expo, stats, refs, sems
-):
+def scores_kernel(group, me, images, scale, pattern, before, *rest):
+    *parts, expo, stats, refs, sems = rest
     step = pl.program_id(0)
     rows = images.shape[0]
 
     @pl.when(step == 0)
     def _():
-        copies = [(by_z.at[z, :, pl.ds(0, cut)], refs.at[:, z, pl.ds(0, cut)]) for z in range(8)]
-        for i, part in enumerate((a0, a1, a2, a3, b0, b1, b2, b3)):
-            y, xl = (me[0] + 4 - i % 4) % 4, (me[1] + i // 4) % 2
-            copies.append((part, refs.at[y * 2 + xl, :, pl.ds(cut, SHARE - cut)]))
+        if len(parts) == 1:
+            copies = [(parts[0].at[z], refs.at[:, z]) for z in range(8)]
+        else:
+            copies = []
+            for i, part in enumerate(parts):
+                y, xl = (me[0] + 4 - i % 4) % 4, (me[1] + i // 4) % 2
+                copies.append((part, refs.at[y * 2 + xl]))
         copies = [pltpu.make_async_copy(a, b, sems.at[i]) for i, (a, b) in enumerate(copies)]
         for c in copies:
             c.start()
+        if group:
+            stats[0 : 16 * group, :] = before[0 : 16 * group, :]
         for c in copies:
             c.wait()
 
-    total = jnp.zeros((rows, REFS), F32)
-    wide = 8 * SHARE
-    for q in range(8):
-        total += jnp.dot(
-            images[:, q * wide : (q + 1) * wide],
-            refs[q].reshape(wide, REFS),
-            preferred_element_type=F32,
-        )
+    total = jnp.dot(
+        images[...], refs[...].reshape(VALUES, GROUP), preferred_element_type=F32
+    )
     scores = total * scale[...] * (1.0 / math.sqrt(VALUES))
-    group = lax.broadcasted_iota(I32, (rows, REFS), 1) // (REFS // 2)
-    flags = pattern[...]
-    active = jnp.where(group == 0, flags[:, 0:1], flags[:, 1:2]) > 0
+    active = pattern[:, group : group + 1] > 0
     masked = jnp.where(active, scores, -1e30)
     peak = jnp.max(masked, axis=1, keepdims=True)
     value = jnp.where(active, jnp.exp(masked - peak), 0.0)
@@ -98,37 +97,43 @@
         part = slice(j * LANES, (j + 1) * LANES)
         at = step * (rows // LANES) + j
         for k, column in enumerate((peak, mass)):
-            stats[pl.ds(k * 8 + at, 1), :] = jnp.sum(
+            stats[pl.ds(16 * group + k * 8 + at, 1), :] = jnp.sum(
                 jnp.where(eye(), column[part], 0.0), axis=0, keepdims=True
             )
 
 
-def scores_of(me, images, scale, pattern, parts, cut, rows=256):
+def scores_of(group, me, images, scale, pattern, before, parts, rows=256):
     return pl.pallas_call(
-        functools.partial(scores_kernel, cut),
+        functools.partial(scores_kernel, group),
         grid=(IMAGES // rows,),
         in_specs=[
             pl.BlockSpec(memory_space=pltpu.SMEM),
             pl.BlockSpec((rows, VALUES), lambda i: (i, 0)),
             pl.BlockSpec((rows, 1), lambda i: (i, 0)),
             pl.BlockSpec((rows, 2), lambda i: (i, 0)),
+            pl.BlockSpec((16, LANES), lambda i: (0, 0)),
         ]
         + [pl.BlockSpec(memory_space=pl.ANY)] * len(parts),
         out_specs=[
-            pl.BlockSpec((REFS, rows), lambda i: (0, i)),
-            pl.BlockSpec((16, LANES), lambda i: (0, 0)),
+            pl.BlockSpec((GROUP, rows), lambda i: (0, i)),
+            pl.BlockSpec((16 * group + 16, LANES), lambda i: (0, 0)),
         ],
         out_shape=[
-            jax.ShapeDtypeStruct((REFS, IMAGES), F32),
-            jax.ShapeDtypeStruct((16, LANES), F32),
+            jax.ShapeDtypeStruct((GROUP, IMAGES), F32),
+            jax.ShapeDtypeStruct((16 * group + 16, LANES), F32),
         ],
         scratch_shapes=[
-            pltpu.VMEM((8, 8, SHARE, REFS), BF16),
-            pltpu.SemaphoreType.DMA((16,)),
+            pltpu.VMEM((8, 8, SHARE, GROUP), BF16),
+            pltpu.SemaphoreType.DMA((8,)),
         ],
         compiler_params=pltpu.CompilerParams(vmem_limit_bytes=VMEM),
-        name="scores",
-    )(me, images, scale, pattern, *parts)
+        cost_estimate=pl.CostEstimate(
+            flops=2 * IMAGES * VALUES * GROUP,
+            bytes_accessed=2 * IMAGES * VALUES + 2 * VALUES * GROUP + 4 * IMAGES * GROUP,
+            transcendentals=IMAGES * GROUP,
+        ),
+        name=f"scores{group}",
+    )(me, images, scale, pattern, before, *parts)
 
 
 UNROLL = 64
@@ -137,21 +142,28 @@
 
 
 def bricks_kernel(
-    cells, scale, s0, s1, s2, s3, expo, images, weights,
+    cells, scale, s0, s1, s2, s3, expo0, expo1, images, weights,
     keep, send, evidence, scaled, tiles, *sums,
 ):
     step = pl.program_id(0)
 
     @pl.when(step == 0)
     def _():
-        pairs = [(s[0:8, :], s[8:16, :]) for s in (s0, s1, s2, s3)]
+        pairs = [
+            (s[16 * g : 16 * g + 8, :], s[16 * g + 8 : 16 * g + 16, :])
+            for s in (s0, s1, s2, s3)
+            for g in range(2)
+        ]
         peak = functools.reduce(jnp.maximum, [p for p, _ in pairs])
         mass = sum(m * jnp.exp(p - peak) for p, m in pairs)
         evidence[...] = peak + jnp.log(mass)
-        factor = jnp.exp(pairs[0][0] - peak) / mass * scale[...]
+        factors = [jnp.exp(pairs[g][0] - peak) / mass * scale[...] for g in range(2)]
         for j in range(IMAGES // LANES):
             part = slice(j * LANES, (j + 1) * LANES)
-            scaled[:, part] = (expo[:, part] * factor[j : j + 1, :]).astype(BF16)
+            for g, (expo, factor) in enumerate(zip((expo0, expo1), factors)):
+                scaled[g * GROUP : (g + 1) * GROUP, part] = (
+                    expo[:, part] * factor[j : j + 1, :]
+                ).astype(BF16)
 
         def clear(i, _):
             for c in sums:
@@ -171,7 +183,7 @@
     def add(i, _):
         for u in range(UNROLL):
             row = i * UNROLL + u
-            cell = pl.ds(cells[step * count + row], 1)
+            cell = pl.ds(cells[row], 1)
             c = sums[u % SUMS]
             c[cell, :] = c[cell, :] + tiles[pl.ds(row, 1), :]
         return 0
@@ -199,17 +211,19 @@
                 send[r - 512 : r - 256, :] = total
 
 
-def bricks_of(cells, scale, stats, expo, images, weights):
+def bricks_of(cells, scale, stats, expos, images, weights):
     positions, width, voxels = weights.shape
     half = pl.BlockSpec((512, voxels), lambda i: (0, 0))
     return pl.pallas_call(
         bricks_kernel,
         grid=(VALUES // WIDE,),
         in_specs=[
-            pl.BlockSpec(memory_space=pltpu.SMEM),
+            pl.BlockSpec(
+                (WIDE // LANES * REFS,), lambda i: (i,), memory_space=pltpu.SMEM
+            ),
             pl.BlockSpec((8, LANES), lambda i: (0, 0)),
-            *[pl.BlockSpec((16, LANES), lambda i: (0, 0))] * 4,
-            pl.BlockSpec((REFS, IMAGES), lambda i: (0, 0)),
+            *[pl.BlockSpec((32, LANES), lambda i: (0, 0))] * 4,
+            *[pl.BlockSpec((GROUP, IMAGES), lambda i: (0, 0))] * 2,
             pl.BlockSpec((IMAGES, WIDE), lambda i: (0, i)),
             pl.BlockSpec((positions, width, voxels), lambda i: (0, 0, 0)),
         ],
@@ -226,7 +240,7 @@
         + [pltpu.VMEM((CELLS, LANES), F32)] * SUMS,
         compiler_params=pltpu.CompilerParams(vmem_limit_bytes=VMEM),
         name="bricks",
-    )(cells, scale, *stats, expo, images, weights)
+    )(cells, scale, *stats, *expos, images, weights)
 
 
 def brick_share(keep, send):
@@ -241,15 +255,13 @@
 
 
 def body(images, img_scale, references, pattern, tile_owner, tile_brick, tile_block, weights):
-    cut = 32
     at = {a: lax.axis_index(a) for a in AXES}
     owned = tile_owner.reshape(-1)
     codes = jnp.concatenate([owned, (tile_brick * 8 + tile_block).reshape(-1)])
-    parts = gathered_references(references, codes, cut)
-
-    code = parts[0][:, :, cut].astype(I32)
+    first, second, code = gathered_references(references, codes)
+
     code = code[..., : owned.size] * 128 + code[..., owned.size :]
-    code = code.swapaxes(0, 1).reshape(REFS, -1).T.reshape(-1)
+    code = code.reshape(REFS, -1).T.reshape(-1)
     block, row = code % 8, code // 8 % 4
     core, xh = code // 32 % 2, code // 64 % 2
     z, xl, y = code // 128 % 8, code // 1024 % 2, code // 2048
@@ -258,12 +270,15 @@
     cells = block * (CELLS // 8) + away * 4 + row
 
     me = jnp.stack([at["y"], at["xl"]]).astype(I32)
-    expo, stats = scores_of(me, images, img_scale[:, None], pattern, parts, cut)
+    column = img_scale[:, None]
+    none = jnp.zeros((16, LANES), F32)
+    expo0, stats = scores_of(0, me, images, column, pattern, none, first)
+    expo1, stats = scores_of(1, me, images, column, pattern, stats, second)
     others = [
         moved(stats, ORI, lambda h, c: (h + dh, c + dc)) for dh, dc in ((0, 1), (1, 0), (1, 1))
     ]
     scale = img_scale.reshape(8, LANES)
-    keep, send, evidence = bricks_of(cells, scale, (stats, *others), expo, images, weights)
+    keep, send, evidence = bricks_of(cells, scale, (stats, *others), (expo0, expo1), images, weights)
     return brick_share(keep, send), evidence.reshape(-1)
 
 

time: 163 us -> 165 us (1.012); the launches traced: 163 us -> 163 us
  blocking collectives: 46.9 us -> 26.2 us
  starting transfers between devices: 19.1 us -> 35.6 us
  local copies, waits for them, and re-layouts: 4.92 us -> 8.03 us
  Pallas kernels: 44.4 us -> 46.7 us
    all_to_all x2 -> x1, blocking collectives: 31.5 us -> 11.9 us  [spread(): return lax.all_to_all(jnp.broadcast_to(x[None], (n, *x.shape)), axes, 0, 0)]
    all_to_all x0 -> x2, starting transfers between devices: none -> 14.6 us  [spread(): return lax.all_to_all(jnp.broadcast_to(x[None], (n, *x.shape)), axes, 0, 0)]
    ppermute x15, waiting for transfers between devices: 26.7 us -> 13.4 us  [moved(): return lax.ppermute(x, axes, pairs)]
    all_to_all x0 -> x2, waiting for transfers between devices: none -> 12.2 us  [spread(): return lax.all_to_all(jnp.broadcast_to(x[None], (n, *x.shape)), axes, 0, 0)]
    pallas_call x1 -> x2, Pallas kernels: 11.8 us -> 18.5 us  [scores_of(): pl.pallas_call(functools.partial(scores_kernel, group), grid=(IMAGES // r...]
    pallas_call x1, Pallas kernels: 32.6 us -> 28.2 us  [bricks_of(): pl.pallas_call(bricks_kernel, grid=(VALUES // WIDE,), in_specs=[pl.BlockS...]
    ppermute x15, starting transfers between devices: 19 us -> 20.9 us  [moved(): return lax.ppermute(x, axes, pairs)]
    unnamed x27 -> x26, local copies, waits for them, and re-layouts: 2.1 us -> 3.3 us
  transfers between devices with their start and end apart: 16 -> 18, of which waited for: 10 -> 10; matrix products, arithmetic and copies ran while one was open for 4% -> 5% of each run, Pallas kernels for 0% -> 6%
where the time goes in v4:
time: 165 us; the launch traced here: 163 us
  Pallas kernels  46.7 us (28%)
  starting transfers between devices  35.6 us (22%)
  waiting for transfers between devices  27 us (16%)
  blocking collectives  26.2 us (16%)
  between operations  14.3 us (9%)
  local copies, waits for them, and re-layouts  8.03 us (5%)
  other arithmetic  5.14 us (3%)
    pallas_call x1, Pallas kernels, bricks_of(): pl.pallas_call(bricks_kernel, grid=(VALUES // WIDE,), in_specs=[pl.BlockS...  28.2 us
    ppermute x15, starting transfers between devices, moved(): return lax.ppermute(x, axes, pairs)  20.9 us
    pallas_call x2, Pallas kernels, scores_of(): pl.pallas_call(functools.partial(scores_kernel, group), grid=(IMAGES // r...  18.5 us
    all_to_all x2, starting transfers between devices, spread(): return lax.all_to_all(jnp.broadcast_to(x[None], (n, *x.shape)), axes, 0, 0)  14.6 us
    all_to_all x1, blocking collectives, brick_share(): x = jnp.sum(lax.all_to_all(x, ('y', 'xl', 'xh'), 0, 0).astype(F32), axis=0)  14.3 us
    ppermute x15, waiting for transfers between devices, moved(): return lax.ppermute(x, axes, pairs)  13.4 us
    all_to_all x2, waiting for transfers between devices, spread(): return lax.all_to_all(jnp.broadcast_to(x[None], (n, *x.shape)), axes, 0, 0)  12.2 us
    all_to_all x1, blocking collectives, spread(): return lax.all_to_all(jnp.broadcast_to(x[None], (n, *x.shape)), axes, 0, 0)  11.9 us
  transfers between devices with their start and end apart: 18, of which 10 were waited for; matrix products, arithmetic and copies ran while one was open for 5% of the time, Pallas kernels for 6%

profile of v4, /device:TPU:2, one launch (start us, length us, event | category | flops | bytes accessed | tf_op | source)
XLA Modules:
  0.0 162.9 jit_solution(13994205712781278979)
XLA Ops:
  7.2 0.8 fusion.34
  8.0 11.9 %all_to_all.20 = bf16[8,64,256]{2,1,0:T(8,128)(2,1)} all-to-all(bf16[8,64,256]{2,1,0:T(8,128)(2,1)S(1)} %broadcast_in_dim.30), channel_id=1, replica_groups=mesh['y'=4,'xl'=2,'z'=8,'xh'=2,'core'=2] {'y','xl'}, dimensions={0} | all-to-all | bytes 524288 | tf_op jit(solution)/shard_map/all_to_all | solution.py:40
  20.0 0.7 convert_reduce_fusion.2
  20.7 0.7 convert_reduce_fusion.1
  21.4 0.7 broadcast_in_dim.12
  22.2 8.5 %all-to-all-start = ((bf16[8,72,256]{2,1,0:T(8,128)(2,1)}), bf16[8,72,256]{2,1,0:T(8,128)(2,1)S(1)}, u32[]{:S(2)}, u32[]{:S(2)}) async-start(bf16[8,72,256]{2,1,0:T(8,128)(2,1)} %broadcast_in_dim.12), calls=%async_computation | async-start | bytes 589824 | tf_op jit(solution)/shard_map/all_to_all | solution.py:40
  30.6 1.7 %copy.20.scale = f32[1024,1]{1,0:T(8,128)} copy(f32[1024,1]{0,1:T(1,128)} %bitcast.21) | data formatting | bytes 8192 | tf_op jit(solution)/shard_map/broadcast_in_dim | solution.py:273
  32.4 1.7 %copy.21.pattern = s32[1024,2]{1,0:T(8,128)} copy(s32[1024,2]{0,1:T(2,128)} %param.11) | data formatting | bytes 16384 | tf_op args[3]
  34.1 10.8 %all-to-all-done = bf16[8,72,256]{2,1,0:T(8,128)(2,1)S(1)} async-done(((bf16[8,72,256]{2,1,0:T(8,128)(2,1)}), bf16[8,72,256]{2,1,0:T(8,128)(2,1)S(1)}, u32[]{:S(2)}, u32[]{:S(2)}) %all-to-all-start) | async-done | bytes 294944 | tf_op jit(solution)/shard_map/all_to_all | solution.py:40
  44.9 0.1 collective-permute-start.1
  45.0 1.5 collective-permute-start.3
  46.5 0.6 broadcast_in_dim.27
  47.1 6.1 %all-to-all-start.1 = ((bf16[8,8,512]{2,1,0:T(8,128)(2,1)}), bf16[8,8,512]{2,1,0:T(8,128)(2,1)S(1)}, u32[]{:S(2)}, u32[]{:S(2)}) async-start(bf16[8,8,512]{2,1,0:T(8,128)(2,1)} %broadcast_in_dim.27), calls=%async_computation.1 | async-start | bytes 131072 | tf_op jit(solution)/shard_map/all_to_all | solution.py:40
  53.2 0.7 pad_add_fusion.me
  53.9 1.5 collective-permute-start
  55.3 1.8 %collective-permute-start.2 = (bf16[8,64,256]{2,1,0:T(8,128)(2,1)S(1)}, bf16[8,64,256]{2,1,0:T(8,128)(2,1)S(1)}, u32[]{:S(2)}, u32[]{:S(2)}) collective-permute-start(bf16[8,64,256]{2,1,0:T(8,128)(2,1)S(1)} %slice.59.rest_0_), channel_id=1, source_target_pairs={{0,192},{64,0},{128,64},{192,128},{1,193},{65,1},{129,65},{193,129... | collective-permute-start | bytes 786440 | tf_op jit(solution)/shard_map/ppermute | solution.py:35
  57.1 1.5 all-to-all-done.1
  58.6 0.6 collective-permute-start.4
  59.3 2.7 %collective-permute-start.6 = (bf16[8,64,256]{2,1,0:T(8,128)(2,1)S(1)}, bf16[8,64,256]{2,1,0:T(8,128)(2,1)S(1)}, u32[]{:S(2)}, u32[]{:S(2)}) collective-permute-start(bf16[8,64,256]{2,1,0:T(8,128)(2,1)S(1)} %collective-permute-done.3.rest_4_), channel_id=1, source_target_pairs={{0,192},{64,0},{128,64},{192,128},{1,193},{65,1},{129,65},{193,129... | collective-permute-start | bytes 786440 | tf_op jit(solution)/shard_map/ppermute | solution.py:35
  61.9 1.4 collective-permute-start.5
  63.3 0.1 reshape.48
  63.4 0.1 copy.17
  63.6 1.3 all-gather.3.cloned.1.call-done
  64.9 0.6 broadcast_in_dim.29.before
  65.5 9.1 %scores0.1 = (f32[256,1024]{1,0:T(8,128)}, f32[16,128]{1,0:T(8,128)}) custom-call(s32[2]{0:T(128)} %pad_add_fusion.me, bf16[1024,4096]{1,0:T(8,128)(2,1)} %images.5, f32[1024,1]{1,0:T(8,128)} %copy.20.scale, s32[1024,2]{1,0:T(8,128)} %copy.21.pattern, f32[16,128]{1,0:T(8,128)} %broadcast_in_dim.29.before, bf16[8,8,64,256]{3,2,1,0:T(8,128)(2,1)} %bitcast.14), custom_call_target="tpu_custom_call" | custom-call | flops 2147483648 | bytes 11534336 | tf_op jit(solution)/shard_map/scores0/pallas_call | solution.py:106
  74.7 0.6 copy-done.3
  75.3 0.1 copy-done.4
  75.6 0.1 copy-done.6
  75.7 9.4 %scores1.1 = (f32[256,1024]{1,0:T(8,128)}, f32[32,128]{1,0:T(8,128)}) custom-call(s32[2]{0:T(128)} %pad_add_fusion.me, bf16[1024,4096]{1,0:T(8,128)(2,1)} %images.5, f32[1024,1]{1,0:T(8,128)} %copy.20.scale, s32[1024,2]{1,0:T(8,128)} %copy.21.pattern, f32[16,128]{1,0:T(8,128)} %get-tuple-element.9.before, bf16[8,64,256]{2,1,0:T(8,128)(2,1)} %copy-done, ...), custom_call_target="tpu_custom_call" | custom-call | flops 2147483648 | bytes 11534336 | tf_op jit(solution)/shard_map/scores1/pallas_call | solution.py:106
  85.2 2.2 %collective-permute-start.8 = (f32[32,128]{1,0:T(8,128)}, f32[32,128]{1,0:T(8,128)S(1)}, u32[]{:S(2)}, u32[]{:S(2)}) collective-permute-start(f32[32,128]{1,0:T(8,128)} %get-tuple-element.10.s0), channel_id=1, source_target_pairs={{0,2},{1,3},{2,0},{3,1},{4,6},{5,7},{6,4},{7,5},{8,10},{9,11},{10,... | collective-permute-start | bytes 49160 | tf_op jit(solution)/shard_map/ppermute | solution.py:35
  87.4 1.1 collective-permute-start.9
  88.5 1.0 fusion.3.cells
  89.5 1.2 collective-permute-done.8.s2
  90.7 1.6 collective-permute-done.9.s3
  92.3 0.6 copy-done.10
  92.9 28.2 %bricks.1 = (f32[512,512]{1,0:T(8,128)}, f32[512,512]{1,0:T(8,128)}, f32[8,128]{1,0:T(8,128)}) custom-call(s32[16384]{0:T(1024)} %fusion.3.cells, f32[8,128]{1,0:T(8,128)} %bitcast.22, f32[32,128]{1,0:T(8,128)} %get-tuple-element.10.s0, f32[32,128]{1,0:T(8,128)} %copy-done.8, f32[32,128]{1,0:T(8,128)} %copy-done.9, f32[32,128]{1,0:T(8,128)} %copy-done.10, ...), custom_call_target="tpu_custom_call" | custom-call | tf_op jit(solution)/shard_map/bricks/pallas_call | solution.py:217
  121.1 0.2 collective-permute-start.10
  121.2 2.7 %collective-permute-done.10 = f32[512,512]{1,0:T(8,128)S(1)} collective-permute-done((f32[512,512]{1,0:T(8,128)}, f32[512,512]{1,0:T(8,128)S(1)}, u32[]{:S(2)}, u32[]{:S(2)}) %collective-permute-start.10) | collective-permute-done | bytes 1048608 | tf_op jit(solution)/shard_map/ppermute | solution.py:35
  123.9 1.4 add_convert_fusion
  125.3 14.3 %all_to_all.21 = bf16[16,32,512]{2,1,0:T(8,128)(2,1)S(1)} all-to-all(bf16[16,32,512]{2,1,0:T(8,128)(2,1)S(1)} %bitcast.15), channel_id=1, replica_groups=mesh['y'=4,'xl'=2,'z'=8,'xh'=2,'core'=2] {'y','xl','xh'}, dimensions={0} | all-to-all | bytes 1048576 | tf_op jit(solution)/shard_map/all_to_all | solution.py:250
  139.7 3.4 %collective-permute-start.11 = (f32[16,512]{1,0:T(8,128)S(1)}, f32[16,512]{1,0:T(8,128)S(1)}, u32[]{:S(2)}, u32[]{:S(2)}) collective-permute-start(f32[16,512]{1,0:T(8,128)S(1)} %slice.61), channel_id=1, source_target_pairs={{0,16},{4,20},{8,24},{12,28},{16,0},{20,4},{24,8},{28,12},{1,17},{... | collective-permute-start | bytes 98312 | tf_op jit(solution)/shard_map/ppermute | solution.py:35
  143.0 4.5 %collective-permute-done.11 = f32[16,512]{1,0:T(8,128)S(1)} collective-permute-done((f32[16,512]{1,0:T(8,128)S(1)}, f32[16,512]{1,0:T(8,128)S(1)}, u32[]{:S(2)}, u32[]{:S(2)}) %collective-permute-start.11) | collective-permute-done | bytes 32800 | tf_op jit(solution)/shard_map/ppermute | solution.py:35
  147.6 3.3 %collective-permute-start.14 = (f32[4,512]{1,0:T(4,128)S(1)}, f32[4,512]{1,0:T(4,128)S(1)}, u32[]{:S(2)}, u32[]{:S(2)}) collective-permute-start(f32[4,512]{1,0:T(4,128)S(1)} %get-tuple-element.19), channel_id=1, source_target_pairs={{0,12},{4,8},{8,4},{12,0},{16,28},{20,24},{24,20},{28,16},{1,13},{... | collective-permute-start | bytes 24584 | tf_op jit(solution)/shard_map/ppermute | solution.py:35
  150.9 1.2 collective-permute-start.13
  152.1 1.1 collective-permute-done.14
  153.1 1.4 collective-permute-done.12
  154.5 0.9 collective-permute-done.13
  155.4 0.6 slice_add_fusion.2
  (44 shorter events, 0.6 us)
Async XLA Ops:
  7.2 57.7 %all-gather.3.cloned.1.call-start = ((), (), s32[]{:S(2)}) async-start(), calls=%async_computation.4 | async-start | bytes 2359296 | tf_op jit(solution)/shard_map/all_gather | solution.py:46
  22.2 22.7 %all-to-all-start = ((bf16[8,72,256]{2,1,0:T(8,128)(2,1)}), bf16[8,72,256]{2,1,0:T(8,128)(2,1)S(1)}, u32[]{:S(2)}, u32[]{:S(2)}) async-start(bf16[8,72,256]{2,1,0:T(8,128)(2,1)} %broadcast_in_dim.12), calls=%async_computation | async-start | bytes 589824 | tf_op jit(solution)/shard_map/all_to_all | solution.py:40
  44.9 29.8 %copy-start = (bf16[8,64,256]{2,1,0:T(8,128)(2,1)}, bf16[8,64,256]{2,1,0:T(8,128)(2,1)S(1)}, u32[]{:S(2)}) copy-start(bf16[8,64,256]{2,1,0:T(8,128)(2,1)S(1)} %slice.59.rest_0_) | copy-start | bytes 786436
  44.9 17.1 %collective-permute-start.1 = (bf16[8,64,256]{2,1,0:T(8,128)(2,1)S(1)}, bf16[8,64,256]{2,1,0:T(8,128)(2,1)S(1)}, u32[]{:S(2)}, u32[]{:S(2)}) collective-permute-start(bf16[8,64,256]{2,1,0:T(8,128)(2,1)S(1)} %slice.59.rest_0_), channel_id=1, source_target_pairs={{0,128},{64,192},{128,0},{192,64},{1,129},{65,193},{129,1},{193,65... | collective-permute-start | bytes 786440 | tf_op jit(solution)/shard_map/ppermute | solution.py:35
  45.0 13.6 %collective-permute-start.3 = (bf16[8,64,256]{2,1,0:T(8,128)(2,1)S(1)}, bf16[8,64,256]{2,1,0:T(8,128)(2,1)S(1)}, u32[]{:S(2)}, u32[]{:S(2)}) collective-permute-start(bf16[8,64,256]{2,1,0:T(8,128)(2,1)S(1)} %slice.59.rest_0_), channel_id=1, source_target_pairs={{0,32},{32,0},{1,33},{33,1},{2,34},{34,2},{3,35},{35,3},{4,36},{36... | collective-permute-start | bytes 786440 | tf_op jit(solution)/shard_map/ppermute | solution.py:35
  47.1 11.5 %all-to-all-start.1 = ((bf16[8,8,512]{2,1,0:T(8,128)(2,1)}), bf16[8,8,512]{2,1,0:T(8,128)(2,1)S(1)}, u32[]{:S(2)}, u32[]{:S(2)}) async-start(bf16[8,8,512]{2,1,0:T(8,128)(2,1)} %broadcast_in_dim.27), calls=%async_computation.1 | async-start | bytes 131072 | tf_op jit(solution)/shard_map/all_to_all | solution.py:40
  53.9 20.7 %collective-permute-start = (bf16[8,64,256]{2,1,0:T(8,128)(2,1)S(1)}, bf16[8,64,256]{2,1,0:T(8,128)(2,1)S(1)}, u32[]{:S(2)}, u32[]{:S(2)}) collective-permute-start(bf16[8,64,256]{2,1,0:T(8,128)(2,1)S(1)} %slice.59.rest_0_), channel_id=1, source_target_pairs={{0,64},{64,128},{128,192},{192,0},{1,65},{65,129},{129,193},{193,1... | collective-permute-start | bytes 786440 | tf_op jit(solution)/shard_map/ppermute | solution.py:35
  55.3 19.3 %collective-permute-start.2 = (bf16[8,64,256]{2,1,0:T(8,128)(2,1)S(1)}, bf16[8,64,256]{2,1,0:T(8,128)(2,1)S(1)}, u32[]{:S(2)}, u32[]{:S(2)}) collective-permute-start(bf16[8,64,256]{2,1,0:T(8,128)(2,1)S(1)} %slice.59.rest_0_), channel_id=1, source_target_pairs={{0,192},{64,0},{128,64},{192,128},{1,193},{65,1},{129,65},{193,129... | collective-permute-start | bytes 786440 | tf_op jit(solution)/shard_map/ppermute | solution.py:35
  58.6 16.1 %copy-start.2 = (bf16[8,64,256]{2,1,0:T(8,128)(2,1)}, bf16[8,64,256]{2,1,0:T(8,128)(2,1)S(1)}, u32[]{:S(2)}) copy-start(bf16[8,64,256]{2,1,0:T(8,128)(2,1)S(1)} %collective-permute-done.3.rest_4_) | copy-start | bytes 786436
  58.6 16.0 %collective-permute-start.4 = (bf16[8,64,256]{2,1,0:T(8,128)(2,1)S(1)}, bf16[8,64,256]{2,1,0:T(8,128)(2,1)S(1)}, u32[]{:S(2)}, u32[]{:S(2)}) collective-permute-start(bf16[8,64,256]{2,1,0:T(8,128)(2,1)S(1)} %collective-permute-done.3.rest_4_), channel_id=1, source_target_pairs={{0,64},{64,128},{128,192},{192,0},{1,65},{65,129},{129,193},{193,1... | collective-permute-start | bytes 786440 | tf_op jit(solution)/shard_map/ppermute | solution.py:35
  59.3 15.4 %collective-permute-start.6 = (bf16[8,64,256]{2,1,0:T(8,128)(2,1)S(1)}, bf16[8,64,256]{2,1,0:T(8,128)(2,1)S(1)}, u32[]{:S(2)}, u32[]{:S(2)}) collective-permute-start(bf16[8,64,256]{2,1,0:T(8,128)(2,1)S(1)} %collective-permute-done.3.rest_4_), channel_id=1, source_target_pairs={{0,192},{64,0},{128,64},{192,128},{1,193},{65,1},{129,65},{193,129... | collective-permute-start | bytes 786440 | tf_op jit(solution)/shard_map/ppermute | solution.py:35
  61.9 12.8 %copy-start.1 = (bf16[8,64,256]{2,1,0:T(8,128)(2,1)}, bf16[8,64,256]{2,1,0:T(8,128)(2,1)S(1)}, u32[]{:S(2)}) copy-start(bf16[8,64,256]{2,1,0:T(8,128)(2,1)S(1)} %collective-permute-done.1.rest_2_) | copy-start | bytes 786436
  61.9 12.7 %collective-permute-start.5 = (bf16[8,64,256]{2,1,0:T(8,128)(2,1)S(1)}, bf16[8,64,256]{2,1,0:T(8,128)(2,1)S(1)}, u32[]{:S(2)}, u32[]{:S(2)}) collective-permute-start(bf16[8,64,256]{2,1,0:T(8,128)(2,1)S(1)} %collective-permute-done.1.rest_2_), channel_id=1, source_target_pairs={{0,32},{32,0},{1,33},{33,1},{2,34},{34,2},{3,35},{35,3},{4,36},{36... | collective-permute-start | bytes 786440 | tf_op jit(solution)/shard_map/ppermute | solution.py:35
  74.6 0.7 copy-start.3
  74.6 0.8 copy-start.4
  74.7 0.8 copy-start.5
  74.7 0.9 copy-start.7
  74.7 1.0 copy-start.6
  85.1 4.4 %collective-permute-start.7 = (f32[32,128]{1,0:T(8,128)}, f32[32,128]{1,0:T(8,128)S(1)}, u32[]{:S(2)}, u32[]{:S(2)}) collective-permute-start(f32[32,128]{1,0:T(8,128)} %get-tuple-element.10.s0), channel_id=1, source_target_pairs={{0,1},{1,0},{2,3},{3,2},{4,5},{5,4},{6,7},{7,6},{8,9},{9,8},{10,11... | collective-permute-start | bytes 49160 | tf_op jit(solution)/shard_map/ppermute | solution.py:35
  85.2 5.5 %collective-permute-start.8 = (f32[32,128]{1,0:T(8,128)}, f32[32,128]{1,0:T(8,128)S(1)}, u32[]{:S(2)}, u32[]{:S(2)}) collective-permute-start(f32[32,128]{1,0:T(8,128)} %get-tuple-element.10.s0), channel_id=1, source_target_pairs={{0,2},{1,3},{2,0},{3,1},{4,6},{5,7},{6,4},{7,5},{8,10},{9,11},{10,... | collective-permute-start | bytes 49160 | tf_op jit(solution)/shard_map/ppermute | solution.py:35
  87.4 4.9 %collective-permute-start.9 = (f32[32,128]{1,0:T(8,128)}, f32[32,128]{1,0:T(8,128)S(1)}, u32[]{:S(2)}, u32[]{:S(2)}) collective-permute-start(f32[32,128]{1,0:T(8,128)} %get-tuple-element.10.s0), channel_id=1, source_target_pairs={{0,3},{1,2},{2,1},{3,0},{4,7},{5,6},{6,5},{7,4},{8,11},{9,10},{10,... | collective-permute-start | bytes 49160 | tf_op jit(solution)/shard_map/ppermute | solution.py:35
  89.5 2.8 %copy-start.8 = (f32[32,128]{1,0:T(8,128)}, f32[32,128]{1,0:T(8,128)S(1)}, u32[]{:S(2)}) copy-start(f32[32,128]{1,0:T(8,128)S(1)} %collective-permute-done.7.s1) | copy-start | bytes 49156
  90.7 1.6 copy-start.9
  92.3 0.6 copy-start.10
  121.1 2.9 %collective-permute-start.10 = (f32[512,512]{1,0:T(8,128)}, f32[512,512]{1,0:T(8,128)S(1)}, u32[]{:S(2)}, u32[]{:S(2)}) collective-permute-start(f32[512,512]{1,0:T(8,128)} %get-tuple-element.14), channel_id=1, source_target_pairs={{0,1},{1,0},{2,3},{3,2},{4,5},{5,4},{6,7},{7,6},{8,9},{9,8},{10,11... | collective-permute-start | bytes 3145736 | tf_op jit(solution)/shard_map/ppermute | solution.py:35
  139.7 7.9 %collective-permute-start.11 = (f32[16,512]{1,0:T(8,128)S(1)}, f32[16,512]{1,0:T(8,128)S(1)}, u32[]{:S(2)}, u32[]{:S(2)}) collective-permute-start(f32[16,512]{1,0:T(8,128)S(1)} %slice.61), channel_id=1, source_target_pairs={{0,16},{4,20},{8,24},{12,28},{16,0},{20,4},{24,8},{28,12},{1,17},{... | collective-permute-start | bytes 98312 | tf_op jit(solution)/shard_map/ppermute | solution.py:35
  147.6 5.5 %collective-permute-start.14 = (f32[4,512]{1,0:T(4,128)S(1)}, f32[4,512]{1,0:T(4,128)S(1)}, u32[]{:S(2)}, u32[]{:S(2)}) collective-permute-start(f32[4,512]{1,0:T(4,128)S(1)} %get-tuple-element.19), channel_id=1, source_target_pairs={{0,12},{4,8},{8,4},{12,0},{16,28},{20,24},{24,20},{28,16},{1,13},{... | collective-permute-start | bytes 24584 | tf_op jit(solution)/shard_map/ppermute | solution.py:35
  150.9 3.7 %collective-permute-start.12 = (f32[4,512]{1,0:T(4,128)S(1)}, f32[4,512]{1,0:T(4,128)S(1)}, u32[]{:S(2)}, u32[]{:S(2)}) collective-permute-start(f32[4,512]{1,0:T(4,128)S(1)} %get-tuple-element.20), channel_id=1, source_target_pairs={{0,4},{4,0},{8,12},{12,8},{16,20},{20,16},{24,28},{28,24},{1,5},{5... | collective-permute-start | bytes 24584 | tf_op jit(solution)/shard_map/ppermute | solution.py:35
  150.9 4.5 %collective-permute-start.13 = (f32[4,512]{1,0:T(4,128)S(1)}, f32[4,512]{1,0:T(4,128)S(1)}, u32[]{:S(2)}, u32[]{:S(2)}) collective-permute-start(f32[4,512]{1,0:T(4,128)S(1)} %get-tuple-element.18), channel_id=1, source_target_pairs={{0,8},{4,12},{8,0},{12,4},{16,24},{20,28},{24,16},{28,20},{1,9},{5... | collective-permute-start | bytes 24584 | tf_op jit(solution)/shard_map/ppermute | solution.py:35
Sparse Core Ops, SparseCore 0:
  20.1 44.7 all-gather.2

commit v5 on v3

--- a/solution.py
+++ b/solution.py
@@ -46,11 +46,10 @@
     ended_z = lax.all_gather(near, "z", axis=0)
     own = spread(share[cut:], ("z",))
     other = moved(own, ("xl",), lambda xl: (xl + 1,))
-    ended_y = []
-    for part in (own, other):
-        ended_y.append(part)
-        ended_y += [moved(part, ("y",), lambda y: (y + d,)) for d in (1, 2, 3)]
-    return [ended_z, *ended_y]
+    near = [own] + [moved(own, ("y",), lambda y: (y + d,)) for d in (1, 2, 3)]
+    far = [other] + [moved(other, ("y",), lambda y: (y + d,)) for d in (1, 3)]
+    far.insert(2, moved(near[2], ("xl",), lambda xl: (xl + 1,)))
+    return [ended_z, *near, *far]
 
 
 def eye():
@@ -71,20 +70,14 @@
         for i, part in enumerate((a0, a1, a2, a3, b0, b1, b2, b3)):
             y, xl = (me[0] + 4 - i % 4) % 4, (me[1] + i // 4) % 2
             copies.append((part, refs.at[y * 2 + xl, :, pl.ds(cut, SHARE - cut)]))
-        copies = [pltpu.make_async_copy(a, b, sems.at[i]) for i, (a, b) in enumerate(copies)]
-        for c in copies:
-            c.start()
-        for c in copies:
-            c.wait()
-
-    total = jnp.zeros((rows, REFS), F32)
-    wide = 8 * SHARE
-    for q in range(8):
-        total += jnp.dot(
-            images[:, q * wide : (q + 1) * wide],
-            refs[q].reshape(wide, REFS),
-            preferred_element_type=F32,
-        )
+        for i, (a, b) in enumerate(copies):
+            pltpu.make_async_copy(a, b, sems.at[i]).start()
+        for i, (a, b) in enumerate(copies):
+            pltpu.make_async_copy(a, b, sems.at[i]).wait()
+
+    total = jnp.dot(
+        images[...], refs[...].reshape(VALUES, REFS), preferred_element_type=F32
+    )
     scores = total * scale[...] * (1.0 / math.sqrt(VALUES))
     group = lax.broadcasted_iota(I32, (rows, REFS), 1) // (REFS // 2)
     flags = pattern[...]
@@ -171,7 +164,7 @@
     def add(i, _):
         for u in range(UNROLL):
             row = i * UNROLL + u
-            cell = pl.ds(cells[step * count + row], 1)
+            cell = pl.ds(cells[row], 1)
             c = sums[u % SUMS]
             c[cell, :] = c[cell, :] + tiles[pl.ds(row, 1), :]
         return 0
@@ -206,7 +199,9 @@
         bricks_kernel,
         grid=(VALUES // WIDE,),
         in_specs=[
-            pl.BlockSpec(memory_space=pltpu.SMEM),
+            pl.BlockSpec(
+                (WIDE // LANES * REFS,), lambda i: (i,), memory_space=pltpu.SMEM
+            ),
             pl.BlockSpec((8, LANES), lambda i: (0, 0)),
             *[pl.BlockSpec((16, LANES), lambda i: (0, 0))] * 4,
             pl.BlockSpec((REFS, IMAGES), lambda i: (0, 0)),

time: 163 us -> 159 us (0.975)
  Pallas kernels: 44.4 us -> 40 us
  waiting for transfers between devices: 27 us -> 25.2 us
  starting transfers between devices: 19.1 us -> 20.9 us
    ppermute x15, waiting for transfers between devices: 26.7 us -> 18.9 us  [moved(): return lax.ppermute(x, axes, pairs)]
    all_gather x1, waiting for transfers between devices: 0.29 us -> 6.3 us  [gathered_references(): ended_z = lax.all_gather(near, 'z', axis=0)]
    pallas_call x1, Pallas kernels: 32.6 us -> 28.2 us  [bricks_of(): pl.pallas_call(bricks_kernel, grid=(VALUES // WIDE,), in_specs=[pl.BlockS...]
    ppermute x15, starting transfers between devices: 19 us -> 20.9 us  [moved(): return lax.ppermute(x, axes, pairs)]
  transfers between devices with their start and end apart: 16 -> 16, of which waited for: 10 -> 9; matrix products, arithmetic and copies ran while one was open for 4% -> 4% of each run, Pallas kernels for 0% -> 0%
where the time goes in v5:
time: 159 us; the launch traced here: 158 us
  blocking collectives  47.2 us (30%)
  Pallas kernels  40 us (25%)
  waiting for transfers between devices  25.2 us (16%)
  starting transfers between devices  20.9 us (13%)
  between operations  14.2 us (9%)
  other arithmetic  6.12 us (4%)
  local copies, waits for them, and re-layouts  4.51 us (3%)
    all_to_all x2, blocking collectives, spread(): return lax.all_to_all(jnp.broadcast_to(x[None], (n, *x.shape)), axes, 0, 0)  31.5 us
    pallas_call x1, Pallas kernels, bricks_of(): pl.pallas_call(bricks_kernel, grid=(VALUES // WIDE,), in_specs=[pl.BlockS...  28.2 us
    ppermute x15, starting transfers between devices, moved(): return lax.ppermute(x, axes, pairs)  20.9 us
    ppermute x15, waiting for transfers between devices, moved(): return lax.ppermute(x, axes, pairs)  18.9 us
    all_to_all x1, blocking collectives, brick_share(): x = jnp.sum(lax.all_to_all(x, ('y', 'xl', 'xh'), 0, 0).astype(F32), axis=0)  15.7 us
    pallas_call x1, Pallas kernels, scores_of(): pl.pallas_call(functools.partial(scores_kernel, cut), grid=(IMAGES // row...  11.8 us
    all_gather x1, waiting for transfers between devices, gathered_references(): ended_z = lax.all_gather(near, 'z', axis=0)  6.3 us
  transfers between devices with their start and end apart: 16, of which 9 were waited for; matrix products, arithmetic and copies ran while one was open for 4% of the time, Pallas kernels for 0%

profile of v5, /device:TPU:2, one launch (start us, length us, event | category | flops | bytes accessed | tf_op | source)
XLA Modules:
  0.0 158.1 jit_solution(2567385940503141820)
XLA Ops:
  7.2 0.0 all-gather.3.cloned.1.call-start
  7.2 0.8 fusion.36
  8.0 0.7 convert_bitcast_fusion
  8.7 0.7 add_convert_fusion.1
  9.4 12.6 %all_to_all.15 = bf16[8,40,512]{2,1,0:T(8,128)(2,1)} all-to-all(bf16[8,40,512]{2,1,0:T(8,128)(2,1)S(1)} %broadcast_in_dim.6), channel_id=1, replica_groups=mesh['y'=4,'xl'=2,'z'=8,'xh'=2,'core'=2] {'y','xl'}, dimensions={0} | all-to-all | bytes 655360 | tf_op jit(solution)/shard_map/all_to_all | solution.py:39
  22.1 0.0 all-gather.3.cloned.1.call-update
  22.1 18.8 %all_to_all.16.a0 = bf16[8,32,512]{2,1,0:T(8,128)(2,1)S(1)} all-to-all(bf16[8,32,512]{2,1,0:T(8,128)(2,1)S(1)} %broadcast_in_dim.8), channel_id=1, replica_groups=mesh['y'=4,'xl'=2,'z'=8,'xh'=2,'core'=2] {'z'}, dimensions={0} | all-to-all | bytes 524288 | tf_op jit(solution)/shard_map/all_to_all | solution.py:39
  41.0 1.3 collective-permute-start.3
  42.3 1.3 collective-permute-start.1
  43.5 0.7 collective-permute-start
  44.2 2.6 %collective-permute-start.2 = (bf16[8,32,512]{2,1,0:T(8,128)(2,1)S(1)}, bf16[8,32,512]{2,1,0:T(8,128)(2,1)S(1)}, u32[]{:S(2)}, u32[]{:S(2)}) collective-permute-start(bf16[8,32,512]{2,1,0:T(8,128)(2,1)S(1)} %all_to_all.16.a0), channel_id=1, source_target_pairs={{0,192},{64,0},{128,64},{192,128},{1,193},{65,1},{129,65},{193,129... | collective-permute-start | bytes 786440 | tf_op jit(solution)/shard_map/ppermute | solution.py:34
  46.8 0.6 collective-permute-done.3.b0
  47.3 0.6 collective-permute-start.4
  47.9 2.6 %collective-permute-start.6 = (bf16[8,32,512]{2,1,0:T(8,128)(2,1)S(1)}, bf16[8,32,512]{2,1,0:T(8,128)(2,1)S(1)}, u32[]{:S(2)}, u32[]{:S(2)}) collective-permute-start(bf16[8,32,512]{2,1,0:T(8,128)(2,1)S(1)} %collective-permute-done.3.b0), channel_id=1, source_target_pairs={{0,192},{64,0},{128,64},{192,128},{1,193},{65,1},{129,65},{193,129... | collective-permute-start | bytes 786440 | tf_op jit(solution)/shard_map/ppermute | solution.py:34
  50.6 2.4 %collective-permute-done.1.a2 = bf16[8,32,512]{2,1,0:T(8,128)(2,1)S(1)} collective-permute-done((bf16[8,32,512]{2,1,0:T(8,128)(2,1)S(1)}, bf16[8,32,512]{2,1,0:T(8,128)(2,1)S(1)}, u32[]{:S(2)}, u32[]{:S(2)}) %collective-permute-start.1) | collective-permute-done | bytes 262176 | tf_op jit(solution)/shard_map/ppermute | solution.py:34
  53.0 0.7 collective-permute-start.5
  53.8 1.7 %copy.17.scale = f32[1024,1]{1,0:T(8,128)} copy(f32[1024,1]{0,1:T(1,128)} %bitcast.26) | data formatting | bytes 8192 | tf_op jit(solution)/shard_map/broadcast_in_dim | solution.py:256
  55.5 1.0 copy.18.pattern
  56.5 0.6 pad_add_fusion.me
  57.1 0.0 collective-permute-done.a1
  57.1 0.0 collective-permute-done.2.a3
  57.1 3.0 %collective-permute-done.4.b1 = bf16[8,32,512]{2,1,0:T(8,128)(2,1)S(1)} collective-permute-done((bf16[8,32,512]{2,1,0:T(8,128)(2,1)S(1)}, bf16[8,32,512]{2,1,0:T(8,128)(2,1)S(1)}, u32[]{:S(2)}, u32[]{:S(2)}) %collective-permute-start.4) | collective-permute-done | bytes 262176 | tf_op jit(solution)/shard_map/ppermute | solution.py:34
  60.1 6.3 %all-gather.3.cloned.1.call-done = bf16[64,40,512]{2,1,0:T(8,128)(2,1)} async-done(((bf16[8,40,512]{2,1,0:T(8,128)(2,1)}), bf16[64,40,512]{2,1,0:T(8,128)(2,1)}) %all-gather.3.cloned.1.call-update) | async-done | bytes 2621456 | tf_op jit(solution)/shard_map/all_gather | solution.py:46
  66.5 11.8 %scores.1 = (f32[512,1024]{1,0:T(8,128)}, f32[16,128]{1,0:T(8,128)}) custom-call(s32[2]{0:T(128)} %pad_add_fusion.me, bf16[1024,4096]{1,0:T(8,128)(2,1)} %images.3, f32[1024,1]{1,0:T(8,128)} %copy.17.scale, s32[1024,2]{1,0:T(8,128)} %copy.18.pattern, bf16[8,8,40,512]{3,2,1,0:T(8,128)(2,1)} %bitcast.18, bf16[8,32,512]{2,1,0:T(8,128)(2,1)} %copy-done, ...), custom_call_target="tpu_custom_call" | custom-call | tf_op jit(solution)/shard_map/scores/pallas_call | solution.py:100
  78.3 0.1 collective-permute-start.7
  78.4 2.2 %collective-permute-start.8 = (f32[16,128]{1,0:T(8,128)}, f32[16,128]{1,0:T(8,128)S(1)}, u32[]{:S(2)}, u32[]{:S(2)}) collective-permute-start(f32[16,128]{1,0:T(8,128)} %get-tuple-element.7.s0), channel_id=1, source_target_pairs={{0,2},{1,3},{2,0},{3,1},{4,6},{5,7},{6,4},{7,5},{8,10},{9,11},{10,... | collective-permute-start | bytes 24584 | tf_op jit(solution)/shard_map/ppermute | solution.py:34
  80.6 1.2 collective-permute-start.9
  81.8 1.1 slice_convert_fusion
  83.0 0.1 reshape.67
  83.1 0.1 copy.16
  83.2 0.9 fusion.2.cells
  84.2 1.2 collective-permute-done.9.s3
  85.4 0.6 copy-done.11
  86.0 28.2 %bricks.1 = (f32[512,512]{1,0:T(8,128)}, f32[512,512]{1,0:T(8,128)}, f32[8,128]{1,0:T(8,128)}) custom-call(s32[16384]{0:T(1024)} %fusion.2.cells, f32[8,128]{1,0:T(8,128)} %bitcast.27, f32[16,128]{1,0:T(8,128)} %get-tuple-element.7.s0, f32[16,128]{1,0:T(8,128)} %copy-done.9, f32[16,128]{1,0:T(8,128)} %copy-done.10, f32[16,128]{1,0:T(8,128)} %copy-done.11, ...), custom_call_target="tpu_custom_call" | custom-call | tf_op jit(solution)/shard_map/bricks/pallas_call | solution.py:198
  114.2 0.1 collective-permute-start.10
  114.3 2.7 %collective-permute-done.10 = f32[512,512]{1,0:T(8,128)S(1)} collective-permute-done((f32[512,512]{1,0:T(8,128)}, f32[512,512]{1,0:T(8,128)S(1)}, u32[]{:S(2)}, u32[]{:S(2)}) %collective-permute-start.10) | collective-permute-done | bytes 1048608 | tf_op jit(solution)/shard_map/ppermute | solution.py:34
  117.0 1.4 add_convert_fusion
  118.4 15.7 %all_to_all.17 = bf16[16,32,512]{2,1,0:T(8,128)(2,1)S(1)} all-to-all(bf16[16,32,512]{2,1,0:T(8,128)(2,1)S(1)} %bitcast.20), channel_id=1, replica_groups=mesh['y'=4,'xl'=2,'z'=8,'xh'=2,'core'=2] {'y','xl','xh'}, dimensions={0} | all-to-all | bytes 1048576 | tf_op jit(solution)/shard_map/all_to_all | solution.py:231
  134.1 0.1 convert_reduce_fusion
  134.2 3.0 %collective-permute-start.11 = (f32[16,512]{1,0:T(8,128)S(1)}, f32[16,512]{1,0:T(8,128)S(1)}, u32[]{:S(2)}, u32[]{:S(2)}) collective-permute-start(f32[16,512]{1,0:T(8,128)S(1)} %slice.56), channel_id=1, source_target_pairs={{0,16},{4,20},{8,24},{12,28},{16,0},{20,4},{24,8},{28,12},{1,17},{... | collective-permute-start | bytes 98312 | tf_op jit(solution)/shard_map/ppermute | solution.py:34
  137.3 5.1 %collective-permute-done.11 = f32[16,512]{1,0:T(8,128)S(1)} collective-permute-done((f32[16,512]{1,0:T(8,128)S(1)}, f32[16,512]{1,0:T(8,128)S(1)}, u32[]{:S(2)}, u32[]{:S(2)}) %collective-permute-start.11) | collective-permute-done | bytes 32800 | tf_op jit(solution)/shard_map/ppermute | solution.py:34
  142.3 1.1 collective-permute-start.12
  143.4 1.8 %collective-permute-start.13 = (f32[4,512]{1,0:T(4,128)S(1)}, f32[4,512]{1,0:T(4,128)S(1)}, u32[]{:S(2)}, u32[]{:S(2)}) collective-permute-start(f32[4,512]{1,0:T(4,128)S(1)} %get-tuple-element.14), channel_id=1, source_target_pairs={{0,8},{4,12},{8,0},{12,4},{16,24},{20,28},{24,16},{28,20},{1,9},{5... | collective-permute-start | bytes 24584 | tf_op jit(solution)/shard_map/ppermute | solution.py:34
  145.2 1.6 collective-permute-start.14
  146.8 0.0 collective-permute-done.12
  146.8 1.1 collective-permute-done.13
  148.0 2.7 %collective-permute-done.14 = f32[4,512]{1,0:T(4,128)S(1)} collective-permute-done((f32[4,512]{1,0:T(4,128)S(1)}, f32[4,512]{1,0:T(4,128)S(1)}, u32[]{:S(2)}, u32[]{:S(2)}) %collective-permute-start.14) | collective-permute-done | bytes 8224 | tf_op jit(solution)/shard_map/ppermute | solution.py:34
  150.7 0.6 slice_add_fusion.2
  (38 shorter events, 0.2 us)
Async XLA Ops:
  7.2 48.3 %copy-start.8 = (s32[1024,2]{0,1:T(2,128)S(1)}, s32[1024,2]{0,1:T(2,128)}, u32[]{:S(2)}) copy-start(s32[1024,2]{0,1:T(2,128)} %param.11) | copy-start | bytes 24580
  7.2 59.2 %all-gather.3.cloned.1.call-start = ((), (), s32[]{:S(2)}) async-start(), calls=%async_computation.3 | async-start | bytes 2949120 | tf_op jit(solution)/shard_map/all_gather | solution.py:46
  41.0 25.4 %copy-start = (bf16[8,32,512]{2,1,0:T(8,128)(2,1)}, bf16[8,32,512]{2,1,0:T(8,128)(2,1)S(1)}, u32[]{:S(2)}) copy-start(bf16[8,32,512]{2,1,0:T(8,128)(2,1)S(1)} %all_to_all.16.a0) | copy-start | bytes 786436
  41.0 6.4 %collective-permute-start.3 = (bf16[8,32,512]{2,1,0:T(8,128)(2,1)S(1)}, bf16[8,32,512]{2,1,0:T(8,128)(2,1)S(1)}, u32[]{:S(2)}, u32[]{:S(2)}) collective-permute-start(bf16[8,32,512]{2,1,0:T(8,128)(2,1)S(1)} %all_to_all.16.a0), channel_id=1, source_target_pairs={{0,32},{32,0},{1,33},{33,1},{2,34},{34,2},{3,35},{35,3},{4,36},{36... | collective-permute-start | bytes 786440 | tf_op jit(solution)/shard_map/ppermute | solution.py:34
  42.3 10.7 %collective-permute-start.1 = (bf16[8,32,512]{2,1,0:T(8,128)(2,1)S(1)}, bf16[8,32,512]{2,1,0:T(8,128)(2,1)S(1)}, u32[]{:S(2)}, u32[]{:S(2)}) collective-permute-start(bf16[8,32,512]{2,1,0:T(8,128)(2,1)S(1)} %all_to_all.16.a0), channel_id=1, source_target_pairs={{0,128},{64,192},{128,0},{192,64},{1,129},{65,193},{129,1},{193,65... | collective-permute-start | bytes 786440 | tf_op jit(solution)/shard_map/ppermute | solution.py:34
  43.5 13.5 %collective-permute-start = (bf16[8,32,512]{2,1,0:T(8,128)(2,1)S(1)}, bf16[8,32,512]{2,1,0:T(8,128)(2,1)S(1)}, u32[]{:S(2)}, u32[]{:S(2)}) collective-permute-start(bf16[8,32,512]{2,1,0:T(8,128)(2,1)S(1)} %all_to_all.16.a0), channel_id=1, source_target_pairs={{0,64},{64,128},{128,192},{192,0},{1,65},{65,129},{129,193},{193,1... | collective-permute-start | bytes 786440 | tf_op jit(solution)/shard_map/ppermute | solution.py:34
  44.2 12.9 %collective-permute-start.2 = (bf16[8,32,512]{2,1,0:T(8,128)(2,1)S(1)}, bf16[8,32,512]{2,1,0:T(8,128)(2,1)S(1)}, u32[]{:S(2)}, u32[]{:S(2)}) collective-permute-start(bf16[8,32,512]{2,1,0:T(8,128)(2,1)S(1)} %all_to_all.16.a0), channel_id=1, source_target_pairs={{0,192},{64,0},{128,64},{192,128},{1,193},{65,1},{129,65},{193,129... | collective-permute-start | bytes 786440 | tf_op jit(solution)/shard_map/ppermute | solution.py:34
  47.3 19.1 %copy-start.1 = (bf16[8,32,512]{2,1,0:T(8,128)(2,1)}, bf16[8,32,512]{2,1,0:T(8,128)(2,1)S(1)}, u32[]{:S(2)}) copy-start(bf16[8,32,512]{2,1,0:T(8,128)(2,1)S(1)} %collective-permute-done.3.b0) | copy-start | bytes 786436
  47.3 12.7 %collective-permute-start.4 = (bf16[8,32,512]{2,1,0:T(8,128)(2,1)S(1)}, bf16[8,32,512]{2,1,0:T(8,128)(2,1)S(1)}, u32[]{:S(2)}, u32[]{:S(2)}) collective-permute-start(bf16[8,32,512]{2,1,0:T(8,128)(2,1)S(1)} %collective-permute-done.3.b0), channel_id=1, source_target_pairs={{0,64},{64,128},{128,192},{192,0},{1,65},{65,129},{129,193},{193,1... | collective-permute-start | bytes 786440 | tf_op jit(solution)/shard_map/ppermute | solution.py:34
  47.9 12.2 %collective-permute-start.6 = (bf16[8,32,512]{2,1,0:T(8,128)(2,1)S(1)}, bf16[8,32,512]{2,1,0:T(8,128)(2,1)S(1)}, u32[]{:S(2)}, u32[]{:S(2)}) collective-permute-start(bf16[8,32,512]{2,1,0:T(8,128)(2,1)S(1)} %collective-permute-done.3.b0), channel_id=1, source_target_pairs={{0,192},{64,0},{128,64},{192,128},{1,193},{65,1},{129,65},{193,129... | collective-permute-start | bytes 786440 | tf_op jit(solution)/shard_map/ppermute | solution.py:34
  53.0 13.4 %copy-start.2 = (bf16[8,32,512]{2,1,0:T(8,128)(2,1)}, bf16[8,32,512]{2,1,0:T(8,128)(2,1)S(1)}, u32[]{:S(2)}) copy-start(bf16[8,32,512]{2,1,0:T(8,128)(2,1)S(1)} %collective-permute-done.1.a2) | copy-start | bytes 786436
  53.0 7.1 %collective-permute-start.5 = (bf16[8,32,512]{2,1,0:T(8,128)(2,1)S(1)}, bf16[8,32,512]{2,1,0:T(8,128)(2,1)S(1)}, u32[]{:S(2)}, u32[]{:S(2)}) collective-permute-start(bf16[8,32,512]{2,1,0:T(8,128)(2,1)S(1)} %collective-permute-done.1.a2), channel_id=1, source_target_pairs={{0,32},{32,0},{1,33},{33,1},{2,34},{34,2},{3,35},{35,3},{4,36},{36... | collective-permute-start | bytes 786440 | tf_op jit(solution)/shard_map/ppermute | solution.py:34
  57.1 9.3 %copy-start.3 = (bf16[8,32,512]{2,1,0:T(8,128)(2,1)}, bf16[8,32,512]{2,1,0:T(8,128)(2,1)S(1)}, u32[]{:S(2)}) copy-start(bf16[8,32,512]{2,1,0:T(8,128)(2,1)S(1)} %collective-permute-done.a1) | copy-start | bytes 786436
  57.1 9.3 %copy-start.4 = (bf16[8,32,512]{2,1,0:T(8,128)(2,1)}, bf16[8,32,512]{2,1,0:T(8,128)(2,1)S(1)}, u32[]{:S(2)}) copy-start(bf16[8,32,512]{2,1,0:T(8,128)(2,1)S(1)} %collective-permute-done.2.a3) | copy-start | bytes 786436
  60.1 6.3 %copy-start.5 = (bf16[8,32,512]{2,1,0:T(8,128)(2,1)}, bf16[8,32,512]{2,1,0:T(8,128)(2,1)S(1)}, u32[]{:S(2)}) copy-start(bf16[8,32,512]{2,1,0:T(8,128)(2,1)S(1)} %collective-permute-done.4.b1) | copy-start | bytes 786436
  60.1 6.4 %copy-start.6 = (bf16[8,32,512]{2,1,0:T(8,128)(2,1)}, bf16[8,32,512]{2,1,0:T(8,128)(2,1)S(1)}, u32[]{:S(2)}) copy-start(bf16[8,32,512]{2,1,0:T(8,128)(2,1)S(1)} %collective-permute-done.6.b3) | copy-start | bytes 786436
  60.1 6.4 %copy-start.7 = (bf16[8,32,512]{2,1,0:T(8,128)(2,1)}, bf16[8,32,512]{2,1,0:T(8,128)(2,1)S(1)}, u32[]{:S(2)}) copy-start(bf16[8,32,512]{2,1,0:T(8,128)(2,1)S(1)} %collective-permute-done.5.b2) | copy-start | bytes 786436
  78.3 5.9 %collective-permute-start.7 = (f32[16,128]{1,0:T(8,128)}, f32[16,128]{1,0:T(8,128)S(1)}, u32[]{:S(2)}, u32[]{:S(2)}) collective-permute-start(f32[16,128]{1,0:T(8,128)} %get-tuple-element.7.s0), channel_id=1, source_target_pairs={{0,1},{1,0},{2,3},{3,2},{4,5},{5,4},{6,7},{7,6},{8,9},{9,8},{10,11... | collective-permute-start | bytes 24584 | tf_op jit(solution)/shard_map/ppermute | solution.py:34
  78.4 5.8 %collective-permute-start.8 = (f32[16,128]{1,0:T(8,128)}, f32[16,128]{1,0:T(8,128)S(1)}, u32[]{:S(2)}, u32[]{:S(2)}) collective-permute-start(f32[16,128]{1,0:T(8,128)} %get-tuple-element.7.s0), channel_id=1, source_target_pairs={{0,2},{1,3},{2,0},{3,1},{4,6},{5,7},{6,4},{7,5},{8,10},{9,11},{10,... | collective-permute-start | bytes 24584 | tf_op jit(solution)/shard_map/ppermute | solution.py:34
  80.6 4.8 %collective-permute-start.9 = (f32[16,128]{1,0:T(8,128)}, f32[16,128]{1,0:T(8,128)S(1)}, u32[]{:S(2)}, u32[]{:S(2)}) collective-permute-start(f32[16,128]{1,0:T(8,128)} %get-tuple-element.7.s0), channel_id=1, source_target_pairs={{0,3},{1,2},{2,1},{3,0},{4,7},{5,6},{6,5},{7,4},{8,11},{9,10},{10,... | collective-permute-start | bytes 24584 | tf_op jit(solution)/shard_map/ppermute | solution.py:34
  84.2 1.2 copy-start.9
  84.2 1.2 copy-start.10
  85.4 0.6 copy-start.11
  114.2 2.9 %collective-permute-start.10 = (f32[512,512]{1,0:T(8,128)}, f32[512,512]{1,0:T(8,128)S(1)}, u32[]{:S(2)}, u32[]{:S(2)}) collective-permute-start(f32[512,512]{1,0:T(8,128)} %get-tuple-element.10), channel_id=1, source_target_pairs={{0,1},{1,0},{2,3},{3,2},{4,5},{5,4},{6,7},{7,6},{8,9},{9,8},{10,11... | collective-permute-start | bytes 3145736 | tf_op jit(solution)/shard_map/ppermute | solution.py:34
  134.2 8.1 %collective-permute-start.11 = (f32[16,512]{1,0:T(8,128)S(1)}, f32[16,512]{1,0:T(8,128)S(1)}, u32[]{:S(2)}, u32[]{:S(2)}) collective-permute-start(f32[16,512]{1,0:T(8,128)S(1)} %slice.56), channel_id=1, source_target_pairs={{0,16},{4,20},{8,24},{12,28},{16,0},{20,4},{24,8},{28,12},{1,17},{... | collective-permute-start | bytes 98312 | tf_op jit(solution)/shard_map/ppermute | solution.py:34
  142.3 4.5 %collective-permute-start.12 = (f32[4,512]{1,0:T(4,128)S(1)}, f32[4,512]{1,0:T(4,128)S(1)}, u32[]{:S(2)}, u32[]{:S(2)}) collective-permute-start(f32[4,512]{1,0:T(4,128)S(1)} %get-tuple-element.16), channel_id=1, source_target_pairs={{0,4},{4,0},{8,12},{12,8},{16,20},{20,16},{24,28},{28,24},{1,5},{5... | collective-permute-start | bytes 24584 | tf_op jit(solution)/shard_map/ppermute | solution.py:34
  143.4 4.5 %collective-permute-start.13 = (f32[4,512]{1,0:T(4,128)S(1)}, f32[4,512]{1,0:T(4,128)S(1)}, u32[]{:S(2)}, u32[]{:S(2)}) collective-permute-start(f32[4,512]{1,0:T(4,128)S(1)} %get-tuple-element.14), channel_id=1, source_target_pairs={{0,8},{4,12},{8,0},{12,4},{16,24},{20,28},{24,16},{28,20},{1,9},{5... | collective-permute-start | bytes 24584 | tf_op jit(solution)/shard_map/ppermute | solution.py:34
  145.2 5.4 %collective-permute-start.14 = (f32[4,512]{1,0:T(4,128)S(1)}, f32[4,512]{1,0:T(4,128)S(1)}, u32[]{:S(2)}, u32[]{:S(2)}) collective-permute-start(f32[4,512]{1,0:T(4,128)S(1)} %get-tuple-element.15), channel_id=1, source_target_pairs={{0,12},{4,8},{8,4},{12,0},{16,28},{20,24},{24,20},{28,16},{1,13},{... | collective-permute-start | bytes 24584 | tf_op jit(solution)/shard_map/ppermute | solution.py:34
Sparse Core Ops, SparseCore 0:
  22.2 44.1 all-gather.2

commit v6 on v5

--- a/solution.py
+++ b/solution.py
@@ -41,15 +41,18 @@
 
 def gathered_references(references, codes, cut):
     share = references.T
+    near = spread(share[:cut], ("y", "xl"))
+    ended_z = lax.all_gather(near, "z", axis=0)
     more = jnp.pad(codes.astype(BF16)[None], ((0, 7), (0, 0)))
-    near = spread(jnp.concatenate([share[:cut], more]), ("y", "xl"))
-    ended_z = lax.all_gather(near, "z", axis=0)
-    own = spread(share[cut:], ("z",))
+    own = spread(jnp.concatenate([share[cut:], more]), ("z",))
+    codes, own = own[:, SHARE - cut], own[:, : SHARE - cut]
     other = moved(own, ("xl",), lambda xl: (xl + 1,))
     near = [own] + [moved(own, ("y",), lambda y: (y + d,)) for d in (1, 2, 3)]
     far = [other] + [moved(other, ("y",), lambda y: (y + d,)) for d in (1, 3)]
     far.insert(2, moved(near[2], ("xl",), lambda xl: (xl + 1,)))
-    return [ended_z, *near, *far]
+    codes, _ = lax.optimization_barrier((codes, other))
+    codes = spread(codes, ("y", "xl")).astype(I32)
+    return [ended_z, *near, *far], codes
 
 
 def eye():
@@ -66,7 +69,7 @@
 
     @pl.when(step == 0)
     def _():
-        copies = [(by_z.at[z, :, pl.ds(0, cut)], refs.at[:, z, pl.ds(0, cut)]) for z in range(8)]
+        copies = [(by_z.at[z], refs.at[:, z, pl.ds(0, cut)]) for z in range(8)]
         for i, part in enumerate((a0, a1, a2, a3, b0, b1, b2, b3)):
             y, xl = (me[0] + 4 - i % 4) % 4, (me[1] + i // 4) % 2
             copies.append((part, refs.at[y * 2 + xl, :, pl.ds(cut, SHARE - cut)]))
@@ -240,11 +243,10 @@
     at = {a: lax.axis_index(a) for a in AXES}
     owned = tile_owner.reshape(-1)
     codes = jnp.concatenate([owned, (tile_brick * 8 + tile_block).reshape(-1)])
-    parts = gathered_references(references, codes, cut)
-
-    code = parts[0][:, :, cut].astype(I32)
+    parts, code = gathered_references(references, codes, cut)
+
     code = code[..., : owned.size] * 128 + code[..., owned.size :]
-    code = code.swapaxes(0, 1).reshape(REFS, -1).T.reshape(-1)
+    code = code.reshape(REFS, -1).T.reshape(-1)
     block, row = code % 8, code // 8 % 4
     core, xh = code // 32 % 2, code // 64 % 2
     z, xl, y = code // 128 % 8, code // 1024 % 2, code // 2048

time: 159 us -> 156 us (0.981)
  waiting for transfers between devices: 25.2 us -> 21.3 us
  blocking collectives: 47.2 us -> 50.2 us
    all_gather x1, waiting for transfers between devices: 6.3 us -> 0.01 us  [gathered_references(): ended_z = lax.all_gather(near, 'z', axis=0)]
    ppermute x15, starting transfers between devices: 20.9 us -> 15.3 us  [moved(): return lax.ppermute(x, axes, pairs)]
    all_to_all x0 -> x1, starting transfers between devices: none -> 4.55 us  [spread(): return lax.all_to_all(jnp.broadcast_to(x[None], (n, *x.shape)), axes, 0, 0)]
    all_to_all x2, blocking collectives: 31.5 us -> 35 us  [spread(): return lax.all_to_all(jnp.broadcast_to(x[None], (n, *x.shape)), axes, 0, 0)]
    ppermute x15, waiting for transfers between devices: 18.9 us -> 21.3 us  [moved(): return lax.ppermute(x, axes, pairs)]
  transfers between devices with their start and end apart: 16 -> 17, of which waited for: 9 -> 10; matrix products, arithmetic and copies ran while one was open for 4% -> 4% of each run, Pallas kernels for 0% -> 0%
where the time goes in v6:
time: 156 us
  blocking collectives  50.2 us (32%)
  Pallas kernels  40 us (26%)
  waiting for transfers between devices  21.3 us (14%)
  starting transfers between devices  19.9 us (13%)
  between operations  14.3 us (9%)
  local copies, waits for them, and re-layouts  5.2 us (3%)
  other arithmetic  5.09 us (3%)
    all_to_all x2, blocking collectives, spread(): return lax.all_to_all(jnp.broadcast_to(x[None], (n, *x.shape)), axes, 0, 0)  35 us
    pallas_call x1, Pallas kernels, bricks_of(): pl.pallas_call(bricks_kernel, grid=(VALUES // WIDE,), in_specs=[pl.BlockS...  28.2 us
    ppermute x15, waiting for transfers between devices, moved(): return lax.ppermute(x, axes, pairs)  21.3 us
    ppermute x15, starting transfers between devices, moved(): return lax.ppermute(x, axes, pairs)  15.3 us
    all_to_all x1, blocking collectives, brick_share(): x = jnp.sum(lax.all_to_all(x, ('y', 'xl', 'xh'), 0, 0).astype(F32), axis=0)  15.2 us
    pallas_call x1, Pallas kernels, scores_of(): pl.pallas_call(functools.partial(scores_kernel, cut), grid=(IMAGES // row...  11.8 us
    all_to_all x1, starting transfers between devices, spread(): return lax.all_to_all(jnp.broadcast_to(x[None], (n, *x.shape)), axes, 0, 0)  4.55 us
  transfers between devices with their start and end apart: 17, of which 10 were waited for; matrix products, arithmetic and copies ran while one was open for 4% of the time, Pallas kernels for 0%

profile of v6, /device:TPU:2, one launch (start us, length us, event | category | flops | bytes accessed | tf_op | source)
XLA Modules:
  0.0 156.0 jit_solution(9129695699373722772)
XLA Ops:
  7.2 0.0 copy-start.8
  7.2 0.0 all-gather.3.cloned.1.call-start
  7.2 0.8 fusion.35
  8.0 11.9 %all_to_all.20 = bf16[8,32,512]{2,1,0:T(8,128)(2,1)} all-to-all(bf16[8,32,512]{2,1,0:T(8,128)(2,1)S(1)} %broadcast_in_dim.11), channel_id=1, replica_groups=mesh['y'=4,'xl'=2,'z'=8,'xh'=2,'core'=2] {'y','xl'}, dimensions={0} | all-to-all | bytes 524288 | tf_op jit(solution)/shard_map/all_to_all | solution.py:39
  20.0 0.0 all-gather.3.cloned.1.call-update
  20.0 0.7 convert_bitcast_fusion
  20.7 0.7 add_convert_fusion.1
  21.5 23.1 %all_to_all.21 = bf16[8,40,512]{2,1,0:T(8,128)(2,1)S(1)} all-to-all(bf16[8,40,512]{2,1,0:T(8,128)(2,1)S(1)} %broadcast_in_dim.8), channel_id=1, replica_groups=mesh['y'=4,'xl'=2,'z'=8,'xh'=2,'core'=2] {'z'}, dimensions={0} | all-to-all | bytes 655360 | tf_op jit(solution)/shard_map/all_to_all | solution.py:39
  44.6 1.4 collective-permute-start
  46.0 2.3 %collective-permute-start.3 = (bf16[8,32,512]{2,1,0:T(8,128)(2,1)S(1)}, bf16[8,32,512]{2,1,0:T(8,128)(2,1)S(1)}, u32[]{:S(2)}, u32[]{:S(2)}) collective-permute-start(bf16[8,32,512]{2,1,0:T(8,128)(2,1)S(1)} %slice.56.a0), channel_id=1, source_target_pairs={{0,192},{64,0},{128,64},{192,128},{1,193},{65,1},{129,65},{193,129... | collective-permute-start | bytes 786440 | tf_op jit(solution)/shard_map/ppermute | solution.py:34
  48.3 3.1 %collective-permute-done.b0 = bf16[8,32,512]{2,1,0:T(8,128)(2,1)S(1)} collective-permute-done((bf16[8,32,512]{2,1,0:T(8,128)(2,1)S(1)}, bf16[8,32,512]{2,1,0:T(8,128)(2,1)S(1)}, u32[]{:S(2)}, u32[]{:S(2)}) %collective-permute-start) | collective-permute-done | bytes 262176 | tf_op jit(solution)/shard_map/ppermute | solution.py:34
  51.4 0.7 broadcast_in_dim.9
  52.1 4.5 %all-to-all-start.1 = ((bf16[8,8,512]{2,1,0:T(8,128)(2,1)}), bf16[8,8,512]{2,1,0:T(8,128)(2,1)S(1)}, u32[]{:S(2)}, u32[]{:S(2)}) async-start(bf16[8,8,512]{2,1,0:T(8,128)(2,1)} %broadcast_in_dim.9), calls=%async_computation.1 | async-start | bytes 131072 | tf_op jit(solution)/shard_map/all_to_all | solution.py:39
  56.6 2.7 %collective-permute-start.6 = (bf16[8,32,512]{2,1,0:T(8,128)(2,1)S(1)}, bf16[8,32,512]{2,1,0:T(8,128)(2,1)S(1)}, u32[]{:S(2)}, u32[]{:S(2)}) collective-permute-start(bf16[8,32,512]{2,1,0:T(8,128)(2,1)S(1)} %collective-permute-done.b0), channel_id=1, source_target_pairs={{0,192},{64,0},{128,64},{192,128},{1,193},{65,1},{129,65},{193,129... | collective-permute-start | bytes 786440 | tf_op jit(solution)/shard_map/ppermute | solution.py:34
  59.3 0.0 collective-permute-start.4
  59.3 0.6 collective-permute-start.5
  60.0 0.7 pad_add_fusion.me
  60.6 1.1 copy.16.pattern
  61.7 1.1 copy.15.scale
  62.8 0.1 reshape.66
  62.9 0.1 copy.14
  63.1 2.7 %collective-permute-done.5.b2 = bf16[8,32,512]{2,1,0:T(8,128)(2,1)S(1)} collective-permute-done((bf16[8,32,512]{2,1,0:T(8,128)(2,1)S(1)}, bf16[8,32,512]{2,1,0:T(8,128)(2,1)S(1)}, u32[]{:S(2)}, u32[]{:S(2)}) %collective-permute-start.5) | collective-permute-done | bytes 262176 | tf_op jit(solution)/shard_map/ppermute | solution.py:34
  65.8 1.1 collective-permute-done.4.b1
  67.0 0.7 copy-done.6
  67.6 11.8 %scores.1 = (f32[512,1024]{1,0:T(8,128)}, f32[16,128]{1,0:T(8,128)}) custom-call(s32[2]{0:T(128)} %pad_add_fusion.me, bf16[1024,4096]{1,0:T(8,128)(2,1)} %images.3, f32[1024,1]{1,0:T(8,128)} %copy.15.scale, s32[1024,2]{1,0:T(8,128)} %copy.16.pattern, bf16[8,8,32,512]{3,2,1,0:T(8,128)(2,1)} %bitcast.17, bf16[8,32,512]{2,1,0:T(8,128)(2,1)} %copy-done, ...), custom_call_target="tpu_custom_call" | custom-call | tf_op jit(solution)/shard_map/scores/pallas_call | solution.py:103
  79.5 0.1 collective-permute-start.9
  79.6 2.1 %collective-permute-start.8 = (f32[16,128]{1,0:T(8,128)}, f32[16,128]{1,0:T(8,128)S(1)}, u32[]{:S(2)}, u32[]{:S(2)}) collective-permute-start(f32[16,128]{1,0:T(8,128)} %get-tuple-element.9.s0), channel_id=1, source_target_pairs={{0,2},{1,3},{2,0},{3,1},{4,6},{5,7},{6,4},{7,5},{8,10},{9,11},{10,... | collective-permute-start | bytes 24584 | tf_op jit(solution)/shard_map/ppermute | solution.py:34
  81.7 1.2 collective-permute-start.7
  82.9 0.9 fusion.2.cells
  83.9 0.5 collective-permute-done.9.s3
  84.4 0.7 collective-permute-done.8.s2
  85.1 0.6 copy-done.11
  85.6 0.0 copy-done.12
  85.7 28.2 %bricks.1 = (f32[512,512]{1,0:T(8,128)}, f32[512,512]{1,0:T(8,128)}, f32[8,128]{1,0:T(8,128)}) custom-call(s32[16384]{0:T(1024)} %fusion.2.cells, f32[8,128]{1,0:T(8,128)} %bitcast.23, f32[16,128]{1,0:T(8,128)} %get-tuple-element.9.s0, f32[16,128]{1,0:T(8,128)} %copy-done.12, f32[16,128]{1,0:T(8,128)} %copy-done.11, f32[16,128]{1,0:T(8,128)} %copy-done.10, ...), custom_call_target="tpu_custom_call" | custom-call | tf_op jit(solution)/shard_map/bricks/pallas_call | solution.py:201
  113.8 0.9 collective-permute-start.10
  114.7 2.5 %collective-permute-done.10 = f32[512,512]{1,0:T(8,128)S(1)} collective-permute-done((f32[512,512]{1,0:T(8,128)}, f32[512,512]{1,0:T(8,128)S(1)}, u32[]{:S(2)}, u32[]{:S(2)}) %collective-permute-start.10) | collective-permute-done | bytes 1048608 | tf_op jit(solution)/shard_map/ppermute | solution.py:34
  117.2 1.4 add_convert_fusion
  118.6 15.2 %all_to_all.22 = bf16[16,32,512]{2,1,0:T(8,128)(2,1)S(1)} all-to-all(bf16[16,32,512]{2,1,0:T(8,128)(2,1)S(1)} %bitcast.16), channel_id=1, replica_groups=mesh['y'=4,'xl'=2,'z'=8,'xh'=2,'core'=2] {'y','xl','xh'}, dimensions={0} | all-to-all | bytes 1048576 | tf_op jit(solution)/shard_map/all_to_all | solution.py:234
  133.8 0.1 convert_reduce_fusion
  133.9 0.3 collective-permute-start.11
  134.2 8.0 %collective-permute-done.11 = f32[16,512]{1,0:T(8,128)S(1)} collective-permute-done((f32[16,512]{1,0:T(8,128)S(1)}, f32[16,512]{1,0:T(8,128)S(1)}, u32[]{:S(2)}, u32[]{:S(2)}) %collective-permute-start.11) | collective-permute-done | bytes 32800 | tf_op jit(solution)/shard_map/ppermute | solution.py:34
  142.1 0.4 collective-permute-start.13
  142.6 2.3 %collective-permute-start.14 = (f32[4,512]{1,0:T(4,128)S(1)}, f32[4,512]{1,0:T(4,128)S(1)}, u32[]{:S(2)}, u32[]{:S(2)}) collective-permute-start(f32[4,512]{1,0:T(4,128)S(1)} %get-tuple-element.17), channel_id=1, source_target_pairs={{0,12},{4,8},{8,4},{12,0},{16,28},{20,24},{24,20},{28,16},{1,13},{... | collective-permute-start | bytes 24584 | tf_op jit(solution)/shard_map/ppermute | solution.py:34
  144.9 0.8 collective-permute-start.12
  145.7 1.1 collective-permute-done.13
  146.8 1.3 collective-permute-done.14
  148.0 0.5 collective-permute-done.12
  148.5 0.6 slice_add_fusion.2
  (44 shorter events, 0.2 us)
Async XLA Ops:
  7.2 53.5 %copy-start.9 = (s32[1024,2]{0,1:T(2,128)S(1)}, s32[1024,2]{0,1:T(2,128)}, u32[]{:S(2)}) copy-start(s32[1024,2]{0,1:T(2,128)} %param.11) | copy-start | bytes 24580
  7.2 54.5 %copy-start.8 = (f32[1024]{0:T(1024)S(1)}, f32[1024]{0:T(1024)}, u32[]{:S(2)}) copy-start(f32[1024]{0:T(1024)} %param.9) | copy-start | bytes 12292
  7.2 59.7 %all-gather.3.cloned.1.call-start = ((), (), s32[]{:S(2)}) async-start(), calls=%async_computation.4 | async-start | bytes 2359296 | tf_op jit(solution)/shard_map/all_gather | solution.py:45
  44.6 22.4 %copy-start = (bf16[8,32,512]{2,1,0:T(8,128)(2,1)}, bf16[8,32,512]{2,1,0:T(8,128)(2,1)S(1)}, u32[]{:S(2)}) copy-start(bf16[8,32,512]{2,1,0:T(8,128)(2,1)S(1)} %slice.56.a0) | copy-start | bytes 786436
  44.6 6.8 %collective-permute-start = (bf16[8,32,512]{2,1,0:T(8,128)(2,1)S(1)}, bf16[8,32,512]{2,1,0:T(8,128)(2,1)S(1)}, u32[]{:S(2)}, u32[]{:S(2)}) collective-permute-start(bf16[8,32,512]{2,1,0:T(8,128)(2,1)S(1)} %slice.56.a0), channel_id=1, source_target_pairs={{0,32},{32,0},{1,33},{33,1},{2,34},{34,2},{3,35},{35,3},{4,36},{36... | collective-permute-start | bytes 786440 | tf_op jit(solution)/shard_map/ppermute | solution.py:34
  46.0 13.4 %collective-permute-start.2 = (bf16[8,32,512]{2,1,0:T(8,128)(2,1)S(1)}, bf16[8,32,512]{2,1,0:T(8,128)(2,1)S(1)}, u32[]{:S(2)}, u32[]{:S(2)}) collective-permute-start(bf16[8,32,512]{2,1,0:T(8,128)(2,1)S(1)} %slice.56.a0), channel_id=1, source_target_pairs={{0,128},{64,192},{128,0},{192,64},{1,129},{65,193},{129,1},{193,65... | collective-permute-start | bytes 786440 | tf_op jit(solution)/shard_map/ppermute | solution.py:34
  46.0 17.1 %collective-permute-start.3 = (bf16[8,32,512]{2,1,0:T(8,128)(2,1)S(1)}, bf16[8,32,512]{2,1,0:T(8,128)(2,1)S(1)}, u32[]{:S(2)}, u32[]{:S(2)}) collective-permute-start(bf16[8,32,512]{2,1,0:T(8,128)(2,1)S(1)} %slice.56.a0), channel_id=1, source_target_pairs={{0,192},{64,0},{128,64},{192,128},{1,193},{65,1},{129,65},{193,129... | collective-permute-start | bytes 786440 | tf_op jit(solution)/shard_map/ppermute | solution.py:34
  48.3 14.8 %collective-permute-start.1 = (bf16[8,32,512]{2,1,0:T(8,128)(2,1)S(1)}, bf16[8,32,512]{2,1,0:T(8,128)(2,1)S(1)}, u32[]{:S(2)}, u32[]{:S(2)}) collective-permute-start(bf16[8,32,512]{2,1,0:T(8,128)(2,1)S(1)} %slice.56.a0), channel_id=1, source_target_pairs={{0,64},{64,128},{128,192},{192,0},{1,65},{65,129},{129,193},{193,1... | collective-permute-start | bytes 786440 | tf_op jit(solution)/shard_map/ppermute | solution.py:34
  51.4 15.5 %copy-start.1 = (bf16[8,32,512]{2,1,0:T(8,128)(2,1)}, bf16[8,32,512]{2,1,0:T(8,128)(2,1)S(1)}, u32[]{:S(2)}) copy-start(bf16[8,32,512]{2,1,0:T(8,128)(2,1)S(1)} %collective-permute-done.b0) | copy-start | bytes 786436
  52.1 10.7 %all-to-all-start.1 = ((bf16[8,8,512]{2,1,0:T(8,128)(2,1)}), bf16[8,8,512]{2,1,0:T(8,128)(2,1)S(1)}, u32[]{:S(2)}, u32[]{:S(2)}) async-start(bf16[8,8,512]{2,1,0:T(8,128)(2,1)} %broadcast_in_dim.9), calls=%async_computation.1 | async-start | bytes 131072 | tf_op jit(solution)/shard_map/all_to_all | solution.py:39
  56.6 9.2 %collective-permute-start.6 = (bf16[8,32,512]{2,1,0:T(8,128)(2,1)S(1)}, bf16[8,32,512]{2,1,0:T(8,128)(2,1)S(1)}, u32[]{:S(2)}, u32[]{:S(2)}) collective-permute-start(bf16[8,32,512]{2,1,0:T(8,128)(2,1)S(1)} %collective-permute-done.b0), channel_id=1, source_target_pairs={{0,192},{64,0},{128,64},{192,128},{1,193},{65,1},{129,65},{193,129... | collective-permute-start | bytes 786440 | tf_op jit(solution)/shard_map/ppermute | solution.py:34
  59.3 7.6 %collective-permute-start.4 = (bf16[8,32,512]{2,1,0:T(8,128)(2,1)S(1)}, bf16[8,32,512]{2,1,0:T(8,128)(2,1)S(1)}, u32[]{:S(2)}, u32[]{:S(2)}) collective-permute-start(bf16[8,32,512]{2,1,0:T(8,128)(2,1)S(1)} %collective-permute-done.b0), channel_id=1, source_target_pairs={{0,64},{64,128},{128,192},{192,0},{1,65},{65,129},{129,193},{193,1... | collective-permute-start | bytes 786440 | tf_op jit(solution)/shard_map/ppermute | solution.py:34
  59.3 7.6 %copy-start.2 = (bf16[8,32,512]{2,1,0:T(8,128)(2,1)}, bf16[8,32,512]{2,1,0:T(8,128)(2,1)S(1)}, u32[]{:S(2)}) copy-start(bf16[8,32,512]{2,1,0:T(8,128)(2,1)S(1)} %collective-permute-done.2.a2) | copy-start | bytes 786436
  59.3 6.5 %collective-permute-start.5 = (bf16[8,32,512]{2,1,0:T(8,128)(2,1)S(1)}, bf16[8,32,512]{2,1,0:T(8,128)(2,1)S(1)}, u32[]{:S(2)}, u32[]{:S(2)}) collective-permute-start(bf16[8,32,512]{2,1,0:T(8,128)(2,1)S(1)} %collective-permute-done.2.a2), channel_id=1, source_target_pairs={{0,32},{32,0},{1,33},{33,1},{2,34},{34,2},{3,35},{35,3},{4,36},{36... | collective-permute-start | bytes 786440 | tf_op jit(solution)/shard_map/ppermute | solution.py:34
  63.1 3.9 %copy-start.3 = (bf16[8,32,512]{2,1,0:T(8,128)(2,1)}, bf16[8,32,512]{2,1,0:T(8,128)(2,1)S(1)}, u32[]{:S(2)}) copy-start(bf16[8,32,512]{2,1,0:T(8,128)(2,1)S(1)} %collective-permute-done.3.a3) | copy-start | bytes 786436
  63.1 3.9 %copy-start.4 = (bf16[8,32,512]{2,1,0:T(8,128)(2,1)}, bf16[8,32,512]{2,1,0:T(8,128)(2,1)S(1)}, u32[]{:S(2)}) copy-start(bf16[8,32,512]{2,1,0:T(8,128)(2,1)S(1)} %collective-permute-done.1.a1) | copy-start | bytes 786436
  65.8 1.2 copy-start.7
  65.8 1.2 copy-start.5
  66.9 0.7 copy-start.6
  79.5 4.9 %collective-permute-start.9 = (f32[16,128]{1,0:T(8,128)}, f32[16,128]{1,0:T(8,128)S(1)}, u32[]{:S(2)}, u32[]{:S(2)}) collective-permute-start(f32[16,128]{1,0:T(8,128)} %get-tuple-element.9.s0), channel_id=1, source_target_pairs={{0,3},{1,2},{2,1},{3,0},{4,7},{5,6},{6,5},{7,4},{8,11},{9,10},{10,... | collective-permute-start | bytes 24584 | tf_op jit(solution)/shard_map/ppermute | solution.py:34
  79.6 5.5 %collective-permute-start.8 = (f32[16,128]{1,0:T(8,128)}, f32[16,128]{1,0:T(8,128)S(1)}, u32[]{:S(2)}, u32[]{:S(2)}) collective-permute-start(f32[16,128]{1,0:T(8,128)} %get-tuple-element.9.s0), channel_id=1, source_target_pairs={{0,2},{1,3},{2,0},{3,1},{4,6},{5,7},{6,4},{7,5},{8,10},{9,11},{10,... | collective-permute-start | bytes 24584 | tf_op jit(solution)/shard_map/ppermute | solution.py:34
  81.7 3.3 %collective-permute-start.7 = (f32[16,128]{1,0:T(8,128)}, f32[16,128]{1,0:T(8,128)S(1)}, u32[]{:S(2)}, u32[]{:S(2)}) collective-permute-start(f32[16,128]{1,0:T(8,128)} %get-tuple-element.9.s0), channel_id=1, source_target_pairs={{0,1},{1,0},{2,3},{3,2},{4,5},{5,4},{6,7},{7,6},{8,9},{9,8},{10,11... | collective-permute-start | bytes 24584 | tf_op jit(solution)/shard_map/ppermute | solution.py:34
  84.4 0.7 copy-start.10
  85.0 0.6 copy-start.11
  85.0 0.6 copy-start.12
  113.8 3.4 %collective-permute-start.10 = (f32[512,512]{1,0:T(8,128)}, f32[512,512]{1,0:T(8,128)S(1)}, u32[]{:S(2)}, u32[]{:S(2)}) collective-permute-start(f32[512,512]{1,0:T(8,128)} %get-tuple-element.12), channel_id=1, source_target_pairs={{0,1},{1,0},{2,3},{3,2},{4,5},{5,4},{6,7},{7,6},{8,9},{9,8},{10,11... | collective-permute-start | bytes 3145736 | tf_op jit(solution)/shard_map/ppermute | solution.py:34
  133.9 8.2 %collective-permute-start.11 = (f32[16,512]{1,0:T(8,128)S(1)}, f32[16,512]{1,0:T(8,128)S(1)}, u32[]{:S(2)}, u32[]{:S(2)}) collective-permute-start(f32[16,512]{1,0:T(8,128)S(1)} %slice.61), channel_id=1, source_target_pairs={{0,16},{4,20},{8,24},{12,28},{16,0},{20,4},{24,8},{28,12},{1,17},{... | collective-permute-start | bytes 98312 | tf_op jit(solution)/shard_map/ppermute | solution.py:34
  142.1 4.6 %collective-permute-start.13 = (f32[4,512]{1,0:T(4,128)S(1)}, f32[4,512]{1,0:T(4,128)S(1)}, u32[]{:S(2)}, u32[]{:S(2)}) collective-permute-start(f32[4,512]{1,0:T(4,128)S(1)} %get-tuple-element.16), channel_id=1, source_target_pairs={{0,8},{4,12},{8,0},{12,4},{16,24},{20,28},{24,16},{28,20},{1,9},{5... | collective-permute-start | bytes 24584 | tf_op jit(solution)/shard_map/ppermute | solution.py:34
  142.6 5.4 %collective-permute-start.14 = (f32[4,512]{1,0:T(4,128)S(1)}, f32[4,512]{1,0:T(4,128)S(1)}, u32[]{:S(2)}, u32[]{:S(2)}) collective-permute-start(f32[4,512]{1,0:T(4,128)S(1)} %get-tuple-element.17), channel_id=1, source_target_pairs={{0,12},{4,8},{8,4},{12,0},{16,28},{20,24},{24,20},{28,16},{1,13},{... | collective-permute-start | bytes 24584 | tf_op jit(solution)/shard_map/ppermute | solution.py:34
  144.9 3.7 %collective-permute-start.12 = (f32[4,512]{1,0:T(4,128)S(1)}, f32[4,512]{1,0:T(4,128)S(1)}, u32[]{:S(2)}, u32[]{:S(2)}) collective-permute-start(f32[4,512]{1,0:T(4,128)S(1)} %get-tuple-element.18), channel_id=1, source_target_pairs={{0,4},{4,0},{8,12},{12,8},{16,20},{20,16},{24,28},{28,24},{1,5},{5... | collective-permute-start | bytes 24584 | tf_op jit(solution)/shard_map/ppermute | solution.py:34
Sparse Core Ops, SparseCore 0:
  20.1 44.4 all-gather.2

commit v7 on v6

--- a/solution.py
+++ b/solution.py
@@ -61,57 +61,88 @@
     )
 
 
+DEEP = 1024
+
+
 def scores_kernel(
-    cut, me, images, scale, pattern, by_z, a0, a1, a2, a3, b0, b1, b2, b3, expo, stats, refs, sems
+    cut, me, images, scale, pattern, by_z, a0, a1, a2, a3, b0, b1, b2, b3,
+    expo, stats, refs, total, sems,
 ):
     step = pl.program_id(0)
-    rows = images.shape[0]
+    each = DEEP // (8 * SHARE)
+
+    def by_y(i, part):
+        y, xl = (me[0] + 4 - i % 4) % 4, (me[1] + i // 4) % 2
+        there = refs.at[y * 2 + xl, :, pl.ds(cut, SHARE - cut)]
+        return pltpu.make_async_copy(part, there, sems.at[8 + i])
+
+    def of_z(q):
+        return pltpu.make_async_copy(
+            by_z.at[:, q], refs.at[q, :, pl.ds(0, cut)], sems.at[q]
+        )
 
     @pl.when(step == 0)
     def _():
-        copies = [(by_z.at[z], refs.at[:, z, pl.ds(0, cut)]) for z in range(8)]
-        for i, part in enumerate((a0, a1, a2, a3, b0, b1, b2, b3)):
-            y, xl = (me[0] + 4 - i % 4) % 4, (me[1] + i // 4) % 2
-            copies.append((part, refs.at[y * 2 + xl, :, pl.ds(cut, SHARE - cut)]))
-        for i, (a, b) in enumerate(copies):
-            pltpu.make_async_copy(a, b, sems.at[i]).start()
-        for i, (a, b) in enumerate(copies):
-            pltpu.make_async_copy(a, b, sems.at[i]).wait()
-
-    total = jnp.dot(
-        images[...], refs[...].reshape(VALUES, REFS), preferred_element_type=F32
+        copies = [by_y(i, p) for i, p in enumerate((a0, a1, a2, a3, b0, b1, b2, b3))]
+        for c in copies:
+            c.start()
+        for q in range(8):
+            of_z(q).start()
+        for c in copies:
+            c.wait()
+
+    for k in range(each):
+        of_z(step * each + k).wait()
+    part = jnp.dot(
+        images[...],
+        refs[pl.ds(step * each, each)].reshape(DEEP, REFS),
+        preferred_element_type=F32,
     )
-    scores = total * scale[...] * (1.0 / math.sqrt(VALUES))
-    group = lax.broadcasted_iota(I32, (rows, REFS), 1) // (REFS // 2)
-    flags = pattern[...]
-    active = jnp.where(group == 0, flags[:, 0:1], flags[:, 1:2]) > 0
-    masked = jnp.where(active, scores, -1e30)
-    peak = jnp.max(masked, axis=1, keepdims=True)
-    value = jnp.where(active, jnp.exp(masked - peak), 0.0)
-    mass = jnp.sum(value, axis=1, keepdims=True)
-    expo[...] = value.T
-    for j in range(rows // LANES):
-        part = slice(j * LANES, (j + 1) * LANES)
-        at = step * (rows // LANES) + j
-        for k, column in enumerate((peak, mass)):
-            stats[pl.ds(k * 8 + at, 1), :] = jnp.sum(
-                jnp.where(eye(), column[part], 0.0), axis=0, keepdims=True
-            )
-
-
-def scores_of(me, images, scale, pattern, parts, cut, rows=256):
+
+    @pl.when(step == 0)
+    def _():
+        total[...] = part
+
+    @pl.when(step > 0)
+    def _():
+        total[...] = total[...] + part
+
+    @pl.when(step == pl.num_programs(0) - 1)
+    def _():
+        rows = 256
+        group = lax.broadcasted_iota(I32, (rows, REFS), 1) // (REFS // 2)
+        for r in range(0, IMAGES, rows):
+            here = slice(r, r + rows)
+            scores = total[here, :] * scale[here, :] * (1.0 / math.sqrt(VALUES))
+            flags = pattern[here, :]
+            active = jnp.where(group == 0, flags[:, 0:1], flags[:, 1:2]) > 0
+            masked = jnp.where(active, scores, -1e30)
+            peak = jnp.max(masked, axis=1, keepdims=True)
+            value = jnp.where(active, jnp.exp(masked - peak), 0.0)
+            mass = jnp.sum(value, axis=1, keepdims=True)
+            expo[:, here] = value.T
+            for j in range(rows // LANES):
+                cut_rows = slice(j * LANES, (j + 1) * LANES)
+                at = r // LANES + j
+                for k, column in enumerate((peak, mass)):
+                    stats[k * 8 + at : k * 8 + at + 1, :] = jnp.sum(
+                        jnp.where(eye(), column[cut_rows], 0.0), axis=0, keepdims=True
+                    )
+
+
+def scores_of(me, images, scale, pattern, parts, cut):
     return pl.pallas_call(
         functools.partial(scores_kernel, cut),
-        grid=(IMAGES // rows,),
+        grid=(VALUES // DEEP,),
         in_specs=[
             pl.BlockSpec(memory_space=pltpu.SMEM),
-            pl.BlockSpec((rows, VALUES), lambda i: (i, 0)),
-            pl.BlockSpec((rows, 1), lambda i: (i, 0)),
-            pl.BlockSpec((rows, 2), lambda i: (i, 0)),
+            pl.BlockSpec((IMAGES, DEEP), lambda i: (0, i)),
+            pl.BlockSpec((IMAGES, 1), lambda i: (0, 0)),
+            pl.BlockSpec((IMAGES, 2), lambda i: (0, 0)),
         ]
         + [pl.BlockSpec(memory_space=pl.ANY)] * len(parts),
         out_specs=[
-            pl.BlockSpec((REFS, rows), lambda i: (0, i)),
+            pl.BlockSpec((REFS, IMAGES), lambda i: (0, 0)),
             pl.BlockSpec((16, LANES), lambda i: (0, 0)),
         ],
         out_shape=[
@@ -120,6 +151,7 @@
         ],
         scratch_shapes=[
             pltpu.VMEM((8, 8, SHARE, REFS), BF16),
+            pltpu.VMEM((IMAGES, REFS), F32),
             pltpu.SemaphoreType.DMA((16,)),
         ],
         compiler_params=pltpu.CompilerParams(vmem_limit_bytes=VMEM),
@@ -127,7 +159,7 @@
     )(me, images, scale, pattern, *parts)
 
 
-UNROLL = 64
+UNROLL = 128
 SUMS = 8
 WIDE = 1024
 

time: 156 us -> 157 us (level)
  no operation moved by 1% of the time
where the time goes in v7:
time: 157 us
  blocking collectives  50.2 us (32%)
  Pallas kernels  40.6 us (26%)
  waiting for transfers between devices  21.3 us (14%)
  starting transfers between devices  19.8 us (13%)
  between operations  14.3 us (9%)
  local copies, waits for them, and re-layouts  5.2 us (3%)
  other arithmetic  5.09 us (3%)
    all_to_all x2, blocking collectives, spread(): return lax.all_to_all(jnp.broadcast_to(x[None], (n, *x.shape)), axes, 0, 0)  35 us
    pallas_call x1, Pallas kernels, bricks_of(): pl.pallas_call(bricks_kernel, grid=(VALUES // WIDE,), in_specs=[pl.BlockS...  27.5 us
    ppermute x15, waiting for transfers between devices, moved(): return lax.ppermute(x, axes, pairs)  21.3 us
    ppermute x15, starting transfers between devices, moved(): return lax.ppermute(x, axes, pairs)  15.2 us
    all_to_all x1, blocking collectives, brick_share(): x = jnp.sum(lax.all_to_all(x, ('y', 'xl', 'xh'), 0, 0).astype(F32), axis=0)  15.2 us
    pallas_call x1, Pallas kernels, scores_of(): pl.pallas_call(functools.partial(scores_kernel, cut), grid=(VALUES // DEE...  13.1 us
    all_to_all x1, starting transfers between devices, spread(): return lax.all_to_all(jnp.broadcast_to(x[None], (n, *x.shape)), axes, 0, 0)  4.55 us
  transfers between devices with their start and end apart: 17, of which 10 were waited for; matrix products, arithmetic and copies ran while one was open for 4% of the time, Pallas kernels for 0%

profile of v7, /device:TPU:2, one launch (start us, length us, event | category | flops | bytes accessed | tf_op | source)
XLA Modules:
  0.0 156.5 jit_solution(9217682225083201586)
XLA Ops:
  7.2 0.0 copy-start.8
  7.2 0.0 all-gather.3.cloned.1.call-start
  7.2 0.8 fusion.35
  8.0 11.9 %all_to_all.20 = bf16[8,32,512]{2,1,0:T(8,128)(2,1)} all-to-all(bf16[8,32,512]{2,1,0:T(8,128)(2,1)S(1)} %broadcast_in_dim.11), channel_id=1, replica_groups=mesh['y'=4,'xl'=2,'z'=8,'xh'=2,'core'=2] {'y','xl'}, dimensions={0} | all-to-all | bytes 524288 | tf_op jit(solution)/shard_map/all_to_all | solution.py:39
  20.0 0.0 all-gather.3.cloned.1.call-update
  20.0 0.7 convert_bitcast_fusion
  20.7 0.7 add_convert_fusion.1
  21.5 23.1 %all_to_all.21 = bf16[8,40,512]{2,1,0:T(8,128)(2,1)S(1)} all-to-all(bf16[8,40,512]{2,1,0:T(8,128)(2,1)S(1)} %broadcast_in_dim.8), channel_id=1, replica_groups=mesh['y'=4,'xl'=2,'z'=8,'xh'=2,'core'=2] {'z'}, dimensions={0} | all-to-all | bytes 655360 | tf_op jit(solution)/shard_map/all_to_all | solution.py:39
  44.6 1.4 collective-permute-start
  46.0 0.0 collective-permute-start.2
  46.0 2.3 %collective-permute-start.3 = (bf16[8,32,512]{2,1,0:T(8,128)(2,1)S(1)}, bf16[8,32,512]{2,1,0:T(8,128)(2,1)S(1)}, u32[]{:S(2)}, u32[]{:S(2)}) collective-permute-start(bf16[8,32,512]{2,1,0:T(8,128)(2,1)S(1)} %slice.56.a0), channel_id=1, source_target_pairs={{0,192},{64,0},{128,64},{192,128},{1,193},{65,1},{129,65},{193,129... | collective-permute-start | bytes 786440 | tf_op jit(solution)/shard_map/ppermute | solution.py:34
  48.3 3.1 %collective-permute-done.b0 = bf16[8,32,512]{2,1,0:T(8,128)(2,1)S(1)} collective-permute-done((bf16[8,32,512]{2,1,0:T(8,128)(2,1)S(1)}, bf16[8,32,512]{2,1,0:T(8,128)(2,1)S(1)}, u32[]{:S(2)}, u32[]{:S(2)}) %collective-permute-start) | collective-permute-done | bytes 262176 | tf_op jit(solution)/shard_map/ppermute | solution.py:34
  51.4 0.7 broadcast_in_dim.9
  52.1 4.5 %all-to-all-start.1 = ((bf16[8,8,512]{2,1,0:T(8,128)(2,1)}), bf16[8,8,512]{2,1,0:T(8,128)(2,1)S(1)}, u32[]{:S(2)}, u32[]{:S(2)}) async-start(bf16[8,8,512]{2,1,0:T(8,128)(2,1)} %broadcast_in_dim.9), calls=%async_computation.1 | async-start | bytes 131072 | tf_op jit(solution)/shard_map/all_to_all | solution.py:39
  56.6 2.7 %collective-permute-start.6 = (bf16[8,32,512]{2,1,0:T(8,128)(2,1)S(1)}, bf16[8,32,512]{2,1,0:T(8,128)(2,1)S(1)}, u32[]{:S(2)}, u32[]{:S(2)}) collective-permute-start(bf16[8,32,512]{2,1,0:T(8,128)(2,1)S(1)} %collective-permute-done.b0), channel_id=1, source_target_pairs={{0,192},{64,0},{128,64},{192,128},{1,193},{65,1},{129,65},{193,129... | collective-permute-start | bytes 786440 | tf_op jit(solution)/shard_map/ppermute | solution.py:34
  59.3 0.6 collective-permute-start.5
  60.0 0.7 pad_add_fusion.me
  60.6 1.1 copy.16.pattern
  61.7 1.1 copy.15.scale
  62.8 0.1 reshape.66
  62.9 0.1 copy.14
  63.1 2.7 %collective-permute-done.5.b2 = bf16[8,32,512]{2,1,0:T(8,128)(2,1)S(1)} collective-permute-done((bf16[8,32,512]{2,1,0:T(8,128)(2,1)S(1)}, bf16[8,32,512]{2,1,0:T(8,128)(2,1)S(1)}, u32[]{:S(2)}, u32[]{:S(2)}) %collective-permute-start.5) | collective-permute-done | bytes 262176 | tf_op jit(solution)/shard_map/ppermute | solution.py:34
  65.8 1.1 collective-permute-done.4.b1
  67.0 0.7 copy-done.6
  67.6 13.1 %scores.1 = (f32[512,1024]{1,0:T(8,128)}, f32[16,128]{1,0:T(8,128)}) custom-call(s32[2]{0:T(128)} %pad_add_fusion.me, bf16[1024,4096]{1,0:T(8,128)(2,1)} %images.3, f32[1024,1]{1,0:T(8,128)} %copy.15.scale, s32[1024,2]{1,0:T(8,128)} %copy.16.pattern, bf16[8,8,32,512]{3,2,1,0:T(8,128)(2,1)} %bitcast.17, bf16[8,32,512]{2,1,0:T(8,128)(2,1)} %copy-done, ...), custom_call_target="tpu_custom_call" | custom-call | tf_op jit(solution)/shard_map/scores/pallas_call | solution.py:134
  80.7 0.1 collective-permute-start.9
  80.8 2.1 %collective-permute-start.8 = (f32[16,128]{1,0:T(8,128)}, f32[16,128]{1,0:T(8,128)S(1)}, u32[]{:S(2)}, u32[]{:S(2)}) collective-permute-start(f32[16,128]{1,0:T(8,128)} %get-tuple-element.9.s0), channel_id=1, source_target_pairs={{0,2},{1,3},{2,0},{3,1},{4,6},{5,7},{6,4},{7,5},{8,10},{9,11},{10,... | collective-permute-start | bytes 24584 | tf_op jit(solution)/shard_map/ppermute | solution.py:34
  82.9 1.2 collective-permute-start.7
  84.2 0.9 fusion.2.cells
  85.1 0.5 collective-permute-done.9.s3
  85.6 0.7 collective-permute-done.8.s2
  86.3 0.6 copy-done.11
  86.9 0.0 copy-done.12
  86.9 27.5 %bricks.1 = (f32[512,512]{1,0:T(8,128)}, f32[512,512]{1,0:T(8,128)}, f32[8,128]{1,0:T(8,128)}) custom-call(s32[16384]{0:T(1024)} %fusion.2.cells, f32[8,128]{1,0:T(8,128)} %bitcast.23, f32[16,128]{1,0:T(8,128)} %get-tuple-element.9.s0, f32[16,128]{1,0:T(8,128)} %copy-done.12, f32[16,128]{1,0:T(8,128)} %copy-done.11, f32[16,128]{1,0:T(8,128)} %copy-done.10, ...), custom_call_target="tpu_custom_call" | custom-call | tf_op jit(solution)/shard_map/bricks/pallas_call | solution.py:233
  114.4 0.9 collective-permute-start.10
  115.3 2.5 %collective-permute-done.10 = f32[512,512]{1,0:T(8,128)S(1)} collective-permute-done((f32[512,512]{1,0:T(8,128)}, f32[512,512]{1,0:T(8,128)S(1)}, u32[]{:S(2)}, u32[]{:S(2)}) %collective-permute-start.10) | collective-permute-done | bytes 1048608 | tf_op jit(solution)/shard_map/ppermute | solution.py:34
  117.8 1.4 add_convert_fusion
  119.2 15.2 %all_to_all.22 = bf16[16,32,512]{2,1,0:T(8,128)(2,1)S(1)} all-to-all(bf16[16,32,512]{2,1,0:T(8,128)(2,1)S(1)} %bitcast.16), channel_id=1, replica_groups=mesh['y'=4,'xl'=2,'z'=8,'xh'=2,'core'=2] {'y','xl','xh'}, dimensions={0} | all-to-all | bytes 1048576 | tf_op jit(solution)/shard_map/all_to_all | solution.py:266
  134.3 0.1 convert_reduce_fusion
  134.4 0.3 collective-permute-start.11
  134.7 8.0 %collective-permute-done.11 = f32[16,512]{1,0:T(8,128)S(1)} collective-permute-done((f32[16,512]{1,0:T(8,128)S(1)}, f32[16,512]{1,0:T(8,128)S(1)}, u32[]{:S(2)}, u32[]{:S(2)}) %collective-permute-start.11) | collective-permute-done | bytes 32800 | tf_op jit(solution)/shard_map/ppermute | solution.py:34
  142.7 0.5 collective-permute-start.13
  143.1 2.3 %collective-permute-start.14 = (f32[4,512]{1,0:T(4,128)S(1)}, f32[4,512]{1,0:T(4,128)S(1)}, u32[]{:S(2)}, u32[]{:S(2)}) collective-permute-start(f32[4,512]{1,0:T(4,128)S(1)} %get-tuple-element.17), channel_id=1, source_target_pairs={{0,12},{4,8},{8,4},{12,0},{16,28},{20,24},{24,20},{28,16},{1,13},{... | collective-permute-start | bytes 24584 | tf_op jit(solution)/shard_map/ppermute | solution.py:34
  145.4 0.8 collective-permute-start.12
  146.3 1.1 collective-permute-done.13
  147.3 1.3 collective-permute-done.14
  148.6 0.5 collective-permute-done.12
  149.1 0.6 slice_add_fusion.2
  (44 shorter events, 0.2 us)
Async XLA Ops:
  7.2 53.5 %copy-start.9 = (s32[1024,2]{0,1:T(2,128)S(1)}, s32[1024,2]{0,1:T(2,128)}, u32[]{:S(2)}) copy-start(s32[1024,2]{0,1:T(2,128)} %param.11) | copy-start | bytes 24580
  7.2 54.5 %copy-start.8 = (f32[1024]{0:T(1024)S(1)}, f32[1024]{0:T(1024)}, u32[]{:S(2)}) copy-start(f32[1024]{0:T(1024)} %param.9) | copy-start | bytes 12292
  7.2 59.7 %all-gather.3.cloned.1.call-start = ((), (), s32[]{:S(2)}) async-start(), calls=%async_computation.4 | async-start | bytes 2359296 | tf_op jit(solution)/shard_map/all_gather | solution.py:45
  44.6 22.4 %copy-start = (bf16[8,32,512]{2,1,0:T(8,128)(2,1)}, bf16[8,32,512]{2,1,0:T(8,128)(2,1)S(1)}, u32[]{:S(2)}) copy-start(bf16[8,32,512]{2,1,0:T(8,128)(2,1)S(1)} %slice.56.a0) | copy-start | bytes 786436
  44.6 6.8 %collective-permute-start = (bf16[8,32,512]{2,1,0:T(8,128)(2,1)S(1)}, bf16[8,32,512]{2,1,0:T(8,128)(2,1)S(1)}, u32[]{:S(2)}, u32[]{:S(2)}) collective-permute-start(bf16[8,32,512]{2,1,0:T(8,128)(2,1)S(1)} %slice.56.a0), channel_id=1, source_target_pairs={{0,32},{32,0},{1,33},{33,1},{2,34},{34,2},{3,35},{35,3},{4,36},{36... | collective-permute-start | bytes 786440 | tf_op jit(solution)/shard_map/ppermute | solution.py:34
  46.0 13.4 %collective-permute-start.2 = (bf16[8,32,512]{2,1,0:T(8,128)(2,1)S(1)}, bf16[8,32,512]{2,1,0:T(8,128)(2,1)S(1)}, u32[]{:S(2)}, u32[]{:S(2)}) collective-permute-start(bf16[8,32,512]{2,1,0:T(8,128)(2,1)S(1)} %slice.56.a0), channel_id=1, source_target_pairs={{0,128},{64,192},{128,0},{192,64},{1,129},{65,193},{129,1},{193,65... | collective-permute-start | bytes 786440 | tf_op jit(solution)/shard_map/ppermute | solution.py:34
  46.0 17.1 %collective-permute-start.3 = (bf16[8,32,512]{2,1,0:T(8,128)(2,1)S(1)}, bf16[8,32,512]{2,1,0:T(8,128)(2,1)S(1)}, u32[]{:S(2)}, u32[]{:S(2)}) collective-permute-start(bf16[8,32,512]{2,1,0:T(8,128)(2,1)S(1)} %slice.56.a0), channel_id=1, source_target_pairs={{0,192},{64,0},{128,64},{192,128},{1,193},{65,1},{129,65},{193,129... | collective-permute-start | bytes 786440 | tf_op jit(solution)/shard_map/ppermute | solution.py:34
  48.3 14.8 %collective-permute-start.1 = (bf16[8,32,512]{2,1,0:T(8,128)(2,1)S(1)}, bf16[8,32,512]{2,1,0:T(8,128)(2,1)S(1)}, u32[]{:S(2)}, u32[]{:S(2)}) collective-permute-start(bf16[8,32,512]{2,1,0:T(8,128)(2,1)S(1)} %slice.56.a0), channel_id=1, source_target_pairs={{0,64},{64,128},{128,192},{192,0},{1,65},{65,129},{129,193},{193,1... | collective-permute-start | bytes 786440 | tf_op jit(solution)/shard_map/ppermute | solution.py:34
  51.4 15.5 %copy-start.1 = (bf16[8,32,512]{2,1,0:T(8,128)(2,1)}, bf16[8,32,512]{2,1,0:T(8,128)(2,1)S(1)}, u32[]{:S(2)}) copy-start(bf16[8,32,512]{2,1,0:T(8,128)(2,1)S(1)} %collective-permute-done.b0) | copy-start | bytes 786436
  52.1 10.7 %all-to-all-start.1 = ((bf16[8,8,512]{2,1,0:T(8,128)(2,1)}), bf16[8,8,512]{2,1,0:T(8,128)(2,1)S(1)}, u32[]{:S(2)}, u32[]{:S(2)}) async-start(bf16[8,8,512]{2,1,0:T(8,128)(2,1)} %broadcast_in_dim.9), calls=%async_computation.1 | async-start | bytes 131072 | tf_op jit(solution)/shard_map/all_to_all | solution.py:39
  56.6 9.2 %collective-permute-start.6 = (bf16[8,32,512]{2,1,0:T(8,128)(2,1)S(1)}, bf16[8,32,512]{2,1,0:T(8,128)(2,1)S(1)}, u32[]{:S(2)}, u32[]{:S(2)}) collective-permute-start(bf16[8,32,512]{2,1,0:T(8,128)(2,1)S(1)} %collective-permute-done.b0), channel_id=1, source_target_pairs={{0,192},{64,0},{128,64},{192,128},{1,193},{65,1},{129,65},{193,129... | collective-permute-start | bytes 786440 | tf_op jit(solution)/shard_map/ppermute | solution.py:34
  59.3 7.6 %collective-permute-start.4 = (bf16[8,32,512]{2,1,0:T(8,128)(2,1)S(1)}, bf16[8,32,512]{2,1,0:T(8,128)(2,1)S(1)}, u32[]{:S(2)}, u32[]{:S(2)}) collective-permute-start(bf16[8,32,512]{2,1,0:T(8,128)(2,1)S(1)} %collective-permute-done.b0), channel_id=1, source_target_pairs={{0,64},{64,128},{128,192},{192,0},{1,65},{65,129},{129,193},{193,1... | collective-permute-start | bytes 786440 | tf_op jit(solution)/shard_map/ppermute | solution.py:34
  59.3 7.6 %copy-start.2 = (bf16[8,32,512]{2,1,0:T(8,128)(2,1)}, bf16[8,32,512]{2,1,0:T(8,128)(2,1)S(1)}, u32[]{:S(2)}) copy-start(bf16[8,32,512]{2,1,0:T(8,128)(2,1)S(1)} %collective-permute-done.2.a2) | copy-start | bytes 786436
  59.3 6.5 %collective-permute-start.5 = (bf16[8,32,512]{2,1,0:T(8,128)(2,1)S(1)}, bf16[8,32,512]{2,1,0:T(8,128)(2,1)S(1)}, u32[]{:S(2)}, u32[]{:S(2)}) collective-permute-start(bf16[8,32,512]{2,1,0:T(8,128)(2,1)S(1)} %collective-permute-done.2.a2), channel_id=1, source_target_pairs={{0,32},{32,0},{1,33},{33,1},{2,34},{34,2},{3,35},{35,3},{4,36},{36... | collective-permute-start | bytes 786440 | tf_op jit(solution)/shard_map/ppermute | solution.py:34
  63.1 3.9 %copy-start.3 = (bf16[8,32,512]{2,1,0:T(8,128)(2,1)}, bf16[8,32,512]{2,1,0:T(8,128)(2,1)S(1)}, u32[]{:S(2)}) copy-start(bf16[8,32,512]{2,1,0:T(8,128)(2,1)S(1)} %collective-permute-done.3.a3) | copy-start | bytes 786436
  63.1 3.9 %copy-start.4 = (bf16[8,32,512]{2,1,0:T(8,128)(2,1)}, bf16[8,32,512]{2,1,0:T(8,128)(2,1)S(1)}, u32[]{:S(2)}) copy-start(bf16[8,32,512]{2,1,0:T(8,128)(2,1)S(1)} %collective-permute-done.1.a1) | copy-start | bytes 786436
  65.8 1.2 copy-start.7
  65.8 1.2 copy-start.5
  66.9 0.7 copy-start.6
  80.7 4.9 %collective-permute-start.9 = (f32[16,128]{1,0:T(8,128)}, f32[16,128]{1,0:T(8,128)S(1)}, u32[]{:S(2)}, u32[]{:S(2)}) collective-permute-start(f32[16,128]{1,0:T(8,128)} %get-tuple-element.9.s0), channel_id=1, source_target_pairs={{0,3},{1,2},{2,1},{3,0},{4,7},{5,6},{6,5},{7,4},{8,11},{9,10},{10,... | collective-permute-start | bytes 24584 | tf_op jit(solution)/shard_map/ppermute | solution.py:34
  80.8 5.5 %collective-permute-start.8 = (f32[16,128]{1,0:T(8,128)}, f32[16,128]{1,0:T(8,128)S(1)}, u32[]{:S(2)}, u32[]{:S(2)}) collective-permute-start(f32[16,128]{1,0:T(8,128)} %get-tuple-element.9.s0), channel_id=1, source_target_pairs={{0,2},{1,3},{2,0},{3,1},{4,6},{5,7},{6,4},{7,5},{8,10},{9,11},{10,... | collective-permute-start | bytes 24584 | tf_op jit(solution)/shard_map/ppermute | solution.py:34
  82.9 3.3 %collective-permute-start.7 = (f32[16,128]{1,0:T(8,128)}, f32[16,128]{1,0:T(8,128)S(1)}, u32[]{:S(2)}, u32[]{:S(2)}) collective-permute-start(f32[16,128]{1,0:T(8,128)} %get-tuple-element.9.s0), channel_id=1, source_target_pairs={{0,1},{1,0},{2,3},{3,2},{4,5},{5,4},{6,7},{7,6},{8,9},{9,8},{10,11... | collective-permute-start | bytes 24584 | tf_op jit(solution)/shard_map/ppermute | solution.py:34
  85.6 0.7 copy-start.10
  86.3 0.6 copy-start.11
  86.3 0.6 copy-start.12
  114.4 3.4 %collective-permute-start.10 = (f32[512,512]{1,0:T(8,128)}, f32[512,512]{1,0:T(8,128)S(1)}, u32[]{:S(2)}, u32[]{:S(2)}) collective-permute-start(f32[512,512]{1,0:T(8,128)} %get-tuple-element.12), channel_id=1, source_target_pairs={{0,1},{1,0},{2,3},{3,2},{4,5},{5,4},{6,7},{7,6},{8,9},{9,8},{10,11... | collective-permute-start | bytes 3145736 | tf_op jit(solution)/shard_map/ppermute | solution.py:34
  134.4 8.2 %collective-permute-start.11 = (f32[16,512]{1,0:T(8,128)S(1)}, f32[16,512]{1,0:T(8,128)S(1)}, u32[]{:S(2)}, u32[]{:S(2)}) collective-permute-start(f32[16,512]{1,0:T(8,128)S(1)} %slice.61), channel_id=1, source_target_pairs={{0,16},{4,20},{8,24},{12,28},{16,0},{20,4},{24,8},{28,12},{1,17},{... | collective-permute-start | bytes 98312 | tf_op jit(solution)/shard_map/ppermute | solution.py:34
  142.7 4.6 %collective-permute-start.13 = (f32[4,512]{1,0:T(4,128)S(1)}, f32[4,512]{1,0:T(4,128)S(1)}, u32[]{:S(2)}, u32[]{:S(2)}) collective-permute-start(f32[4,512]{1,0:T(4,128)S(1)} %get-tuple-element.16), channel_id=1, source_target_pairs={{0,8},{4,12},{8,0},{12,4},{16,24},{20,28},{24,16},{28,20},{1,9},{5... | collective-permute-start | bytes 24584 | tf_op jit(solution)/shard_map/ppermute | solution.py:34
  143.1 5.4 %collective-permute-start.14 = (f32[4,512]{1,0:T(4,128)S(1)}, f32[4,512]{1,0:T(4,128)S(1)}, u32[]{:S(2)}, u32[]{:S(2)}) collective-permute-start(f32[4,512]{1,0:T(4,128)S(1)} %get-tuple-element.17), channel_id=1, source_target_pairs={{0,12},{4,8},{8,4},{12,0},{16,28},{20,24},{24,20},{28,16},{1,13},{... | collective-permute-start | bytes 24584 | tf_op jit(solution)/shard_map/ppermute | solution.py:34
  145.4 3.7 %collective-permute-start.12 = (f32[4,512]{1,0:T(4,128)S(1)}, f32[4,512]{1,0:T(4,128)S(1)}, u32[]{:S(2)}, u32[]{:S(2)}) collective-permute-start(f32[4,512]{1,0:T(4,128)S(1)} %get-tuple-element.18), channel_id=1, source_target_pairs={{0,4},{4,0},{8,12},{12,8},{16,20},{20,16},{24,28},{28,24},{1,5},{5... | collective-permute-start | bytes 24584 | tf_op jit(solution)/shard_map/ppermute | solution.py:34
Sparse Core Ops, SparseCore 0:
  20.1 44.4 all-gather.2

commit v8 on v6

--- a/solution.py
+++ b/solution.py
@@ -127,7 +127,7 @@
     )(me, images, scale, pattern, *parts)
 
 
-UNROLL = 64
+UNROLL = 128
 SUMS = 8
 WIDE = 1024
 
@@ -176,10 +176,10 @@
 
     @pl.when(step == pl.num_programs(0) - 1)
     def _():
-        for r in range(0, 1024, 256):
-            total = jnp.zeros((256, weights.shape[2]), F32)
+        for r, out in ((0, keep), (512, send)):
+            total = jnp.zeros((512, weights.shape[2]), F32)
             for p in range(8):
-                part = pl.ds(p * 1024 + r, 256)
+                part = pl.ds(p * 1024 + r, 512)
                 cell = functools.reduce(jnp.add, [c[part, :] for c in sums])
                 high = cell.astype(BF16)
                 low = (cell - high.astype(F32)).astype(BF16)
@@ -189,10 +189,7 @@
                     jnp.concatenate([w, w], axis=0),
                     preferred_element_type=F32,
                 )
-            if r < 512:
-                keep[r : r + 256, :] = total
-            else:
-                send[r - 512 : r - 256, :] = total
+            out[...] = total
 
 
 def bricks_of(cells, scale, stats, expo, images, weights):

time: 156 us -> 156 us (level)
  no operation moved by 1% of the time
where the time goes in v8:
time: 156 us; the launch traced here: 155 us
  blocking collectives  50.2 us (32%)
  Pallas kernels  39.3 us (25%)
  waiting for transfers between devices  21.3 us (14%)
  starting transfers between devices  19.8 us (13%)
  between operations  14.3 us (9%)
  local copies, waits for them, and re-layouts  5.2 us (3%)
  other arithmetic  5.09 us (3%)
    all_to_all x2, blocking collectives, spread(): return lax.all_to_all(jnp.broadcast_to(x[None], (n, *x.shape)), axes, 0, 0)  35 us
    pallas_call x1, Pallas kernels, bricks_of(): pl.pallas_call(bricks_kernel, grid=(VALUES // WIDE,), in_specs=[pl.BlockS...  27.5 us
    ppermute x15, waiting for transfers between devices, moved(): return lax.ppermute(x, axes, pairs)  21.3 us
    ppermute x15, starting transfers between devices, moved(): return lax.ppermute(x, axes, pairs)  15.3 us
    all_to_all x1, blocking collectives, brick_share(): x = jnp.sum(lax.all_to_all(x, ('y', 'xl', 'xh'), 0, 0).astype(F32), axis=0)  15.2 us
    pallas_call x1, Pallas kernels, scores_of(): pl.pallas_call(functools.partial(scores_kernel, cut), grid=(IMAGES // row...  11.8 us
    all_to_all x1, starting transfers between devices, spread(): return lax.all_to_all(jnp.broadcast_to(x[None], (n, *x.shape)), axes, 0, 0)  4.55 us
  transfers between devices with their start and end apart: 17, of which 10 were waited for; matrix products, arithmetic and copies ran while one was open for 4% of the time, Pallas kernels for 0%

profile of v8, /device:TPU:2, one launch (start us, length us, event | category | flops | bytes accessed | tf_op | source)
XLA Modules:
  0.0 155.3 jit_solution(11719730774711434993)
XLA Ops:
  7.2 0.0 copy-start.8
  7.2 0.0 all-gather.3.cloned.1.call-start
  7.2 0.8 fusion.35
  8.0 11.9 %all_to_all.20 = bf16[8,32,512]{2,1,0:T(8,128)(2,1)} all-to-all(bf16[8,32,512]{2,1,0:T(8,128)(2,1)S(1)} %broadcast_in_dim.11), channel_id=1, replica_groups=mesh['y'=4,'xl'=2,'z'=8,'xh'=2,'core'=2] {'y','xl'}, dimensions={0} | all-to-all | bytes 524288 | tf_op jit(solution)/shard_map/all_to_all | solution.py:39
  20.0 0.0 all-gather.3.cloned.1.call-update
  20.0 0.7 convert_bitcast_fusion
  20.7 0.7 add_convert_fusion.1
  21.5 23.1 %all_to_all.21 = bf16[8,40,512]{2,1,0:T(8,128)(2,1)S(1)} all-to-all(bf16[8,40,512]{2,1,0:T(8,128)(2,1)S(1)} %broadcast_in_dim.8), channel_id=1, replica_groups=mesh['y'=4,'xl'=2,'z'=8,'xh'=2,'core'=2] {'z'}, dimensions={0} | all-to-all | bytes 655360 | tf_op jit(solution)/shard_map/all_to_all | solution.py:39
  44.6 1.4 collective-permute-start
  46.0 2.3 %collective-permute-start.3 = (bf16[8,32,512]{2,1,0:T(8,128)(2,1)S(1)}, bf16[8,32,512]{2,1,0:T(8,128)(2,1)S(1)}, u32[]{:S(2)}, u32[]{:S(2)}) collective-permute-start(bf16[8,32,512]{2,1,0:T(8,128)(2,1)S(1)} %slice.56.a0), channel_id=1, source_target_pairs={{0,192},{64,0},{128,64},{192,128},{1,193},{65,1},{129,65},{193,129... | collective-permute-start | bytes 786440 | tf_op jit(solution)/shard_map/ppermute | solution.py:34
  48.3 3.1 %collective-permute-done.b0 = bf16[8,32,512]{2,1,0:T(8,128)(2,1)S(1)} collective-permute-done((bf16[8,32,512]{2,1,0:T(8,128)(2,1)S(1)}, bf16[8,32,512]{2,1,0:T(8,128)(2,1)S(1)}, u32[]{:S(2)}, u32[]{:S(2)}) %collective-permute-start) | collective-permute-done | bytes 262176 | tf_op jit(solution)/shard_map/ppermute | solution.py:34
  51.4 0.7 broadcast_in_dim.9
  52.1 4.5 %all-to-all-start.1 = ((bf16[8,8,512]{2,1,0:T(8,128)(2,1)}), bf16[8,8,512]{2,1,0:T(8,128)(2,1)S(1)}, u32[]{:S(2)}, u32[]{:S(2)}) async-start(bf16[8,8,512]{2,1,0:T(8,128)(2,1)} %broadcast_in_dim.9), calls=%async_computation.1 | async-start | bytes 131072 | tf_op jit(solution)/shard_map/all_to_all | solution.py:39
  56.6 2.7 %collective-permute-start.6 = (bf16[8,32,512]{2,1,0:T(8,128)(2,1)S(1)}, bf16[8,32,512]{2,1,0:T(8,128)(2,1)S(1)}, u32[]{:S(2)}, u32[]{:S(2)}) collective-permute-start(bf16[8,32,512]{2,1,0:T(8,128)(2,1)S(1)} %collective-permute-done.b0), channel_id=1, source_target_pairs={{0,192},{64,0},{128,64},{192,128},{1,193},{65,1},{129,65},{193,129... | collective-permute-start | bytes 786440 | tf_op jit(solution)/shard_map/ppermute | solution.py:34
  59.3 0.0 collective-permute-start.4
  59.3 0.6 collective-permute-start.5
  60.0 0.7 pad_add_fusion.me
  60.6 1.1 copy.16.pattern
  61.7 1.1 copy.15.scale
  62.8 0.1 reshape.66
  62.9 0.1 copy.14
  63.1 2.7 %collective-permute-done.5.b2 = bf16[8,32,512]{2,1,0:T(8,128)(2,1)S(1)} collective-permute-done((bf16[8,32,512]{2,1,0:T(8,128)(2,1)S(1)}, bf16[8,32,512]{2,1,0:T(8,128)(2,1)S(1)}, u32[]{:S(2)}, u32[]{:S(2)}) %collective-permute-start.5) | collective-permute-done | bytes 262176 | tf_op jit(solution)/shard_map/ppermute | solution.py:34
  65.8 1.1 collective-permute-done.4.b1
  67.0 0.7 copy-done.6
  67.6 11.8 %scores.1 = (f32[512,1024]{1,0:T(8,128)}, f32[16,128]{1,0:T(8,128)}) custom-call(s32[2]{0:T(128)} %pad_add_fusion.me, bf16[1024,4096]{1,0:T(8,128)(2,1)} %images.3, f32[1024,1]{1,0:T(8,128)} %copy.15.scale, s32[1024,2]{1,0:T(8,128)} %copy.16.pattern, bf16[8,8,32,512]{3,2,1,0:T(8,128)(2,1)} %bitcast.17, bf16[8,32,512]{2,1,0:T(8,128)(2,1)} %copy-done, ...), custom_call_target="tpu_custom_call" | custom-call | tf_op jit(solution)/shard_map/scores/pallas_call | solution.py:103
  79.5 0.1 collective-permute-start.9
  79.6 2.1 %collective-permute-start.8 = (f32[16,128]{1,0:T(8,128)}, f32[16,128]{1,0:T(8,128)S(1)}, u32[]{:S(2)}, u32[]{:S(2)}) collective-permute-start(f32[16,128]{1,0:T(8,128)} %get-tuple-element.9.s0), channel_id=1, source_target_pairs={{0,2},{1,3},{2,0},{3,1},{4,6},{5,7},{6,4},{7,5},{8,10},{9,11},{10,... | collective-permute-start | bytes 24584 | tf_op jit(solution)/shard_map/ppermute | solution.py:34
  81.7 1.2 collective-permute-start.7
  82.9 0.9 fusion.2.cells
  83.9 0.5 collective-permute-done.9.s3
  84.4 0.7 collective-permute-done.8.s2
  85.1 0.6 copy-done.11
  85.6 0.0 copy-done.12
  85.7 27.5 %bricks.1 = (f32[512,512]{1,0:T(8,128)}, f32[512,512]{1,0:T(8,128)}, f32[8,128]{1,0:T(8,128)}) custom-call(s32[16384]{0:T(1024)} %fusion.2.cells, f32[8,128]{1,0:T(8,128)} %bitcast.23, f32[16,128]{1,0:T(8,128)} %get-tuple-element.9.s0, f32[16,128]{1,0:T(8,128)} %copy-done.12, f32[16,128]{1,0:T(8,128)} %copy-done.11, f32[16,128]{1,0:T(8,128)} %copy-done.10, ...), custom_call_target="tpu_custom_call" | custom-call | tf_op jit(solution)/shard_map/bricks/pallas_call | solution.py:198
  113.2 0.9 collective-permute-start.10
  114.1 2.5 %collective-permute-done.10 = f32[512,512]{1,0:T(8,128)S(1)} collective-permute-done((f32[512,512]{1,0:T(8,128)}, f32[512,512]{1,0:T(8,128)S(1)}, u32[]{:S(2)}, u32[]{:S(2)}) %collective-permute-start.10) | collective-permute-done | bytes 1048608 | tf_op jit(solution)/shard_map/ppermute | solution.py:34
  116.6 1.4 add_convert_fusion
  117.9 15.2 %all_to_all.22 = bf16[16,32,512]{2,1,0:T(8,128)(2,1)S(1)} all-to-all(bf16[16,32,512]{2,1,0:T(8,128)(2,1)S(1)} %bitcast.16), channel_id=1, replica_groups=mesh['y'=4,'xl'=2,'z'=8,'xh'=2,'core'=2] {'y','xl','xh'}, dimensions={0} | all-to-all | bytes 1048576 | tf_op jit(solution)/shard_map/all_to_all | solution.py:231
  133.1 0.1 convert_reduce_fusion
  133.2 0.3 collective-permute-start.11
  133.5 8.0 %collective-permute-done.11 = f32[16,512]{1,0:T(8,128)S(1)} collective-permute-done((f32[16,512]{1,0:T(8,128)S(1)}, f32[16,512]{1,0:T(8,128)S(1)}, u32[]{:S(2)}, u32[]{:S(2)}) %collective-permute-start.11) | collective-permute-done | bytes 32800 | tf_op jit(solution)/shard_map/ppermute | solution.py:34
  141.5 0.5 collective-permute-start.13
  141.9 2.3 %collective-permute-start.14 = (f32[4,512]{1,0:T(4,128)S(1)}, f32[4,512]{1,0:T(4,128)S(1)}, u32[]{:S(2)}, u32[]{:S(2)}) collective-permute-start(f32[4,512]{1,0:T(4,128)S(1)} %get-tuple-element.17), channel_id=1, source_target_pairs={{0,12},{4,8},{8,4},{12,0},{16,28},{20,24},{24,20},{28,16},{1,13},{... | collective-permute-start | bytes 24584 | tf_op jit(solution)/shard_map/ppermute | solution.py:34
  144.2 0.8 collective-permute-start.12
  145.0 1.1 collective-permute-done.13
  146.1 1.3 collective-permute-done.14
  147.4 0.5 collective-permute-done.12
  147.8 0.6 slice_add_fusion.2
  (44 shorter events, 0.2 us)
Async XLA Ops:
  7.2 53.5 %copy-start.9 = (s32[1024,2]{0,1:T(2,128)S(1)}, s32[1024,2]{0,1:T(2,128)}, u32[]{:S(2)}) copy-start(s32[1024,2]{0,1:T(2,128)} %param.11) | copy-start | bytes 24580
  7.2 54.5 %copy-start.8 = (f32[1024]{0:T(1024)S(1)}, f32[1024]{0:T(1024)}, u32[]{:S(2)}) copy-start(f32[1024]{0:T(1024)} %param.9) | copy-start | bytes 12292
  7.2 59.7 %all-gather.3.cloned.1.call-start = ((), (), s32[]{:S(2)}) async-start(), calls=%async_computation.4 | async-start | bytes 2359296 | tf_op jit(solution)/shard_map/all_gather | solution.py:45
  44.6 22.4 %copy-start = (bf16[8,32,512]{2,1,0:T(8,128)(2,1)}, bf16[8,32,512]{2,1,0:T(8,128)(2,1)S(1)}, u32[]{:S(2)}) copy-start(bf16[8,32,512]{2,1,0:T(8,128)(2,1)S(1)} %slice.56.a0) | copy-start | bytes 786436
  44.6 6.8 %collective-permute-start = (bf16[8,32,512]{2,1,0:T(8,128)(2,1)S(1)}, bf16[8,32,512]{2,1,0:T(8,128)(2,1)S(1)}, u32[]{:S(2)}, u32[]{:S(2)}) collective-permute-start(bf16[8,32,512]{2,1,0:T(8,128)(2,1)S(1)} %slice.56.a0), channel_id=1, source_target_pairs={{0,32},{32,0},{1,33},{33,1},{2,34},{34,2},{3,35},{35,3},{4,36},{36... | collective-permute-start | bytes 786440 | tf_op jit(solution)/shard_map/ppermute | solution.py:34
  46.0 13.4 %collective-permute-start.2 = (bf16[8,32,512]{2,1,0:T(8,128)(2,1)S(1)}, bf16[8,32,512]{2,1,0:T(8,128)(2,1)S(1)}, u32[]{:S(2)}, u32[]{:S(2)}) collective-permute-start(bf16[8,32,512]{2,1,0:T(8,128)(2,1)S(1)} %slice.56.a0), channel_id=1, source_target_pairs={{0,128},{64,192},{128,0},{192,64},{1,129},{65,193},{129,1},{193,65... | collective-permute-start | bytes 786440 | tf_op jit(solution)/shard_map/ppermute | solution.py:34
  46.0 17.1 %collective-permute-start.3 = (bf16[8,32,512]{2,1,0:T(8,128)(2,1)S(1)}, bf16[8,32,512]{2,1,0:T(8,128)(2,1)S(1)}, u32[]{:S(2)}, u32[]{:S(2)}) collective-permute-start(bf16[8,32,512]{2,1,0:T(8,128)(2,1)S(1)} %slice.56.a0), channel_id=1, source_target_pairs={{0,192},{64,0},{128,64},{192,128},{1,193},{65,1},{129,65},{193,129... | collective-permute-start | bytes 786440 | tf_op jit(solution)/shard_map/ppermute | solution.py:34
  48.3 14.8 %collective-permute-start.1 = (bf16[8,32,512]{2,1,0:T(8,128)(2,1)S(1)}, bf16[8,32,512]{2,1,0:T(8,128)(2,1)S(1)}, u32[]{:S(2)}, u32[]{:S(2)}) collective-permute-start(bf16[8,32,512]{2,1,0:T(8,128)(2,1)S(1)} %slice.56.a0), channel_id=1, source_target_pairs={{0,64},{64,128},{128,192},{192,0},{1,65},{65,129},{129,193},{193,1... | collective-permute-start | bytes 786440 | tf_op jit(solution)/shard_map/ppermute | solution.py:34
  51.4 15.5 %copy-start.1 = (bf16[8,32,512]{2,1,0:T(8,128)(2,1)}, bf16[8,32,512]{2,1,0:T(8,128)(2,1)S(1)}, u32[]{:S(2)}) copy-start(bf16[8,32,512]{2,1,0:T(8,128)(2,1)S(1)} %collective-permute-done.b0) | copy-start | bytes 786436
  52.1 10.7 %all-to-all-start.1 = ((bf16[8,8,512]{2,1,0:T(8,128)(2,1)}), bf16[8,8,512]{2,1,0:T(8,128)(2,1)S(1)}, u32[]{:S(2)}, u32[]{:S(2)}) async-start(bf16[8,8,512]{2,1,0:T(8,128)(2,1)} %broadcast_in_dim.9), calls=%async_computation.1 | async-start | bytes 131072 | tf_op jit(solution)/shard_map/all_to_all | solution.py:39
  56.6 9.2 %collective-permute-start.6 = (bf16[8,32,512]{2,1,0:T(8,128)(2,1)S(1)}, bf16[8,32,512]{2,1,0:T(8,128)(2,1)S(1)}, u32[]{:S(2)}, u32[]{:S(2)}) collective-permute-start(bf16[8,32,512]{2,1,0:T(8,128)(2,1)S(1)} %collective-permute-done.b0), channel_id=1, source_target_pairs={{0,192},{64,0},{128,64},{192,128},{1,193},{65,1},{129,65},{193,129... | collective-permute-start | bytes 786440 | tf_op jit(solution)/shard_map/ppermute | solution.py:34
  59.3 7.6 %collective-permute-start.4 = (bf16[8,32,512]{2,1,0:T(8,128)(2,1)S(1)}, bf16[8,32,512]{2,1,0:T(8,128)(2,1)S(1)}, u32[]{:S(2)}, u32[]{:S(2)}) collective-permute-start(bf16[8,32,512]{2,1,0:T(8,128)(2,1)S(1)} %collective-permute-done.b0), channel_id=1, source_target_pairs={{0,64},{64,128},{128,192},{192,0},{1,65},{65,129},{129,193},{193,1... | collective-permute-start | bytes 786440 | tf_op jit(solution)/shard_map/ppermute | solution.py:34
  59.3 7.6 %copy-start.2 = (bf16[8,32,512]{2,1,0:T(8,128)(2,1)}, bf16[8,32,512]{2,1,0:T(8,128)(2,1)S(1)}, u32[]{:S(2)}) copy-start(bf16[8,32,512]{2,1,0:T(8,128)(2,1)S(1)} %collective-permute-done.2.a2) | copy-start | bytes 786436
  59.3 6.5 %collective-permute-start.5 = (bf16[8,32,512]{2,1,0:T(8,128)(2,1)S(1)}, bf16[8,32,512]{2,1,0:T(8,128)(2,1)S(1)}, u32[]{:S(2)}, u32[]{:S(2)}) collective-permute-start(bf16[8,32,512]{2,1,0:T(8,128)(2,1)S(1)} %collective-permute-done.2.a2), channel_id=1, source_target_pairs={{0,32},{32,0},{1,33},{33,1},{2,34},{34,2},{3,35},{35,3},{4,36},{36... | collective-permute-start | bytes 786440 | tf_op jit(solution)/shard_map/ppermute | solution.py:34
  63.1 3.9 %copy-start.3 = (bf16[8,32,512]{2,1,0:T(8,128)(2,1)}, bf16[8,32,512]{2,1,0:T(8,128)(2,1)S(1)}, u32[]{:S(2)}) copy-start(bf16[8,32,512]{2,1,0:T(8,128)(2,1)S(1)} %collective-permute-done.3.a3) | copy-start | bytes 786436
  63.1 3.9 %copy-start.4 = (bf16[8,32,512]{2,1,0:T(8,128)(2,1)}, bf16[8,32,512]{2,1,0:T(8,128)(2,1)S(1)}, u32[]{:S(2)}) copy-start(bf16[8,32,512]{2,1,0:T(8,128)(2,1)S(1)} %collective-permute-done.1.a1) | copy-start | bytes 786436
  65.8 1.2 copy-start.7
  65.8 1.2 copy-start.5
  66.9 0.7 copy-start.6
  79.5 4.9 %collective-permute-start.9 = (f32[16,128]{1,0:T(8,128)}, f32[16,128]{1,0:T(8,128)S(1)}, u32[]{:S(2)}, u32[]{:S(2)}) collective-permute-start(f32[16,128]{1,0:T(8,128)} %get-tuple-element.9.s0), channel_id=1, source_target_pairs={{0,3},{1,2},{2,1},{3,0},{4,7},{5,6},{6,5},{7,4},{8,11},{9,10},{10,... | collective-permute-start | bytes 24584 | tf_op jit(solution)/shard_map/ppermute | solution.py:34
  79.6 5.5 %collective-permute-start.8 = (f32[16,128]{1,0:T(8,128)}, f32[16,128]{1,0:T(8,128)S(1)}, u32[]{:S(2)}, u32[]{:S(2)}) collective-permute-start(f32[16,128]{1,0:T(8,128)} %get-tuple-element.9.s0), channel_id=1, source_target_pairs={{0,2},{1,3},{2,0},{3,1},{4,6},{5,7},{6,4},{7,5},{8,10},{9,11},{10,... | collective-permute-start | bytes 24584 | tf_op jit(solution)/shard_map/ppermute | solution.py:34
  81.7 3.3 %collective-permute-start.7 = (f32[16,128]{1,0:T(8,128)}, f32[16,128]{1,0:T(8,128)S(1)}, u32[]{:S(2)}, u32[]{:S(2)}) collective-permute-start(f32[16,128]{1,0:T(8,128)} %get-tuple-element.9.s0), channel_id=1, source_target_pairs={{0,1},{1,0},{2,3},{3,2},{4,5},{5,4},{6,7},{7,6},{8,9},{9,8},{10,11... | collective-permute-start | bytes 24584 | tf_op jit(solution)/shard_map/ppermute | solution.py:34
  84.4 0.7 copy-start.10
  85.0 0.6 copy-start.11
  85.0 0.6 copy-start.12
  113.2 3.4 %collective-permute-start.10 = (f32[512,512]{1,0:T(8,128)}, f32[512,512]{1,0:T(8,128)S(1)}, u32[]{:S(2)}, u32[]{:S(2)}) collective-permute-start(f32[512,512]{1,0:T(8,128)} %get-tuple-element.12), channel_id=1, source_target_pairs={{0,1},{1,0},{2,3},{3,2},{4,5},{5,4},{6,7},{7,6},{8,9},{9,8},{10,11... | collective-permute-start | bytes 3145736 | tf_op jit(solution)/shard_map/ppermute | solution.py:34
  133.2 8.2 %collective-permute-start.11 = (f32[16,512]{1,0:T(8,128)S(1)}, f32[16,512]{1,0:T(8,128)S(1)}, u32[]{:S(2)}, u32[]{:S(2)}) collective-permute-start(f32[16,512]{1,0:T(8,128)S(1)} %slice.61), channel_id=1, source_target_pairs={{0,16},{4,20},{8,24},{12,28},{16,0},{20,4},{24,8},{28,12},{1,17},{... | collective-permute-start | bytes 98312 | tf_op jit(solution)/shard_map/ppermute | solution.py:34
  141.5 4.6 %collective-permute-start.13 = (f32[4,512]{1,0:T(4,128)S(1)}, f32[4,512]{1,0:T(4,128)S(1)}, u32[]{:S(2)}, u32[]{:S(2)}) collective-permute-start(f32[4,512]{1,0:T(4,128)S(1)} %get-tuple-element.16), channel_id=1, source_target_pairs={{0,8},{4,12},{8,0},{12,4},{16,24},{20,28},{24,16},{28,20},{1,9},{5... | collective-permute-start | bytes 24584 | tf_op jit(solution)/shard_map/ppermute | solution.py:34
  141.9 5.4 %collective-permute-start.14 = (f32[4,512]{1,0:T(4,128)S(1)}, f32[4,512]{1,0:T(4,128)S(1)}, u32[]{:S(2)}, u32[]{:S(2)}) collective-permute-start(f32[4,512]{1,0:T(4,128)S(1)} %get-tuple-element.17), channel_id=1, source_target_pairs={{0,12},{4,8},{8,4},{12,0},{16,28},{20,24},{24,20},{28,16},{1,13},{... | collective-permute-start | bytes 24584 | tf_op jit(solution)/shard_map/ppermute | solution.py:34
  144.2 3.7 %collective-permute-start.12 = (f32[4,512]{1,0:T(4,128)S(1)}, f32[4,512]{1,0:T(4,128)S(1)}, u32[]{:S(2)}, u32[]{:S(2)}) collective-permute-start(f32[4,512]{1,0:T(4,128)S(1)} %get-tuple-element.18), channel_id=1, source_target_pairs={{0,4},{4,0},{8,12},{12,8},{16,20},{20,16},{24,28},{28,24},{1,5},{5... | collective-permute-start | bytes 24584 | tf_op jit(solution)/shard_map/ppermute | solution.py:34
Sparse Core Ops, SparseCore 0:
  20.1 44.4 all-gather.2

commit v9 on v8

--- a/solution.py
+++ b/solution.py
@@ -129,7 +129,7 @@
 
 UNROLL = 128
 SUMS = 8
-WIDE = 1024
+WIDE = 2048
 
 
 def bricks_kernel(

time: 156 us -> 156 us (level)
  no operation moved by 1% of the time
where the time goes in v9:
time: 156 us; the launch traced here: 155 us
  blocking collectives  50.2 us (32%)
  Pallas kernels  39.5 us (25%)
  waiting for transfers between devices  21.3 us (14%)
  starting transfers between devices  19.8 us (13%)
  between operations  14.3 us (9%)
  local copies, waits for them, and re-layouts  5.2 us (3%)
  other arithmetic  5.09 us (3%)
    all_to_all x2, blocking collectives, spread(): return lax.all_to_all(jnp.broadcast_to(x[None], (n, *x.shape)), axes, 0, 0)  35 us
    pallas_call x1, Pallas kernels, bricks_of(): pl.pallas_call(bricks_kernel, grid=(VALUES // WIDE,), in_specs=[pl.BlockS...  27.7 us
    ppermute x15, waiting for transfers between devices, moved(): return lax.ppermute(x, axes, pairs)  21.3 us
    ppermute x15, starting transfers between devices, moved(): return lax.ppermute(x, axes, pairs)  15.3 us
    all_to_all x1, blocking collectives, brick_share(): x = jnp.sum(lax.all_to_all(x, ('y', 'xl', 'xh'), 0, 0).astype(F32), axis=0)  15.2 us
    pallas_call x1, Pallas kernels, scores_of(): pl.pallas_call(functools.partial(scores_kernel, cut), grid=(IMAGES // row...  11.8 us
    all_to_all x1, starting transfers between devices, spread(): return lax.all_to_all(jnp.broadcast_to(x[None], (n, *x.shape)), axes, 0, 0)  4.55 us
  transfers between devices with their start and end apart: 17, of which 10 were waited for; matrix products, arithmetic and copies ran while one was open for 4% of the time, Pallas kernels for 0%

profile of v9, /device:TPU:2, one launch (start us, length us, event | category | flops | bytes accessed | tf_op | source)
XLA Modules:
  0.0 155.4 jit_solution(3067690234719704802)
XLA Ops:
  7.2 0.0 copy-start.8
  7.2 0.0 all-gather.3.cloned.1.call-start
  7.2 0.8 fusion.35
  8.0 11.9 %all_to_all.20 = bf16[8,32,512]{2,1,0:T(8,128)(2,1)} all-to-all(bf16[8,32,512]{2,1,0:T(8,128)(2,1)S(1)} %broadcast_in_dim.11), channel_id=1, replica_groups=mesh['y'=4,'xl'=2,'z'=8,'xh'=2,'core'=2] {'y','xl'}, dimensions={0} | all-to-all | bytes 524288 | tf_op jit(solution)/shard_map/all_to_all | solution.py:39
  20.0 0.0 all-gather.3.cloned.1.call-update
  20.0 0.7 convert_bitcast_fusion
  20.7 0.7 add_convert_fusion.1
  21.5 23.1 %all_to_all.21 = bf16[8,40,512]{2,1,0:T(8,128)(2,1)S(1)} all-to-all(bf16[8,40,512]{2,1,0:T(8,128)(2,1)S(1)} %broadcast_in_dim.8), channel_id=1, replica_groups=mesh['y'=4,'xl'=2,'z'=8,'xh'=2,'core'=2] {'z'}, dimensions={0} | all-to-all | bytes 655360 | tf_op jit(solution)/shard_map/all_to_all | solution.py:39
  44.6 1.4 collective-permute-start
  46.0 0.0 collective-permute-start.2
  46.0 2.3 %collective-permute-start.3 = (bf16[8,32,512]{2,1,0:T(8,128)(2,1)S(1)}, bf16[8,32,512]{2,1,0:T(8,128)(2,1)S(1)}, u32[]{:S(2)}, u32[]{:S(2)}) collective-permute-start(bf16[8,32,512]{2,1,0:T(8,128)(2,1)S(1)} %slice.56.a0), channel_id=1, source_target_pairs={{0,192},{64,0},{128,64},{192,128},{1,193},{65,1},{129,65},{193,129... | collective-permute-start | bytes 786440 | tf_op jit(solution)/shard_map/ppermute | solution.py:34
  48.3 3.1 %collective-permute-done.b0 = bf16[8,32,512]{2,1,0:T(8,128)(2,1)S(1)} collective-permute-done((bf16[8,32,512]{2,1,0:T(8,128)(2,1)S(1)}, bf16[8,32,512]{2,1,0:T(8,128)(2,1)S(1)}, u32[]{:S(2)}, u32[]{:S(2)}) %collective-permute-start) | collective-permute-done | bytes 262176 | tf_op jit(solution)/shard_map/ppermute | solution.py:34
  51.4 0.7 broadcast_in_dim.9
  52.1 4.5 %all-to-all-start.1 = ((bf16[8,8,512]{2,1,0:T(8,128)(2,1)}), bf16[8,8,512]{2,1,0:T(8,128)(2,1)S(1)}, u32[]{:S(2)}, u32[]{:S(2)}) async-start(bf16[8,8,512]{2,1,0:T(8,128)(2,1)} %broadcast_in_dim.9), calls=%async_computation.1 | async-start | bytes 131072 | tf_op jit(solution)/shard_map/all_to_all | solution.py:39
  56.6 2.7 %collective-permute-start.6 = (bf16[8,32,512]{2,1,0:T(8,128)(2,1)S(1)}, bf16[8,32,512]{2,1,0:T(8,128)(2,1)S(1)}, u32[]{:S(2)}, u32[]{:S(2)}) collective-permute-start(bf16[8,32,512]{2,1,0:T(8,128)(2,1)S(1)} %collective-permute-done.b0), channel_id=1, source_target_pairs={{0,192},{64,0},{128,64},{192,128},{1,193},{65,1},{129,65},{193,129... | collective-permute-start | bytes 786440 | tf_op jit(solution)/shard_map/ppermute | solution.py:34
  59.3 0.6 collective-permute-start.5
  60.0 0.7 pad_add_fusion.me
  60.6 1.1 copy.16.pattern
  61.7 1.1 copy.15.scale
  62.8 0.1 reshape.66
  62.9 0.1 copy.14
  63.1 2.7 %collective-permute-done.5.b2 = bf16[8,32,512]{2,1,0:T(8,128)(2,1)S(1)} collective-permute-done((bf16[8,32,512]{2,1,0:T(8,128)(2,1)S(1)}, bf16[8,32,512]{2,1,0:T(8,128)(2,1)S(1)}, u32[]{:S(2)}, u32[]{:S(2)}) %collective-permute-start.5) | collective-permute-done | bytes 262176 | tf_op jit(solution)/shard_map/ppermute | solution.py:34
  65.8 1.1 collective-permute-done.4.b1
  67.0 0.7 copy-done.6
  67.6 11.8 %scores.1 = (f32[512,1024]{1,0:T(8,128)}, f32[16,128]{1,0:T(8,128)}) custom-call(s32[2]{0:T(128)} %pad_add_fusion.me, bf16[1024,4096]{1,0:T(8,128)(2,1)} %images.3, f32[1024,1]{1,0:T(8,128)} %copy.15.scale, s32[1024,2]{1,0:T(8,128)} %copy.16.pattern, bf16[8,8,32,512]{3,2,1,0:T(8,128)(2,1)} %bitcast.17, bf16[8,32,512]{2,1,0:T(8,128)(2,1)} %copy-done, ...), custom_call_target="tpu_custom_call" | custom-call | tf_op jit(solution)/shard_map/scores/pallas_call | solution.py:103
  79.5 0.1 collective-permute-start.9
  79.6 2.1 %collective-permute-start.8 = (f32[16,128]{1,0:T(8,128)}, f32[16,128]{1,0:T(8,128)S(1)}, u32[]{:S(2)}, u32[]{:S(2)}) collective-permute-start(f32[16,128]{1,0:T(8,128)} %get-tuple-element.9.s0), channel_id=1, source_target_pairs={{0,2},{1,3},{2,0},{3,1},{4,6},{5,7},{6,4},{7,5},{8,10},{9,11},{10,... | collective-permute-start | bytes 24584 | tf_op jit(solution)/shard_map/ppermute | solution.py:34
  81.7 1.2 collective-permute-start.7
  82.9 0.9 fusion.2.cells
  83.9 0.5 collective-permute-done.9.s3
  84.4 0.7 collective-permute-done.8.s2
  85.1 0.6 copy-done.11
  85.6 0.0 copy-done.12
  85.7 27.7 %bricks.1 = (f32[512,512]{1,0:T(8,128)}, f32[512,512]{1,0:T(8,128)}, f32[8,128]{1,0:T(8,128)}) custom-call(s32[16384]{0:T(1024)} %fusion.2.cells, f32[8,128]{1,0:T(8,128)} %bitcast.23, f32[16,128]{1,0:T(8,128)} %get-tuple-element.9.s0, f32[16,128]{1,0:T(8,128)} %copy-done.12, f32[16,128]{1,0:T(8,128)} %copy-done.11, f32[16,128]{1,0:T(8,128)} %copy-done.10, ...), custom_call_target="tpu_custom_call" | custom-call | tf_op jit(solution)/shard_map/bricks/pallas_call | solution.py:198
  113.3 0.9 collective-permute-start.10
  114.2 2.5 %collective-permute-done.10 = f32[512,512]{1,0:T(8,128)S(1)} collective-permute-done((f32[512,512]{1,0:T(8,128)}, f32[512,512]{1,0:T(8,128)S(1)}, u32[]{:S(2)}, u32[]{:S(2)}) %collective-permute-start.10) | collective-permute-done | bytes 1048608 | tf_op jit(solution)/shard_map/ppermute | solution.py:34
  116.7 1.4 add_convert_fusion
  118.1 15.2 %all_to_all.22 = bf16[16,32,512]{2,1,0:T(8,128)(2,1)S(1)} all-to-all(bf16[16,32,512]{2,1,0:T(8,128)(2,1)S(1)} %bitcast.16), channel_id=1, replica_groups=mesh['y'=4,'xl'=2,'z'=8,'xh'=2,'core'=2] {'y','xl','xh'}, dimensions={0} | all-to-all | bytes 1048576 | tf_op jit(solution)/shard_map/all_to_all | solution.py:231
  133.3 0.1 convert_reduce_fusion
  133.4 0.3 collective-permute-start.11
  133.6 8.0 %collective-permute-done.11 = f32[16,512]{1,0:T(8,128)S(1)} collective-permute-done((f32[16,512]{1,0:T(8,128)S(1)}, f32[16,512]{1,0:T(8,128)S(1)}, u32[]{:S(2)}, u32[]{:S(2)}) %collective-permute-start.11) | collective-permute-done | bytes 32800 | tf_op jit(solution)/shard_map/ppermute | solution.py:34
  141.6 0.5 collective-permute-start.13
  142.1 2.3 %collective-permute-start.14 = (f32[4,512]{1,0:T(4,128)S(1)}, f32[4,512]{1,0:T(4,128)S(1)}, u32[]{:S(2)}, u32[]{:S(2)}) collective-permute-start(f32[4,512]{1,0:T(4,128)S(1)} %get-tuple-element.17), channel_id=1, source_target_pairs={{0,12},{4,8},{8,4},{12,0},{16,28},{20,24},{24,20},{28,16},{1,13},{... | collective-permute-start | bytes 24584 | tf_op jit(solution)/shard_map/ppermute | solution.py:34
  144.3 0.8 collective-permute-start.12
  145.2 1.1 collective-permute-done.13
  146.3 1.3 collective-permute-done.14
  147.5 0.5 collective-permute-done.12
  148.0 0.6 slice_add_fusion.2
  (44 shorter events, 0.2 us)
Async XLA Ops:
  7.2 53.5 %copy-start.9 = (s32[1024,2]{0,1:T(2,128)S(1)}, s32[1024,2]{0,1:T(2,128)}, u32[]{:S(2)}) copy-start(s32[1024,2]{0,1:T(2,128)} %param.11) | copy-start | bytes 24580
  7.2 54.5 %copy-start.8 = (f32[1024]{0:T(1024)S(1)}, f32[1024]{0:T(1024)}, u32[]{:S(2)}) copy-start(f32[1024]{0:T(1024)} %param.9) | copy-start | bytes 12292
  7.2 59.7 %all-gather.3.cloned.1.call-start = ((), (), s32[]{:S(2)}) async-start(), calls=%async_computation.4 | async-start | bytes 2359296 | tf_op jit(solution)/shard_map/all_gather | solution.py:45
  44.6 22.4 %copy-start = (bf16[8,32,512]{2,1,0:T(8,128)(2,1)}, bf16[8,32,512]{2,1,0:T(8,128)(2,1)S(1)}, u32[]{:S(2)}) copy-start(bf16[8,32,512]{2,1,0:T(8,128)(2,1)S(1)} %slice.56.a0) | copy-start | bytes 786436
  44.6 6.8 %collective-permute-start = (bf16[8,32,512]{2,1,0:T(8,128)(2,1)S(1)}, bf16[8,32,512]{2,1,0:T(8,128)(2,1)S(1)}, u32[]{:S(2)}, u32[]{:S(2)}) collective-permute-start(bf16[8,32,512]{2,1,0:T(8,128)(2,1)S(1)} %slice.56.a0), channel_id=1, source_target_pairs={{0,32},{32,0},{1,33},{33,1},{2,34},{34,2},{3,35},{35,3},{4,36},{36... | collective-permute-start | bytes 786440 | tf_op jit(solution)/shard_map/ppermute | solution.py:34
  46.0 13.4 %collective-permute-start.2 = (bf16[8,32,512]{2,1,0:T(8,128)(2,1)S(1)}, bf16[8,32,512]{2,1,0:T(8,128)(2,1)S(1)}, u32[]{:S(2)}, u32[]{:S(2)}) collective-permute-start(bf16[8,32,512]{2,1,0:T(8,128)(2,1)S(1)} %slice.56.a0), channel_id=1, source_target_pairs={{0,128},{64,192},{128,0},{192,64},{1,129},{65,193},{129,1},{193,65... | collective-permute-start | bytes 786440 | tf_op jit(solution)/shard_map/ppermute | solution.py:34
  46.0 17.1 %collective-permute-start.3 = (bf16[8,32,512]{2,1,0:T(8,128)(2,1)S(1)}, bf16[8,32,512]{2,1,0:T(8,128)(2,1)S(1)}, u32[]{:S(2)}, u32[]{:S(2)}) collective-permute-start(bf16[8,32,512]{2,1,0:T(8,128)(2,1)S(1)} %slice.56.a0), channel_id=1, source_target_pairs={{0,192},{64,0},{128,64},{192,128},{1,193},{65,1},{129,65},{193,129... | collective-permute-start | bytes 786440 | tf_op jit(solution)/shard_map/ppermute | solution.py:34
  48.3 14.8 %collective-permute-start.1 = (bf16[8,32,512]{2,1,0:T(8,128)(2,1)S(1)}, bf16[8,32,512]{2,1,0:T(8,128)(2,1)S(1)}, u32[]{:S(2)}, u32[]{:S(2)}) collective-permute-start(bf16[8,32,512]{2,1,0:T(8,128)(2,1)S(1)} %slice.56.a0), channel_id=1, source_target_pairs={{0,64},{64,128},{128,192},{192,0},{1,65},{65,129},{129,193},{193,1... | collective-permute-start | bytes 786440 | tf_op jit(solution)/shard_map/ppermute | solution.py:34
  51.4 15.5 %copy-start.1 = (bf16[8,32,512]{2,1,0:T(8,128)(2,1)}, bf16[8,32,512]{2,1,0:T(8,128)(2,1)S(1)}, u32[]{:S(2)}) copy-start(bf16[8,32,512]{2,1,0:T(8,128)(2,1)S(1)} %collective-permute-done.b0) | copy-start | bytes 786436
  52.1 10.7 %all-to-all-start.1 = ((bf16[8,8,512]{2,1,0:T(8,128)(2,1)}), bf16[8,8,512]{2,1,0:T(8,128)(2,1)S(1)}, u32[]{:S(2)}, u32[]{:S(2)}) async-start(bf16[8,8,512]{2,1,0:T(8,128)(2,1)} %broadcast_in_dim.9), calls=%async_computation.1 | async-start | bytes 131072 | tf_op jit(solution)/shard_map/all_to_all | solution.py:39
  56.6 9.2 %collective-permute-start.6 = (bf16[8,32,512]{2,1,0:T(8,128)(2,1)S(1)}, bf16[8,32,512]{2,1,0:T(8,128)(2,1)S(1)}, u32[]{:S(2)}, u32[]{:S(2)}) collective-permute-start(bf16[8,32,512]{2,1,0:T(8,128)(2,1)S(1)} %collective-permute-done.b0), channel_id=1, source_target_pairs={{0,192},{64,0},{128,64},{192,128},{1,193},{65,1},{129,65},{193,129... | collective-permute-start | bytes 786440 | tf_op jit(solution)/shard_map/ppermute | solution.py:34
  59.3 7.6 %collective-permute-start.4 = (bf16[8,32,512]{2,1,0:T(8,128)(2,1)S(1)}, bf16[8,32,512]{2,1,0:T(8,128)(2,1)S(1)}, u32[]{:S(2)}, u32[]{:S(2)}) collective-permute-start(bf16[8,32,512]{2,1,0:T(8,128)(2,1)S(1)} %collective-permute-done.b0), channel_id=1, source_target_pairs={{0,64},{64,128},{128,192},{192,0},{1,65},{65,129},{129,193},{193,1... | collective-permute-start | bytes 786440 | tf_op jit(solution)/shard_map/ppermute | solution.py:34
  59.3 7.6 %copy-start.2 = (bf16[8,32,512]{2,1,0:T(8,128)(2,1)}, bf16[8,32,512]{2,1,0:T(8,128)(2,1)S(1)}, u32[]{:S(2)}) copy-start(bf16[8,32,512]{2,1,0:T(8,128)(2,1)S(1)} %collective-permute-done.2.a2) | copy-start | bytes 786436
  59.3 6.5 %collective-permute-start.5 = (bf16[8,32,512]{2,1,0:T(8,128)(2,1)S(1)}, bf16[8,32,512]{2,1,0:T(8,128)(2,1)S(1)}, u32[]{:S(2)}, u32[]{:S(2)}) collective-permute-start(bf16[8,32,512]{2,1,0:T(8,128)(2,1)S(1)} %collective-permute-done.2.a2), channel_id=1, source_target_pairs={{0,32},{32,0},{1,33},{33,1},{2,34},{34,2},{3,35},{35,3},{4,36},{36... | collective-permute-start | bytes 786440 | tf_op jit(solution)/shard_map/ppermute | solution.py:34
  63.1 3.9 %copy-start.3 = (bf16[8,32,512]{2,1,0:T(8,128)(2,1)}, bf16[8,32,512]{2,1,0:T(8,128)(2,1)S(1)}, u32[]{:S(2)}) copy-start(bf16[8,32,512]{2,1,0:T(8,128)(2,1)S(1)} %collective-permute-done.3.a3) | copy-start | bytes 786436
  63.1 3.9 %copy-start.4 = (bf16[8,32,512]{2,1,0:T(8,128)(2,1)}, bf16[8,32,512]{2,1,0:T(8,128)(2,1)S(1)}, u32[]{:S(2)}) copy-start(bf16[8,32,512]{2,1,0:T(8,128)(2,1)S(1)} %collective-permute-done.1.a1) | copy-start | bytes 786436
  65.8 1.2 copy-start.7
  65.8 1.2 copy-start.5
  66.9 0.7 copy-start.6
  79.5 4.9 %collective-permute-start.9 = (f32[16,128]{1,0:T(8,128)}, f32[16,128]{1,0:T(8,128)S(1)}, u32[]{:S(2)}, u32[]{:S(2)}) collective-permute-start(f32[16,128]{1,0:T(8,128)} %get-tuple-element.9.s0), channel_id=1, source_target_pairs={{0,3},{1,2},{2,1},{3,0},{4,7},{5,6},{6,5},{7,4},{8,11},{9,10},{10,... | collective-permute-start | bytes 24584 | tf_op jit(solution)/shard_map/ppermute | solution.py:34
  79.6 5.5 %collective-permute-start.8 = (f32[16,128]{1,0:T(8,128)}, f32[16,128]{1,0:T(8,128)S(1)}, u32[]{:S(2)}, u32[]{:S(2)}) collective-permute-start(f32[16,128]{1,0:T(8,128)} %get-tuple-element.9.s0), channel_id=1, source_target_pairs={{0,2},{1,3},{2,0},{3,1},{4,6},{5,7},{6,4},{7,5},{8,10},{9,11},{10,... | collective-permute-start | bytes 24584 | tf_op jit(solution)/shard_map/ppermute | solution.py:34
  81.7 3.3 %collective-permute-start.7 = (f32[16,128]{1,0:T(8,128)}, f32[16,128]{1,0:T(8,128)S(1)}, u32[]{:S(2)}, u32[]{:S(2)}) collective-permute-start(f32[16,128]{1,0:T(8,128)} %get-tuple-element.9.s0), channel_id=1, source_target_pairs={{0,1},{1,0},{2,3},{3,2},{4,5},{5,4},{6,7},{7,6},{8,9},{9,8},{10,11... | collective-permute-start | bytes 24584 | tf_op jit(solution)/shard_map/ppermute | solution.py:34
  84.4 0.7 copy-start.10
  85.0 0.6 copy-start.11
  85.0 0.6 copy-start.12
  113.3 3.4 %collective-permute-start.10 = (f32[512,512]{1,0:T(8,128)}, f32[512,512]{1,0:T(8,128)S(1)}, u32[]{:S(2)}, u32[]{:S(2)}) collective-permute-start(f32[512,512]{1,0:T(8,128)} %get-tuple-element.12), channel_id=1, source_target_pairs={{0,1},{1,0},{2,3},{3,2},{4,5},{5,4},{6,7},{7,6},{8,9},{9,8},{10,11... | collective-permute-start | bytes 3145736 | tf_op jit(solution)/shard_map/ppermute | solution.py:34
  133.4 8.2 %collective-permute-start.11 = (f32[16,512]{1,0:T(8,128)S(1)}, f32[16,512]{1,0:T(8,128)S(1)}, u32[]{:S(2)}, u32[]{:S(2)}) collective-permute-start(f32[16,512]{1,0:T(8,128)S(1)} %slice.61), channel_id=1, source_target_pairs={{0,16},{4,20},{8,24},{12,28},{16,0},{20,4},{24,8},{28,12},{1,17},{... | collective-permute-start | bytes 98312 | tf_op jit(solution)/shard_map/ppermute | solution.py:34
  141.6 4.6 %collective-permute-start.13 = (f32[4,512]{1,0:T(4,128)S(1)}, f32[4,512]{1,0:T(4,128)S(1)}, u32[]{:S(2)}, u32[]{:S(2)}) collective-permute-start(f32[4,512]{1,0:T(4,128)S(1)} %get-tuple-element.16), channel_id=1, source_target_pairs={{0,8},{4,12},{8,0},{12,4},{16,24},{20,28},{24,16},{28,20},{1,9},{5... | collective-permute-start | bytes 24584 | tf_op jit(solution)/shard_map/ppermute | solution.py:34
  142.1 5.4 %collective-permute-start.14 = (f32[4,512]{1,0:T(4,128)S(1)}, f32[4,512]{1,0:T(4,128)S(1)}, u32[]{:S(2)}, u32[]{:S(2)}) collective-permute-start(f32[4,512]{1,0:T(4,128)S(1)} %get-tuple-element.17), channel_id=1, source_target_pairs={{0,12},{4,8},{8,4},{12,0},{16,28},{20,24},{24,20},{28,16},{1,13},{... | collective-permute-start | bytes 24584 | tf_op jit(solution)/shard_map/ppermute | solution.py:34
  144.3 3.7 %collective-permute-start.12 = (f32[4,512]{1,0:T(4,128)S(1)}, f32[4,512]{1,0:T(4,128)S(1)}, u32[]{:S(2)}, u32[]{:S(2)}) collective-permute-start(f32[4,512]{1,0:T(4,128)S(1)} %get-tuple-element.18), channel_id=1, source_target_pairs={{0,4},{4,0},{8,12},{12,8},{16,20},{20,16},{24,28},{28,24},{1,5},{5... | collective-permute-start | bytes 24584 | tf_op jit(solution)/shard_map/ppermute | solution.py:34
Sparse Core Ops, SparseCore 0:
  20.1 44.4 all-gather.2
